TPU v7x, 256 devices: a whole 4x4x8 slice. The times are simulated.
256 devices in a mesh: sub: 16 (over y, z_lo, core), grid: 16 (over x, z_hi).
Axes of the slice: x: 4, y: 4, z: 8 (z_hi: 4, z_lo: 2; z = z_hi * 2 + z_lo), core: 2. Of those that a mesh axis runs over, the one named last changes fastest.
Arguments:
- load_parts: float32 [256, 1152, 256], P(('sub', 'grid')), may hold values from -6 to 6
- iface_len: int32 [256], P(('sub', 'grid')), may hold values from 512 to 1152
- face_rows: int32 [256, 4, 128], P(('sub', 'grid')), may hold values from 0 to 1151, as said below
- face_count: int32 [256, 4], P(('sub', 'grid')), may hold values from 0 to 128, as said below
- local_inverse: bfloat16 [256, 1152, 1152], P(('sub', 'grid')), may hold values from -0.1875 to 0.1875
- schur_offdiag: bfloat16 [256, 1152, 1152], P(('sub', 'grid')), may hold values from -0.1875 to 0.1875
- schur_diag: float32 [256, 1152], P(('sub', 'grid')), may hold values from 1 to 2
- mode_basis: bfloat16 [256, 32, 1152], P(('sub', 'grid')), may hold values from -0.1875 to 0.1875
- coarse_inverse: float32 [8192, 8192], P('grid', 'sub'), may hold values from -0.25 to 0.25
Outputs:
- solution: float32 [256, 1152, 256], P(('sub', 'grid'))
- residual: float32 [256, 1152, 256], P(('sub', 'grid'))
Inputs may be any that keep to these rules, and one draw needn't show every extreme that they name: `face_rows`: each of a subdomain's 4 * 128 listed rows is below its interface length, and all are distinct. `face_count`: A face and the neighbour's opposite face have equal counts; faces at the edge of the arrangement have count 0.
All inputs are finite; a program needn't handle non-finite values.
Results may differ from a plain program's by a relative error of at most 0.0037.
Values sent between devices are 32-bit elements; how exact they have to be, the bound alone decides.
No kernel may reach another device: no remote copies, remote signals or barrier semaphores. Data moves between devices by JAX's collectives and lax.ppermute only.
A program may use at most 64 MiB of HBM per device.

v0:
```python
import jax
import jax.numpy as jnp
from jax import lax
from jax.sharding import PartitionSpec as P

ITERS = 2


def shifted(array, axis, by):
    size = lax.axis_size(axis)
    pairs = [(i, i + by) for i in range(size) if 0 <= i + by < size]
    return lax.ppermute(array, axis, pairs)


def assemble(values, rows, counts):
    usable = (jnp.arange(rows.shape[1])[None, :] < counts[:, None]).astype(jnp.float32)
    outgoing = values[rows] * usable[..., None]
    from_above_sub = shifted(outgoing[1], "sub", -1)
    from_below_sub = shifted(outgoing[0], "sub", 1)
    from_above_grid = shifted(outgoing[3], "grid", -1)
    from_below_grid = shifted(outgoing[2], "grid", 1)
    received = jnp.stack([from_above_sub, from_below_sub, from_above_grid, from_below_grid], axis=0)
    return values.at[rows.reshape(-1)].add(received.reshape(-1, values.shape[1]))


def local_product(matrix, vector):
    return jnp.dot(matrix, vector, preferred_element_type=jnp.float32)


def body(
    load_parts,
    iface_len,
    face_rows,
    face_count,
    local_inverse,
    schur_offdiag,
    schur_diag,
    mode_basis,
    coarse_inverse,
):
    loads_here = load_parts[0]
    length = iface_len[0]
    rows = face_rows[0]
    counts = face_count[0]
    inverse_here = local_inverse[0]
    offdiag_here = schur_offdiag[0]
    diag_here = schur_diag[0][:, None]
    basis_here = mode_basis[0]
    basis_wide = basis_here.astype(jnp.float32)
    nmodes = basis_here.shape[0]
    live = (jnp.arange(loads_here.shape[0]) < length).astype(jnp.float32)[:, None]
    resid = loads_here * live
    solution = jnp.zeros_like(resid)
    for sweep in range(ITERS):
        assembled_b = assemble(resid, rows, counts).astype(jnp.bfloat16)
        coarse_in = jnp.dot(basis_here, assembled_b, preferred_element_type=jnp.float32)
        gathered = lax.all_gather(coarse_in, "grid", axis=0, tiled=True)
        local_part = local_product(inverse_here, assembled_b)
        partial_rows = jnp.dot(coarse_inverse, gathered, precision=lax.Precision.HIGHEST)
        totals = lax.psum(partial_rows, "sub")
        coarse_out = lax.dynamic_slice_in_dim(totals, lax.axis_index("sub") * nmodes, nmodes, 0)
        spread = lax.dot_general(
            basis_wide,
            coarse_out,
            (((0,), (0,)), ((), ())),
            precision=lax.Precision.HIGHEST,
            preferred_element_type=jnp.float32,
        )
        correction = live * (local_part + spread)
        increment = assemble(correction, rows, counts)
        solution = solution + increment
        applied = local_product(offdiag_here, increment.astype(jnp.bfloat16))
        applied = applied + diag_here * increment
        resid = resid - live * applied
    return (solution[None], resid[None])


def solution(mesh):
    in_specs = (
        P(("sub", "grid"), None, None),
        P(("sub", "grid")),
        P(("sub", "grid"), None, None),
        P(("sub", "grid"), None),
        P(("sub", "grid"), None, None),
        P(("sub", "grid"), None, None),
        P(("sub", "grid"), None),
        P(("sub", "grid"), None, None),
        P("grid", "sub"),
    )
    out_specs = (P(("sub", "grid"), None, None), P(("sub", "grid"), None, None))
    return jax.shard_map(body, mesh=mesh, in_specs=in_specs, out_specs=out_specs, check_vma=False)
```

profile of v0, /device:TPU:72, one launch (start us, length us, event | category | flops | bytes accessed | tf_op | source)
XLA Modules:
  0.0 497.1 jit_solution(14613327687857058898)
XLA Ops:
  17.1 2.8 gather_fusion
  20.2 3.2 collective-permute-start
  23.3 5.5 %collective-permute-start.3 = (f32[128,256]{1,0:T(8,128)S(1)}, f32[128,256]{1,0:T(8,128)S(1)}, u32[]{:S(2)}, u32[]{:S(2)}) collective-permute-start(f32[128,256]{1,0:T(8,128)S(1)} %get-tuple-element.21), channel_id=1, source_target_pairs={{0,1},{1,2},{2,3},{3,4},{4,5},{5,6},{6,7},{7,8},{8,9},{9,10},{10,1... | collective-permute-start | bytes 393224 | tf_op jit(solution)/shard_map/ppermute | solution.py:12
  34.4 6.4 %collective-permute-done.2 = f32[128,256]{1,0:T(8,128)S(1)} collective-permute-done((f32[128,256]{1,0:T(8,128)S(1)}, f32[128,256]{1,0:T(8,128)S(1)}, u32[]{:S(2)}, u32[]{:S(2)}) %collective-permute-start.2) | collective-permute-done | bytes 131104 | tf_op jit(solution)/shard_map/ppermute | solution.py:12
  40.9 5.3 %scatter_fusion = f32[1152,256]{1,0:T(8,128)} fusion(f32[1152,256]{1,0:T(8,128)} %copy.45, s32[512]{0:T(512)S(1)} %bitcast.149, f32[512,256]{1,0:T(8,128)S(1)} %bitcast.127), kind=kCustom, calls=%fused_computation.4 | custom fusion | flops 131072 | bytes 1574912 | tf_op jit(solution)/shard_map/scatter-add | solution.py:23
  47.8 41.9 %all_gather.6 = f32[512,256]{1,0:T(8,128)S(1)} all-gather(f32[32,256]{1,0:T(8,128)S(1)} %convolution_bitcast_fusion.5), channel_id=1, replica_groups=mesh['sub'=16,'grid'=16] {'grid'}, dimensions={0}, use_global_device_ids=true | all-gather | bytes 557056 | tf_op jit(solution)/shard_map/all_gather | solution.py:57
  89.7 2.7 convolution_bitcast_fusion.3
  92.5 3.3 fusion.15
  95.8 111.8 %all-reduce.3.cloned.1.call-done = f32[512,256]{0,1:T(8,128)} async-done(((f32[512,256]{0,1:T(8,128)}), f32[512,256]{0,1:T(8,128)}) %all-reduce.3.cloned.1.call-update) | async-done | bytes 524304 | tf_op jit(solution)/shard_map/psum | solution.py:60
  207.6 3.0 fusion.3
  213.3 2.8 gather_fusion.1
  217.0 5.4 %collective-permute-start.4 = (f32[128,256]{1,0:T(8,128)}, f32[128,256]{1,0:T(8,128)S(1)}, u32[]{:S(2)}, u32[]{:S(2)}) collective-permute-start(f32[128,256]{1,0:T(8,128)} %get-tuple-element.16), channel_id=1, source_target_pairs={{16,0},{32,16},{48,32},{64,48},{80,64},{96,80},{112,96},{128,112},... | collective-permute-start | bytes 393224 | tf_op jit(solution)/shard_map/ppermute | solution.py:12
  222.4 4.8 collective-permute-start.7
  231.9 4.6 collective-permute-done.6
  239.4 5.3 %scatter_fusion.1 = f32[1152,256]{1,0:T(8,128)} fusion(f32[1152,256]{1,0:T(8,128)} %copy.47, s32[512]{0:T(512)S(1)} %bitcast.150, f32[512,256]{1,0:T(8,128)S(1)} %bitcast.128), kind=kCustom, calls=%fused_computation.5 | custom fusion | flops 131072 | bytes 1574912 | tf_op jit(solution)/shard_map/scatter-add | solution.py:23
  247.3 4.8 fusion.10
  254.8 2.8 gather_fusion.2
  259.8 6.2 %collective-permute-start.11 = (f32[128,256]{1,0:T(8,128)S(1)}, f32[128,256]{1,0:T(8,128)S(1)}, u32[]{:S(2)}, u32[]{:S(2)}) collective-permute-start(f32[128,256]{1,0:T(8,128)S(1)} %get-tuple-element.13), channel_id=1, source_target_pairs={{0,1},{1,2},{2,3},{3,4},{4,5},{5,6},{6,7},{7,8},{8,9},{9,10},{10,1... | collective-permute-start | bytes 393224 | tf_op jit(solution)/shard_map/ppermute | solution.py:12
  270.1 5.5 %collective-permute-done.10 = f32[128,256]{1,0:T(8,128)S(1)} collective-permute-done((f32[128,256]{1,0:T(8,128)S(1)}, f32[128,256]{1,0:T(8,128)S(1)}, u32[]{:S(2)}, u32[]{:S(2)}) %collective-permute-start.10) | collective-permute-done | bytes 131104 | tf_op jit(solution)/shard_map/ppermute | solution.py:12
  278.2 5.3 %scatter_fusion.2 = f32[1152,256]{1,0:T(8,128)} fusion(f32[1152,256]{1,0:T(8,128)} %copy.50, s32[512]{0:T(512)S(1)} %bitcast.151, f32[512,256]{1,0:T(8,128)S(1)} %bitcast.129), kind=kCustom, calls=%fused_computation.6 | custom fusion | flops 131072 | bytes 1574912 | tf_op jit(solution)/shard_map/scatter-add | solution.py:23
  285.0 41.1 %all_gather.7 = f32[512,256]{1,0:T(8,128)S(1)} all-gather(f32[32,256]{1,0:T(8,128)S(1)} %convolution_bitcast_fusion.4), channel_id=1, replica_groups=mesh['sub'=16,'grid'=16] {'grid'}, dimensions={0}, use_global_device_ids=true | all-gather | bytes 557056 | tf_op jit(solution)/shard_map/all_gather | solution.py:57
  326.1 2.7 convolution_bitcast_fusion.2
  328.8 3.3 fusion.13
  332.2 109.8 %all-reduce.5.cloned.1.call-done = f32[512,256]{0,1:T(8,128)} async-done(((f32[512,256]{0,1:T(8,128)}), f32[512,256]{0,1:T(8,128)}) %all-reduce.5.cloned.1.call-update) | async-done | bytes 524304 | tf_op jit(solution)/shard_map/psum | solution.py:60
  441.9 3.0 fusion.2
  447.6 2.8 gather_fusion.3
  450.6 5.4 %collective-permute-start.12 = (f32[128,256]{1,0:T(8,128)S(1)}, f32[128,256]{1,0:T(8,128)S(1)}, u32[]{:S(2)}, u32[]{:S(2)}) collective-permute-start(f32[128,256]{1,0:T(8,128)S(1)} %get-tuple-element.8), channel_id=1, source_target_pairs={{16,0},{32,16},{48,32},{64,48},{80,64},{96,80},{112,96},{128,112},... | collective-permute-start | bytes 393224 | tf_op jit(solution)/shard_map/ppermute | solution.py:12
  456.1 4.8 collective-permute-start.15
  465.6 4.6 collective-permute-done.14
  472.0 5.3 %scatter_fusion.3 = f32[1152,256]{1,0:T(8,128)} fusion(f32[1152,256]{1,0:T(8,128)} %copy.52, s32[512]{0:T(512)S(1)} %bitcast.152, f32[512,256]{1,0:T(8,128)S(1)} %bitcast.126), kind=kCustom, calls=%fused_computation.7 | custom fusion | flops 131072 | bytes 1574912 | tf_op jit(solution)/shard_map/scatter-add | solution.py:23
  477.3 2.8 add_bitcast_fusion
  482.7 4.9 fusion.7
  (68 shorter events, 57.9 us)
Async XLA Ops:
  7.2 85.3 %copy-start = (bf16[1,1152,1152]{2,1,0:T(8,128)(2,1)S(1)}, bf16[1,1152,1152]{2,1,0:T(8,128)(2,1)}, u32[]{:S(2)}) copy-start(bf16[1,1152,1152]{2,1,0:T(8,128)(2,1)} %param.13) | copy-start | bytes 7962628
  7.2 200.4 %all-reduce.3.cloned.1.call-start = ((), (), s32[]{:S(2)}) async-start(), calls=%async_computation | async-start | bytes 1048576 | tf_op jit(solution)/shard_map/psum | solution.py:60
  20.0 12.7 %copy-start.5 = (s32[1,4,128]{2,1,0:T(4,128)S(1)}, s32[1,4,128]{2,1,0:T(4,128)}, u32[]{:S(2)}) copy-start(s32[1,4,128]{2,1,0:T(4,128)} %param.11) | copy-start | bytes 6148
  20.2 12.5 %collective-permute-start = (f32[128,256]{1,0:T(8,128)S(1)}, f32[128,256]{1,0:T(8,128)S(1)}, u32[]{:S(2)}, u32[]{:S(2)}) collective-permute-start(f32[128,256]{1,0:T(8,128)S(1)} %get-tuple-element.20), channel_id=1, source_target_pairs={{16,0},{32,16},{48,32},{64,48},{80,64},{96,80},{112,96},{128,112},... | collective-permute-start | bytes 393224 | tf_op jit(solution)/shard_map/ppermute | solution.py:12
  23.3 11.1 %collective-permute-start.3 = (f32[128,256]{1,0:T(8,128)S(1)}, f32[128,256]{1,0:T(8,128)S(1)}, u32[]{:S(2)}, u32[]{:S(2)}) collective-permute-start(f32[128,256]{1,0:T(8,128)S(1)} %get-tuple-element.21), channel_id=1, source_target_pairs={{0,1},{1,2},{2,3},{3,4},{4,5},{5,6},{6,7},{7,8},{8,9},{9,10},{10,1... | collective-permute-start | bytes 393224 | tf_op jit(solution)/shard_map/ppermute | solution.py:12
  28.8 12.0 %collective-permute-start.2 = (f32[128,256]{1,0:T(8,128)S(1)}, f32[128,256]{1,0:T(8,128)S(1)}, u32[]{:S(2)}, u32[]{:S(2)}) collective-permute-start(f32[128,256]{1,0:T(8,128)S(1)} %get-tuple-element.22), channel_id=1, source_target_pairs={{1,0},{2,1},{3,2},{4,3},{5,4},{6,5},{7,6},{8,7},{9,8},{10,9},{11,1... | collective-permute-start | bytes 393224 | tf_op jit(solution)/shard_map/ppermute | solution.py:12
  30.8 10.0 %collective-permute-start.1 = (f32[128,256]{1,0:T(8,128)S(1)}, f32[128,256]{1,0:T(8,128)S(1)}, u32[]{:S(2)}, u32[]{:S(2)}) collective-permute-start(f32[128,256]{1,0:T(8,128)S(1)} %get-tuple-element.23), channel_id=1, source_target_pairs={{0,16},{16,32},{32,48},{48,64},{64,80},{80,96},{96,112},{112,128},... | collective-permute-start | bytes 393224 | tf_op jit(solution)/shard_map/ppermute | solution.py:12
  40.8 5.3 %copy-start.3 = (bf16[1,32,1152]{2,1,0:T(8,128)(2,1)S(1)}, bf16[1,32,1152]{2,1,0:T(8,128)(2,1)}, u32[]{:S(2)}) copy-start(bf16[1,32,1152]{2,1,0:T(8,128)(2,1)} %param.16) | copy-start | bytes 221188
  46.2 43.5 %copy-start.1 = (f32[512,512]{1,0:T(8,128)S(1)}, f32[512,512]{1,0:T(8,128)}, u32[]{:S(2)}) copy-start(f32[512,512]{1,0:T(8,128)} %param.17) | copy-start | bytes 3145732
  92.4 349.5 %all-reduce.5.cloned.1.call-start = ((), (), s32[]{:S(2)}) async-start(), calls=%async_computation.1 | async-start | bytes 1048576 | tf_op jit(solution)/shard_map/psum | solution.py:60
  216.1 15.0 %copy-start.6 = (f32[1,1152]{1,0:T(1,128)S(1)}, f32[1,1152]{1,0:T(1,128)}, u32[]{:S(2)}) copy-start(f32[1,1152]{1,0:T(1,128)} %param.15) | copy-start | bytes 13828
  217.0 14.1 %collective-permute-start.4 = (f32[128,256]{1,0:T(8,128)}, f32[128,256]{1,0:T(8,128)S(1)}, u32[]{:S(2)}, u32[]{:S(2)}) collective-permute-start(f32[128,256]{1,0:T(8,128)} %get-tuple-element.16), channel_id=1, source_target_pairs={{16,0},{32,16},{48,32},{64,48},{80,64},{96,80},{112,96},{128,112},... | collective-permute-start | bytes 393224 | tf_op jit(solution)/shard_map/ppermute | solution.py:12
  222.4 9.5 %collective-permute-start.7 = (f32[128,256]{1,0:T(8,128)S(1)}, f32[128,256]{1,0:T(8,128)S(1)}, u32[]{:S(2)}, u32[]{:S(2)}) collective-permute-start(f32[128,256]{1,0:T(8,128)S(1)} %get-tuple-element.17), channel_id=1, source_target_pairs={{0,1},{1,2},{2,3},{3,4},{4,5},{5,6},{6,7},{7,8},{8,9},{9,10},{10,1... | collective-permute-start | bytes 393224 | tf_op jit(solution)/shard_map/ppermute | solution.py:12
  227.2 9.3 %collective-permute-start.6 = (f32[128,256]{1,0:T(8,128)S(1)}, f32[128,256]{1,0:T(8,128)S(1)}, u32[]{:S(2)}, u32[]{:S(2)}) collective-permute-start(f32[128,256]{1,0:T(8,128)S(1)} %get-tuple-element.18), channel_id=1, source_target_pairs={{1,0},{2,1},{3,2},{4,3},{5,4},{6,5},{7,6},{8,7},{9,8},{10,9},{11,1... | collective-permute-start | bytes 393224 | tf_op jit(solution)/shard_map/ppermute | solution.py:12
  229.2 9.2 %collective-permute-start.5 = (f32[128,256]{1,0:T(8,128)S(1)}, f32[128,256]{1,0:T(8,128)}, u32[]{:S(2)}, u32[]{:S(2)}) collective-permute-start(f32[128,256]{1,0:T(8,128)S(1)} %get-tuple-element.19), channel_id=1, source_target_pairs={{0,16},{16,32},{32,48},{48,64},{64,80},{80,96},{96,112},{112,128},... | collective-permute-start | bytes 393224 | tf_op jit(solution)/shard_map/ppermute | solution.py:12
  236.5 1.9 copy-start.4
  257.8 12.2 %collective-permute-start.8 = (f32[128,256]{1,0:T(8,128)S(1)}, f32[128,256]{1,0:T(8,128)S(1)}, u32[]{:S(2)}, u32[]{:S(2)}) collective-permute-start(f32[128,256]{1,0:T(8,128)S(1)} %get-tuple-element.12), channel_id=1, source_target_pairs={{16,0},{32,16},{48,32},{64,48},{80,64},{96,80},{112,96},{128,112},... | collective-permute-start | bytes 393224 | tf_op jit(solution)/shard_map/ppermute | solution.py:12
  259.8 10.3 %collective-permute-start.11 = (f32[128,256]{1,0:T(8,128)S(1)}, f32[128,256]{1,0:T(8,128)S(1)}, u32[]{:S(2)}, u32[]{:S(2)}) collective-permute-start(f32[128,256]{1,0:T(8,128)S(1)} %get-tuple-element.13), channel_id=1, source_target_pairs={{0,1},{1,2},{2,3},{3,4},{4,5},{5,6},{6,7},{7,8},{8,9},{9,10},{10,1... | collective-permute-start | bytes 393224 | tf_op jit(solution)/shard_map/ppermute | solution.py:12
  266.0 9.6 %collective-permute-start.10 = (f32[128,256]{1,0:T(8,128)S(1)}, f32[128,256]{1,0:T(8,128)S(1)}, u32[]{:S(2)}, u32[]{:S(2)}) collective-permute-start(f32[128,256]{1,0:T(8,128)S(1)} %get-tuple-element.14), channel_id=1, source_target_pairs={{1,0},{2,1},{3,2},{4,3},{5,4},{6,5},{7,6},{8,7},{9,8},{10,9},{11,1... | collective-permute-start | bytes 393224 | tf_op jit(solution)/shard_map/ppermute | solution.py:12
  267.9 10.3 %collective-permute-start.9 = (f32[128,256]{1,0:T(8,128)S(1)}, f32[128,256]{1,0:T(8,128)S(1)}, u32[]{:S(2)}, u32[]{:S(2)}) collective-permute-start(f32[128,256]{1,0:T(8,128)S(1)} %get-tuple-element.15), channel_id=1, source_target_pairs={{0,16},{16,32},{32,48},{48,64},{64,80},{80,96},{96,112},{112,128},... | collective-permute-start | bytes 393224 | tf_op jit(solution)/shard_map/ppermute | solution.py:12
  283.5 42.6 %copy-start.2 = (f32[512,512]{1,0:T(8,128)S(1)}, f32[512,512]{1,0:T(8,128)}, u32[]{:S(2)}) copy-start(f32[512,512]{1,0:T(8,128)} %param.17) | copy-start | bytes 3145732
  450.6 14.3 %collective-permute-start.12 = (f32[128,256]{1,0:T(8,128)S(1)}, f32[128,256]{1,0:T(8,128)S(1)}, u32[]{:S(2)}, u32[]{:S(2)}) collective-permute-start(f32[128,256]{1,0:T(8,128)S(1)} %get-tuple-element.8), channel_id=1, source_target_pairs={{16,0},{32,16},{48,32},{64,48},{80,64},{96,80},{112,96},{128,112},... | collective-permute-start | bytes 393224 | tf_op jit(solution)/shard_map/ppermute | solution.py:12
  456.1 9.5 %collective-permute-start.15 = (f32[128,256]{1,0:T(8,128)S(1)}, f32[128,256]{1,0:T(8,128)S(1)}, u32[]{:S(2)}, u32[]{:S(2)}) collective-permute-start(f32[128,256]{1,0:T(8,128)S(1)} %get-tuple-element.9), channel_id=1, source_target_pairs={{0,1},{1,2},{2,3},{3,4},{4,5},{5,6},{6,7},{7,8},{8,9},{9,10},{10,1... | collective-permute-start | bytes 393224 | tf_op jit(solution)/shard_map/ppermute | solution.py:12
  460.8 9.3 %collective-permute-start.14 = (f32[128,256]{1,0:T(8,128)S(1)}, f32[128,256]{1,0:T(8,128)S(1)}, u32[]{:S(2)}, u32[]{:S(2)}) collective-permute-start(f32[128,256]{1,0:T(8,128)S(1)} %get-tuple-element.10), channel_id=1, source_target_pairs={{1,0},{2,1},{3,2},{4,3},{5,4},{6,5},{7,6},{8,7},{9,8},{10,9},{11,1... | collective-permute-start | bytes 393224 | tf_op jit(solution)/shard_map/ppermute | solution.py:12
  462.8 9.1 %collective-permute-start.13 = (f32[128,256]{1,0:T(8,128)S(1)}, f32[128,256]{1,0:T(8,128)S(1)}, u32[]{:S(2)}, u32[]{:S(2)}) collective-permute-start(f32[128,256]{1,0:T(8,128)S(1)} %get-tuple-element.11), channel_id=1, source_target_pairs={{0,16},{16,32},{32,48},{48,64},{64,80},{80,96},{96,112},{112,128},... | collective-permute-start | bytes 393224 | tf_op jit(solution)/shard_map/ppermute | solution.py:12
Sparse Core Ops, SparseCore 0:
  92.5 114.9 all-reduce.2
  328.9 112.9 all-reduce.4
where the time goes:
time: 502 us; the launch traced here: 497 us
  waiting for transfers between devices  252 us (50%)
  blocking collectives  83 us (17%)
  starting transfers between devices  53.1 us (11%)
  local copies, waits for them, and re-layouts  33.5 us (7%)
  matrix products  30.9 us (6%)
  other arithmetic  29.4 us (6%)
  between operations  15.2 us (3%)
    psum x2, waiting for transfers between devices, body(): totals = lax.psum(partial_rows, 'sub')  222 us
    all_gather x2, blocking collectives, body(): gathered = lax.all_gather(coarse_in, 'grid', axis=0, tiled=True)  83 us
    ppermute x16, starting transfers between devices, shifted(): return lax.ppermute(array, axis, pairs)  53 us
    ppermute x16, waiting for transfers between devices, shifted(): return lax.ppermute(array, axis, pairs)  30.4 us
    scatter-add x4, other arithmetic, assemble(): values.at[rows.reshape(-1)].add(received.reshape(-1, values.shape[1]))  21.2 us
    dot_general x4, matrix products, local_product(): return jnp.dot(matrix, vector, preferred_element_type=jnp.float32)  16.4 us
    gather x4, local copies, waits for them, and re-layouts, assemble(): outgoing = values[rows] * usable[..., None]  11.3 us
  transfers between devices with their start and end apart: 18, of which 12 were waited for; matrix products, arithmetic and copies ran while one was open for 1% of the time, Pallas kernels for 0%

commit v1 on v0

v1 whole, which is shorter than its diff:
```python
import functools

import jax
import jax.numpy as jnp
from jax import lax
from jax.experimental import pallas as pl
from jax.experimental.pallas import tpu as pltpu
from jax.sharding import PartitionSpec as P

ITERS = 2
VMEM_LIMIT = 32 * 1024 * 1024
F32 = jnp.float32
BF16 = jnp.bfloat16


def dot(a, b):
    return jnp.dot(a, b, preferred_element_type=F32)


def halves(v):
    high = v.astype(BF16)
    return high, (v - high.astype(F32)).astype(BF16)


def pick(onehot, v):
    high, low = halves(v)
    return dot(onehot, high) + dot(onehot, low)


def live_of(length_ref, n):
    return (lax.broadcasted_iota(jnp.int32, (n, 1), 0) < length_ref[0]).astype(F32)


def store_faces(faces, refs):
    share = refs[0].shape[0]
    for j, ref in enumerate(refs):
        ref[...] = faces[j * share : (j + 1) * share]


def load_faces(refs):
    return jnp.concatenate([ref[...] for ref in refs], axis=0)


def begin_kernel(length, rows, loads, resid, take, *faces):
    n = loads.shape[0]
    spot = lax.broadcasted_iota(jnp.int32, take.shape, 1)
    take[...] = (rows[...] == spot).astype(F32).astype(BF16)
    resid[...] = loads[...] * live_of(length, n)
    store_faces(pick(take[...], resid[...]), faces)


def tables_kernel(rows, coarse, put, coarse_high, coarse_low):
    spot = lax.broadcasted_iota(jnp.int32, put.shape, 0)
    put[...] = (rows[...] == spot).astype(F32).astype(BF16)
    high, low = halves(coarse[...])
    coarse_high[...] = high
    coarse_low[...] = low


def coarse_in_kernel(resid, f0, f1, f2, f3, put, basis, assembled, coarse_in):
    received = load_faces((f0, f1, f2, f3))
    assembled[...] = (resid[...] + pick(put[...], received)).astype(BF16)
    block = dot(basis[...], assembled[...])
    for j in range(coarse_in.shape[0]):
        coarse_in[j] = block


def local_kernel(inverse, assembled, local):
    local[...] = dot(inverse[...], assembled[...])


def coarse_kernel(core, high, low, gathered, keep, send):
    groups, modes, loads = gathered.shape
    g_high, g_low = halves(gathered[...].reshape(groups * modes, loads))
    out = dot(high[...], g_high) + dot(high[...], g_low) + dot(low[...], g_high)
    pairs = out.reshape(-1, 2, modes, loads)
    even = pairs[:, 0].reshape(keep.shape)
    odd = pairs[:, 1].reshape(keep.shape)
    first = core[0] == 0
    keep[...] = jnp.where(first, even, odd)
    send[...] = jnp.where(first, odd, even)


def correction_kernel(length, local, basis_t, parts, take, correction, *faces):
    n = local.shape[0]
    total = jnp.sum(parts[...], axis=0)
    high, low = halves(total)
    spread = dot(basis_t[...], high) + dot(basis_t[...], low)
    correction[...] = live_of(length, n) * (local[...] + spread)
    store_faces(pick(take[...], correction[...]), faces)


def increment_kernel(first, last, *refs):
    length, correction, f0, f1, f2, f3, put, offdiag, diag, resid = refs[:10]
    refs = refs[10:]
    if not first:
        before, refs = refs[0], refs[1:]
    if not last:
        take, refs = refs[0], refs[1:]
    solution_out, resid_out, *faces = refs
    n = correction.shape[0]
    increment = correction[...] + pick(put[...], load_faces((f0, f1, f2, f3)))
    solution_out[...] = increment if first else before[...] + increment
    applied = dot(offdiag[...], increment.astype(BF16)) + diag[...] * increment
    resid_out[...] = resid[...] - live_of(length, n) * applied
    if not last:
        store_faces(pick(take[...], resid_out[...]), faces)


def call(kernel, outs, args, scalars=0, flops=0):
    size = lambda a: a.size * a.dtype.itemsize
    specs = [pl.BlockSpec(memory_space=pltpu.SMEM)] * scalars
    specs += [pl.BlockSpec(memory_space=pltpu.VMEM)] * (len(args) - scalars)
    return pl.pallas_call(
        kernel,
        out_shape=outs,
        in_specs=specs,
        out_specs=[pl.BlockSpec(memory_space=pltpu.VMEM)] * len(outs),
        compiler_params=pltpu.CompilerParams(vmem_limit_bytes=VMEM_LIMIT),
        cost_estimate=pl.CostEstimate(
            flops=flops,
            bytes_accessed=sum(size(a) for a in args) + sum(size(a) for a in outs),
            transcendentals=0,
        ),
    )(*args)


def like(*shape, dtype=F32):
    return jax.ShapeDtypeStruct(shape, dtype)


def swap(array, axis, odd):
    size = lax.axis_size(axis)
    pairs = [(i, ((i + odd) ^ 1) - odd) for i in range(size)]
    return lax.ppermute(array, axis, [(i, j) for i, j in pairs if 0 <= j < size])


def exchange(faces):
    return (
        swap(faces[0], "sub", 0),
        swap(faces[1], "sub", 1),
        swap(faces[2], "grid", 0),
        swap(faces[3], "grid", 1),
    )


def body(
    load_parts,
    iface_len,
    face_rows,
    face_count,
    local_inverse,
    schur_offdiag,
    schur_diag,
    mode_basis,
    coarse_inverse,
):
    loads = load_parts[0]
    inverse = local_inverse[0]
    offdiag = schur_offdiag[0]
    diag = schur_diag[0][:, None]
    basis = mode_basis[0]
    basis_t = basis.T
    n, nloads = loads.shape
    modes = basis.shape[0]
    share = face_rows.shape[2]
    nsub = lax.axis_size("sub")
    ngrid = lax.axis_size("grid")
    core = lax.rem(lax.axis_index("sub"), 2)
    column = lax.rem(lax.axis_index("grid"), 2)

    usable = jnp.arange(share)[None, :] < face_count[0][:, None]
    rows = jnp.where(usable, face_rows[0], -1)
    rows_sub = jnp.where(core == 0, rows[:2], rows[1::-1])
    rows_grid = jnp.where(column == 0, rows[2:], rows[:1:-1])
    rows = jnp.concatenate([rows_sub, rows_grid], axis=0).reshape(-1)
    nrows = rows.shape[0]
    core = core[None]

    face = like(share, nloads)
    block = like(n, nloads)
    gather_flops = 4 * nrows * n * nloads
    square_flops = 2 * n * n * nloads

    resid, take, *faces = call(
        begin_kernel,
        [block, like(nrows, n, dtype=BF16)] + [face] * 4,
        (iface_len, rows[:, None], loads),
        scalars=1,
        flops=gather_flops,
    )
    order = coarse_inverse.shape
    put, coarse_high, coarse_low = call(
        tables_kernel,
        [like(n, nrows, dtype=BF16), like(*order, dtype=BF16), like(*order, dtype=BF16)],
        (rows[None, :], coarse_inverse),
    )
    solution = None
    for sweep in range(ITERS):
        first, last = sweep == 0, sweep == ITERS - 1
        received = exchange(faces)
        assembled, coarse_in = call(
            coarse_in_kernel,
            [like(n, nloads, dtype=BF16), like(ngrid, modes, nloads)],
            (resid, *received, put, basis),
            flops=gather_flops,
        )
        gathered = lax.all_to_all(coarse_in, "grid", 0, 0)
        keep, send = call(
            coarse_kernel,
            [like(order[0] // 2, nloads)] * 2,
            (core, coarse_high, coarse_low, gathered),
            scalars=1,
            flops=6 * order[0] * order[1] * nloads,
        )
        other = swap(send, "sub", 0)
        (local,) = call(local_kernel, [block], (inverse, assembled), flops=square_flops)
        parts = (keep + other).reshape(nsub // 2, modes, nloads)
        groups = [list(range(i, nsub, 2)) for i in range(2)]
        parts = lax.all_to_all(parts, "sub", 0, 0, axis_index_groups=groups)
        correction, *faces = call(
            correction_kernel,
            [block] + [face] * 4,
            (iface_len, local, basis_t, parts, take),
            scalars=1,
            flops=gather_flops,
        )
        received = exchange(faces)
        args = (iface_len, correction, *received, put, offdiag, diag, resid)
        args += () if first else (solution,)
        args += () if last else (take,)
        solution, resid, *faces = call(
            functools.partial(increment_kernel, first, last),
            [block, block] + ([] if last else [face] * 4),
            args,
            scalars=1,
            flops=square_flops + gather_flops * (1 if last else 2),
        )
    return (solution[None], resid[None])


def solution(mesh):
    in_specs = (
        P(("sub", "grid"), None, None),
        P(("sub", "grid")),
        P(("sub", "grid"), None, None),
        P(("sub", "grid"), None),
        P(("sub", "grid"), None, None),
        P(("sub", "grid"), None, None),
        P(("sub", "grid"), None),
        P(("sub", "grid"), None, None),
        P("grid", "sub"),
    )
    out_specs = (P(("sub", "grid"), None, None), P(("sub", "grid"), None, None))
    return jax.shard_map(body, mesh=mesh, in_specs=in_specs, out_specs=out_specs, check_vma=False)
```

time: 502 us -> 177 us (0.35)
  waiting for transfers between devices: 252 us -> 35.2 us
  blocking collectives: 83 us -> 51 us
  matrix products: 30.9 us -> 0 us
  other arithmetic: 29.4 us -> 2.26 us
  Pallas kernels: 0 us -> 18.9 us
  between operations: 15.2 us -> 1.7 us
  local copies, waits for them, and re-layouts: 33.5 us -> 20.5 us
  starting transfers between devices: 53.1 us -> 45.8 us
    psum x2 -> x0, waiting for transfers between devices: 222 us -> none  [body(): totals = lax.psum(partial_rows, 'sub')]
    all_gather x2 -> x0, blocking collectives: 83 us -> none  [body(): gathered = lax.all_gather(coarse_in, 'grid', axis=0, tiled=True)]
    all_to_all x0 -> x2, blocking collectives: none -> 51 us  [body(): gathered = lax.all_to_all(coarse_in, 'grid', 0, 0)]
    dot_general x10 -> x0, matrix products: 30.9 us -> none  [the longest x4 16.4 us: local_product(): return jnp.dot(matrix, vector, preferred_element_type=jnp.float32)]
    scatter-add x4 -> x0, other arithmetic: 21.2 us -> none  [assemble(): values.at[rows.reshape(-1)].add(received.reshape(-1, values.shape[1]))]
    pallas_call x0 -> x12, Pallas kernels: none -> 18.9 us  [call(): pl.pallas_call(kernel, out_shape=outs, in_specs=specs, out_specs=[pl.Bloc...]
    ppermute x16 -> x18, starting transfers between devices: 53 us -> 34.7 us  [swap(): lax.ppermute(array, axis, [(i, j) for i, j in pairs if 0 <= j < size])]
    unnamed x16 -> x59, local copies, waits for them, and re-layouts: 5.35 us -> 20.1 us
  transfers between devices with their start and end apart: 18 -> 20, of which waited for: 12 -> 12; matrix products, arithmetic and copies ran while one was open for 1% -> 1% of each run, Pallas kernels for 0% -> 1%
where the time goes in v1:
time: 177 us; the launch traced here: 175 us
  blocking collectives  51 us (29%)
  starting transfers between devices  45.8 us (26%)
  waiting for transfers between devices  35.2 us (20%)
  local copies, waits for them, and re-layouts  20.5 us (12%)
  Pallas kernels  18.9 us (11%)
  other arithmetic  2.26 us (1%)
    all_to_all x2, blocking collectives, body(): gathered = lax.all_to_all(coarse_in, 'grid', 0, 0)  51 us
    ppermute x18, starting transfers between devices, swap(): lax.ppermute(array, axis, [(i, j) for i, j in pairs if 0 <= j < size])  34.7 us
    ppermute x18, waiting for transfers between devices, swap(): lax.ppermute(array, axis, [(i, j) for i, j in pairs if 0 <= j < size])  32.6 us
    unnamed x59, local copies, waits for them, and re-layouts  20.1 us
    pallas_call x12, Pallas kernels, call(): pl.pallas_call(kernel, out_shape=outs, in_specs=specs, out_specs=[pl.Bloc...  18.9 us
    all_to_all x2, starting transfers between devices, body(): parts = lax.all_to_all(parts, 'sub', 0, 0, axis_index_groups=groups)  11.1 us
  transfers between devices with their start and end apart: 20, of which 12 were waited for; matrix products, arithmetic and copies ran while one was open for 1% of the time, Pallas kernels for 1%

profile of v1, /device:TPU:72, one launch (start us, length us, event | category | flops | bytes accessed | tf_op | source)
XLA Modules:
  0.0 175.3 jit_solution(325749710289298011)
XLA Ops:
  2.3 1.3 copy-done.27
  4.8 3.8 %collective-permute-start.1 = (f32[128,256]{1,0:T(8,128)S(1)}, f32[128,256]{1,0:T(8,128)S(1)}, u32[]{:S(2)}, u32[]{:S(2)}) collective-permute-start(f32[128,256]{1,0:T(8,128)S(1)} %get-tuple-element.39), channel_id=1, source_target_pairs={{16,32},{32,16},{48,64},{64,48},{80,96},{96,80},{112,128},{128,112... | collective-permute-start | bytes 393224 | tf_op jit(solution)/shard_map/ppermute | solution.py:135
  8.8 6.9 %collective-permute-start.3 = (f32[128,256]{1,0:T(8,128)S(1)}, f32[128,256]{1,0:T(8,128)S(1)}, u32[]{:S(2)}, u32[]{:S(2)}) collective-permute-start(f32[128,256]{1,0:T(8,128)S(1)} %get-tuple-element.41), channel_id=1, source_target_pairs={{1,2},{2,1},{3,4},{4,3},{5,6},{6,5},{7,8},{8,7},{9,10},{10,9},{11,... | collective-permute-start | bytes 393224 | tf_op jit(solution)/shard_map/ppermute | solution.py:135
  16.1 3.3 %collective-permute-done.3.f3 = f32[128,256]{1,0:T(8,128)S(1)} collective-permute-done((f32[128,256]{1,0:T(8,128)S(1)}, f32[128,256]{1,0:T(8,128)S(1)}, u32[]{:S(2)}, u32[]{:S(2)}) %collective-permute-start.3) | collective-permute-done | bytes 131104 | tf_op jit(solution)/shard_map/ppermute | solution.py:135
  20.5 26.9 %all_to_all.20.gathered = f32[16,32,256]{2,1,0:T(8,128)S(1)} all-to-all(f32[16,32,256]{2,1,0:T(8,128)S(1)} %get-tuple-element.46), channel_id=1, replica_groups=mesh['sub'=16,'grid'=16] {'grid'}, dimensions={0} | all-to-all | bytes 1048576 | tf_op jit(solution)/shard_map/all_to_all | solution.py:208
  48.1 1.5 collective-permute-done.4
  50.4 6.6 %all-to-all-start.1 = ((f32[8,32,256]{2,1,0:T(8,128)}), f32[8,32,256]{2,1,0:T(8,128)}, u32[]{:S(2)}, u32[]{:S(2)}) async-start(f32[8,32,256]{2,1,0:T(8,128)} %bitcast.10), calls=%async_computation.1 | async-start | bytes 524288 | tf_op jit(solution)/shard_map/all_to_all | solution.py:220
  57.9 1.7 copy-done
  61.7 1.4 all-to-all-done.1.parts
  64.0 3.4 %shard_map.109 = (f32[1152,256]{1,0:T(8,128)S(1)}, f32[128,256]{1,0:T(8,128)}, f32[128,256]{1,0:T(8,128)}, f32[128,256]{1,0:T(8,128)}, f32[128,256]{1,0:T(8,128)}) custom-call(s32[1]{0:T(128)S(6)} %copy.21.length.refs_0_, f32[1152,256]{1,0:T(8,128)S(1)} %shard_map.107.local, bf16[1152,32]{1,0:T(8,128)(2,1)S(1)} %bitcast.22, ...), custom_call_target="tpu_custom_call" | custom-call | flops 603979776 | bytes 4399108 | tf_op jit(solution)/shard_map/pallas_call | solution.py:114
  68.5 4.0 %collective-permute-start.6 = (f32[128,256]{1,0:T(8,128)}, f32[128,256]{1,0:T(8,128)S(1)}, u32[]{:S(2)}, u32[]{:S(2)}) collective-permute-start(f32[128,256]{1,0:T(8,128)} %get-tuple-element.52), channel_id=1, source_target_pairs={{16,32},{32,16},{48,64},{64,48},{80,96},{96,80},{112,128},{128,112... | collective-permute-start | bytes 393224 | tf_op jit(solution)/shard_map/ppermute | solution.py:135
  72.4 3.0 %collective-permute-start.7 = (f32[128,256]{1,0:T(8,128)}, f32[128,256]{1,0:T(8,128)S(1)}, u32[]{:S(2)}, u32[]{:S(2)}) collective-permute-start(f32[128,256]{1,0:T(8,128)} %get-tuple-element.53), channel_id=1, source_target_pairs={{0,1},{1,0},{2,3},{3,2},{4,5},{5,4},{6,7},{7,6},{8,9},{9,8},{10,11... | collective-permute-start | bytes 393224 | tf_op jit(solution)/shard_map/ppermute | solution.py:135
  75.5 2.3 %collective-permute-start.8 = (f32[128,256]{1,0:T(8,128)}, f32[128,256]{1,0:T(8,128)S(1)}, u32[]{:S(2)}, u32[]{:S(2)}) collective-permute-start(f32[128,256]{1,0:T(8,128)} %get-tuple-element.54), channel_id=1, source_target_pairs={{1,2},{2,1},{3,4},{4,3},{5,6},{6,5},{7,8},{8,7},{9,10},{10,9},{11,... | collective-permute-start | bytes 393224 | tf_op jit(solution)/shard_map/ppermute | solution.py:135
  78.1 5.2 %collective-permute-done.7.refs_4_ = f32[128,256]{1,0:T(8,128)S(1)} collective-permute-done((f32[128,256]{1,0:T(8,128)}, f32[128,256]{1,0:T(8,128)S(1)}, u32[]{:S(2)}, u32[]{:S(2)}) %collective-permute-start.7) | collective-permute-done | bytes 131104 | tf_op jit(solution)/shard_map/ppermute | solution.py:135
  83.3 3.4 %collective-permute-done.8.refs_5_ = f32[128,256]{1,0:T(8,128)S(1)} collective-permute-done((f32[128,256]{1,0:T(8,128)}, f32[128,256]{1,0:T(8,128)S(1)}, u32[]{:S(2)}, u32[]{:S(2)}) %collective-permute-start.8) | collective-permute-done | bytes 131104 | tf_op jit(solution)/shard_map/ppermute | solution.py:135
  86.7 1.7 copy-done.2
  91.0 3.5 %shard_map.110 = (f32[1152,256]{1,0:T(8,128)S(1)}, f32[1152,256]{1,0:T(8,128)S(1)}, f32[128,256]{1,0:T(8,128)S(1)}, f32[128,256]{1,0:T(8,128)S(1)}, f32[128,256]{1,0:T(8,128)S(1)}, /*index=5*/f32[128,256]{1,0:T(8,128)S(1)}) custom-call(s32[1]{0:T(128)S(6)} %copy.21.length.refs_0_, f32[1152,256]{1,0:T(8,128)S(1)} %copy-done.19, ...), custom_call_target="tpu_custom_call" | custom-call | flops 1887436800 | bytes 10785284 | tf_op jit(solution)/shard_map/pallas_call | solution.py:114
  95.6 1.9 %collective-permute-start.10 = (f32[128,256]{1,0:T(8,128)S(1)}, f32[128,256]{1,0:T(8,128)S(1)}, u32[]{:S(2)}, u32[]{:S(2)}) collective-permute-start(f32[128,256]{1,0:T(8,128)S(1)} %get-tuple-element.57), channel_id=1, source_target_pairs={{16,32},{32,16},{48,64},{64,48},{80,96},{96,80},{112,128},{128,112... | collective-permute-start | bytes 393224 | tf_op jit(solution)/shard_map/ppermute | solution.py:135
  97.7 4.2 %collective-permute-start.12 = (f32[128,256]{1,0:T(8,128)S(1)}, f32[128,256]{1,0:T(8,128)S(1)}, u32[]{:S(2)}, u32[]{:S(2)}) collective-permute-start(f32[128,256]{1,0:T(8,128)S(1)} %get-tuple-element.59), channel_id=1, source_target_pairs={{1,2},{2,1},{3,4},{4,3},{5,6},{6,5},{7,8},{8,7},{9,10},{10,9},{11,... | collective-permute-start | bytes 393224 | tf_op jit(solution)/shard_map/ppermute | solution.py:135
  101.9 4.7 %collective-permute-done.10.f1 = f32[128,256]{1,0:T(8,128)S(1)} collective-permute-done((f32[128,256]{1,0:T(8,128)S(1)}, f32[128,256]{1,0:T(8,128)S(1)}, u32[]{:S(2)}, u32[]{:S(2)}) %collective-permute-start.10) | collective-permute-done | bytes 131104 | tf_op jit(solution)/shard_map/ppermute | solution.py:135
  106.6 3.8 %collective-permute-done.12.f3 = f32[128,256]{1,0:T(8,128)S(1)} collective-permute-done((f32[128,256]{1,0:T(8,128)S(1)}, f32[128,256]{1,0:T(8,128)S(1)}, u32[]{:S(2)}, u32[]{:S(2)}) %collective-permute-start.12) | collective-permute-done | bytes 131104 | tf_op jit(solution)/shard_map/ppermute | solution.py:135
  111.5 24.1 %all_to_all.21.gathered = f32[16,32,256]{2,1,0:T(8,128)S(1)} all-to-all(f32[16,32,256]{2,1,0:T(8,128)S(1)} %get-tuple-element.61), channel_id=1, replica_groups=mesh['sub'=16,'grid'=16] {'grid'}, dimensions={0} | all-to-all | bytes 1048576 | tf_op jit(solution)/shard_map/all_to_all | solution.py:208
  136.3 1.5 collective-permute-done.13
  138.5 4.5 %all-to-all-start.3 = ((f32[8,32,256]{2,1,0:T(8,128)}), f32[8,32,256]{2,1,0:T(8,128)S(1)}, u32[]{:S(2)}, u32[]{:S(2)}) async-start(f32[8,32,256]{2,1,0:T(8,128)} %bitcast.13), calls=%async_computation.3 | async-start | bytes 524288 | tf_op jit(solution)/shard_map/all_to_all | solution.py:220
  143.0 1.7 copy-done.1
  150.2 1.7 shard_map.114
  152.0 3.9 %collective-permute-start.15 = (f32[128,256]{1,0:T(8,128)S(1)}, f32[128,256]{1,0:T(8,128)S(1)}, u32[]{:S(2)}, u32[]{:S(2)}) collective-permute-start(f32[128,256]{1,0:T(8,128)S(1)} %get-tuple-element.66), channel_id=1, source_target_pairs={{16,32},{32,16},{48,64},{64,48},{80,96},{96,80},{112,128},{128,112... | collective-permute-start | bytes 393224 | tf_op jit(solution)/shard_map/ppermute | solution.py:135
  156.0 2.1 %collective-permute-start.16 = (f32[128,256]{1,0:T(8,128)S(1)}, f32[128,256]{1,0:T(8,128)S(1)}, u32[]{:S(2)}, u32[]{:S(2)}) collective-permute-start(f32[128,256]{1,0:T(8,128)S(1)} %get-tuple-element.67), channel_id=1, source_target_pairs={{0,1},{1,0},{2,3},{3,2},{4,5},{5,4},{6,7},{7,6},{8,9},{9,8},{10,11... | collective-permute-start | bytes 393224 | tf_op jit(solution)/shard_map/ppermute | solution.py:135
  158.1 1.9 %collective-permute-start.17 = (f32[128,256]{1,0:T(8,128)S(1)}, f32[128,256]{1,0:T(8,128)S(1)}, u32[]{:S(2)}, u32[]{:S(2)}) collective-permute-start(f32[128,256]{1,0:T(8,128)S(1)} %get-tuple-element.68), channel_id=1, source_target_pairs={{1,2},{2,1},{3,4},{4,3},{5,6},{6,5},{7,8},{8,7},{9,10},{10,9},{11,... | collective-permute-start | bytes 393224 | tf_op jit(solution)/shard_map/ppermute | solution.py:135
  160.8 4.3 %collective-permute-done.16.refs_4_ = f32[128,256]{1,0:T(8,128)S(1)} collective-permute-done((f32[128,256]{1,0:T(8,128)S(1)}, f32[128,256]{1,0:T(8,128)S(1)}, u32[]{:S(2)}, u32[]{:S(2)}) %collective-permute-start.16) | collective-permute-done | bytes 131104 | tf_op jit(solution)/shard_map/ppermute | solution.py:135
  165.1 4.1 %collective-permute-done.17.refs_5_ = f32[128,256]{1,0:T(8,128)S(1)} collective-permute-done((f32[128,256]{1,0:T(8,128)S(1)}, f32[128,256]{1,0:T(8,128)S(1)}, u32[]{:S(2)}, u32[]{:S(2)}) %collective-permute-start.17) | collective-permute-done | bytes 131104 | tf_op jit(solution)/shard_map/ppermute | solution.py:135
  171.7 3.7 %shard_map.115 = (f32[1152,256]{1,0:T(8,128)}, f32[1152,256]{1,0:T(8,128)}) custom-call(s32[1]{0:T(128)S(6)} %copy.21.length.refs_0_, f32[1152,256]{1,0:T(8,128)S(1)} %get-tuple-element.64.refs_1_, f32[128,256]{1,0:T(8,128)S(1)} %collective-permute-done.14.refs_2_, f32[128,256]{1,0:T(8,128)S(1)} %collective-permute-done.15.refs_3_, ...), custom_call_target="tpu_custom_call" | custom-call | flops 1283457024 | bytes 10260996 | tf_op jit(solution)/shard_map/pallas_call | solution.py:114
  (91 shorter events, 25.2 us)
Async XLA Ops:
  3.7 15.8 %copy-start.21 = (bf16[1,32,1152]{2,1,0:T(8,128)(2,1)S(1)}, bf16[1,32,1152]{2,1,0:T(8,128)(2,1)}, u32[]{:S(2)}) copy-start(bf16[1,32,1152]{2,1,0:T(8,128)(2,1)} %param.16) | copy-start | bytes 221188
  4.7 15.7 %copy-start.6 = (f32[1152,256]{1,0:T(8,128)}, f32[1152,256]{1,0:T(8,128)S(1)}, u32[]{:S(2)}) copy-start(f32[1152,256]{1,0:T(8,128)S(1)} %get-tuple-element.37.resid.refs_9_) | copy-start | bytes 3538948
  4.7 11.4 %collective-permute-start = (f32[128,256]{1,0:T(8,128)S(1)}, f32[128,256]{1,0:T(8,128)S(1)}, u32[]{:S(2)}, u32[]{:S(2)}) collective-permute-start(f32[128,256]{1,0:T(8,128)S(1)} %get-tuple-element.38), channel_id=1, source_target_pairs={{0,16},{16,0},{32,48},{48,32},{64,80},{80,64},{96,112},{112,96},{1... | collective-permute-start | bytes 393224 | tf_op jit(solution)/shard_map/ppermute | solution.py:135
  4.8 11.3 %collective-permute-start.1 = (f32[128,256]{1,0:T(8,128)S(1)}, f32[128,256]{1,0:T(8,128)S(1)}, u32[]{:S(2)}, u32[]{:S(2)}) collective-permute-start(f32[128,256]{1,0:T(8,128)S(1)} %get-tuple-element.39), channel_id=1, source_target_pairs={{16,32},{32,16},{48,64},{64,48},{80,96},{96,80},{112,128},{128,112... | collective-permute-start | bytes 393224 | tf_op jit(solution)/shard_map/ppermute | solution.py:135
  8.7 7.5 %collective-permute-start.2 = (f32[128,256]{1,0:T(8,128)S(1)}, f32[128,256]{1,0:T(8,128)S(1)}, u32[]{:S(2)}, u32[]{:S(2)}) collective-permute-start(f32[128,256]{1,0:T(8,128)S(1)} %get-tuple-element.40), channel_id=1, source_target_pairs={{0,1},{1,0},{2,3},{3,2},{4,5},{5,4},{6,7},{7,6},{8,9},{9,8},{10,11... | collective-permute-start | bytes 393224 | tf_op jit(solution)/shard_map/ppermute | solution.py:135
  8.8 10.7 %collective-permute-start.3 = (f32[128,256]{1,0:T(8,128)S(1)}, f32[128,256]{1,0:T(8,128)S(1)}, u32[]{:S(2)}, u32[]{:S(2)}) collective-permute-start(f32[128,256]{1,0:T(8,128)S(1)} %get-tuple-element.41), channel_id=1, source_target_pairs={{1,2},{2,1},{3,4},{4,3},{5,6},{6,5},{7,8},{8,7},{9,10},{10,9},{11,... | collective-permute-start | bytes 393224 | tf_op jit(solution)/shard_map/ppermute | solution.py:135
  16.1 31.3 %copy-start.12 = (bf16[512,512]{1,0:T(8,128)(2,1)}, bf16[512,512]{1,0:T(8,128)(2,1)S(1)}, u32[]{:S(2)}) copy-start(bf16[512,512]{1,0:T(8,128)(2,1)S(1)} %get-tuple-element.44.high) | copy-start | bytes 1572868
  16.1 31.3 %copy-start.14 = (bf16[512,512]{1,0:T(8,128)(2,1)}, bf16[512,512]{1,0:T(8,128)(2,1)S(1)}, u32[]{:S(2)}) copy-start(bf16[512,512]{1,0:T(8,128)(2,1)S(1)} %get-tuple-element.45.low) | copy-start | bytes 1572868
  20.5 27.5 %copy-start.25 = (bf16[1152,256]{1,0:T(8,128)(2,1)}, bf16[1152,256]{1,0:T(8,128)(2,1)S(1)}, u32[]{:S(2)}) copy-start(bf16[1152,256]{1,0:T(8,128)(2,1)S(1)} %get-tuple-element.43.assembled) | copy-start | bytes 1769476
  48.0 1.6 collective-permute-start.4
  50.4 12.7 %all-to-all-start.1 = ((f32[8,32,256]{2,1,0:T(8,128)}), f32[8,32,256]{2,1,0:T(8,128)}, u32[]{:S(2)}, u32[]{:S(2)}) async-start(f32[8,32,256]{2,1,0:T(8,128)} %bitcast.10), calls=%async_computation.1 | async-start | bytes 524288 | tf_op jit(solution)/shard_map/all_to_all | solution.py:220
  64.0 13.8 %copy-start.28 = (f32[1,1152]{1,0:T(1,128)S(1)}, f32[1,1152]{1,0:T(1,128)}, u32[]{:S(2)}) copy-start(f32[1,1152]{1,0:T(1,128)} %param.15) | copy-start | bytes 13828
  68.5 9.6 %collective-permute-start.5 = (f32[128,256]{1,0:T(8,128)}, f32[128,256]{1,0:T(8,128)S(1)}, u32[]{:S(2)}, u32[]{:S(2)}) collective-permute-start(f32[128,256]{1,0:T(8,128)} %get-tuple-element.51), channel_id=1, source_target_pairs={{0,16},{16,0},{32,48},{48,32},{64,80},{80,64},{96,112},{112,96},{1... | collective-permute-start | bytes 393224 | tf_op jit(solution)/shard_map/ppermute | solution.py:135
  68.5 9.6 %collective-permute-start.6 = (f32[128,256]{1,0:T(8,128)}, f32[128,256]{1,0:T(8,128)S(1)}, u32[]{:S(2)}, u32[]{:S(2)}) collective-permute-start(f32[128,256]{1,0:T(8,128)} %get-tuple-element.52), channel_id=1, source_target_pairs={{16,32},{32,16},{48,64},{64,48},{80,96},{96,80},{112,128},{128,112... | collective-permute-start | bytes 393224 | tf_op jit(solution)/shard_map/ppermute | solution.py:135
  72.4 10.9 %collective-permute-start.7 = (f32[128,256]{1,0:T(8,128)}, f32[128,256]{1,0:T(8,128)S(1)}, u32[]{:S(2)}, u32[]{:S(2)}) collective-permute-start(f32[128,256]{1,0:T(8,128)} %get-tuple-element.53), channel_id=1, source_target_pairs={{0,1},{1,0},{2,3},{3,2},{4,5},{5,4},{6,7},{7,6},{8,9},{9,8},{10,11... | collective-permute-start | bytes 393224 | tf_op jit(solution)/shard_map/ppermute | solution.py:135
  75.5 11.2 %collective-permute-start.8 = (f32[128,256]{1,0:T(8,128)}, f32[128,256]{1,0:T(8,128)S(1)}, u32[]{:S(2)}, u32[]{:S(2)}) collective-permute-start(f32[128,256]{1,0:T(8,128)} %get-tuple-element.54), channel_id=1, source_target_pairs={{1,2},{2,1},{3,4},{4,3},{5,6},{6,5},{7,8},{8,7},{9,10},{10,9},{11,... | collective-permute-start | bytes 393224 | tf_op jit(solution)/shard_map/ppermute | solution.py:135
  91.0 19.4 %copy-start.22 = (bf16[1,32,1152]{2,1,0:T(8,128)(2,1)S(1)}, bf16[1,32,1152]{2,1,0:T(8,128)(2,1)}, u32[]{:S(2)}) copy-start(bf16[1,32,1152]{2,1,0:T(8,128)(2,1)} %param.16) | copy-start | bytes 221188
  95.6 15.8 %copy-start.4 = (f32[1152,256]{1,0:T(8,128)}, f32[1152,256]{1,0:T(8,128)S(1)}, u32[]{:S(2)}) copy-start(f32[1152,256]{1,0:T(8,128)S(1)} %get-tuple-element.55.resid.refs_9_) | copy-start | bytes 3538948
  95.6 6.2 %collective-permute-start.9 = (f32[128,256]{1,0:T(8,128)S(1)}, f32[128,256]{1,0:T(8,128)S(1)}, u32[]{:S(2)}, u32[]{:S(2)}) collective-permute-start(f32[128,256]{1,0:T(8,128)S(1)} %get-tuple-element.56), channel_id=1, source_target_pairs={{0,16},{16,0},{32,48},{48,32},{64,80},{80,64},{96,112},{112,96},{1... | collective-permute-start | bytes 393224 | tf_op jit(solution)/shard_map/ppermute | solution.py:135
  95.6 10.9 %collective-permute-start.10 = (f32[128,256]{1,0:T(8,128)S(1)}, f32[128,256]{1,0:T(8,128)S(1)}, u32[]{:S(2)}, u32[]{:S(2)}) collective-permute-start(f32[128,256]{1,0:T(8,128)S(1)} %get-tuple-element.57), channel_id=1, source_target_pairs={{16,32},{32,16},{48,64},{64,48},{80,96},{96,80},{112,128},{128,112... | collective-permute-start | bytes 393224 | tf_op jit(solution)/shard_map/ppermute | solution.py:135
  97.6 9.0 %collective-permute-start.11 = (f32[128,256]{1,0:T(8,128)S(1)}, f32[128,256]{1,0:T(8,128)S(1)}, u32[]{:S(2)}, u32[]{:S(2)}) collective-permute-start(f32[128,256]{1,0:T(8,128)S(1)} %get-tuple-element.58), channel_id=1, source_target_pairs={{0,1},{1,0},{2,3},{3,2},{4,5},{5,4},{6,7},{7,6},{8,9},{9,8},{10,11... | collective-permute-start | bytes 393224 | tf_op jit(solution)/shard_map/ppermute | solution.py:135
  97.7 12.7 %collective-permute-start.12 = (f32[128,256]{1,0:T(8,128)S(1)}, f32[128,256]{1,0:T(8,128)S(1)}, u32[]{:S(2)}, u32[]{:S(2)}) collective-permute-start(f32[128,256]{1,0:T(8,128)S(1)} %get-tuple-element.59), channel_id=1, source_target_pairs={{1,2},{2,1},{3,4},{4,3},{5,6},{6,5},{7,8},{8,7},{9,10},{10,9},{11,... | collective-permute-start | bytes 393224 | tf_op jit(solution)/shard_map/ppermute | solution.py:135
  110.4 25.2 %copy-start.13 = (bf16[512,512]{1,0:T(8,128)(2,1)S(1)}, bf16[512,512]{1,0:T(8,128)(2,1)}, u32[]{:S(2)}) copy-start(bf16[512,512]{1,0:T(8,128)(2,1)} %copy-done.12) | copy-start | bytes 1572868
  110.4 25.2 %copy-start.15 = (bf16[512,512]{1,0:T(8,128)(2,1)S(1)}, bf16[512,512]{1,0:T(8,128)(2,1)}, u32[]{:S(2)}) copy-start(bf16[512,512]{1,0:T(8,128)(2,1)} %copy-done.14) | copy-start | bytes 1572868
  111.4 24.7 %copy-start.23 = (bf16[1152,256]{1,0:T(8,128)(2,1)}, bf16[1152,256]{1,0:T(8,128)(2,1)S(1)}, u32[]{:S(2)}) copy-start(bf16[1152,256]{1,0:T(8,128)(2,1)S(1)} %get-tuple-element.60.assembled) | copy-start | bytes 1769476
  136.2 1.6 collective-permute-start.13
  138.5 10.4 %all-to-all-start.3 = ((f32[8,32,256]{2,1,0:T(8,128)}), f32[8,32,256]{2,1,0:T(8,128)S(1)}, u32[]{:S(2)}, u32[]{:S(2)}) async-start(f32[8,32,256]{2,1,0:T(8,128)} %bitcast.13), calls=%async_computation.3 | async-start | bytes 524288 | tf_op jit(solution)/shard_map/all_to_all | solution.py:220
  150.2 18.9 %copy-start.3 = (bf16[1,1152,1152]{2,1,0:T(8,128)(2,1)S(1)}, bf16[1,1152,1152]{2,1,0:T(8,128)(2,1)}, u32[]{:S(2)}) copy-start(bf16[1,1152,1152]{2,1,0:T(8,128)(2,1)} %param.14) | copy-start | bytes 7962628
  151.9 8.1 %collective-permute-start.14 = (f32[128,256]{1,0:T(8,128)S(1)}, f32[128,256]{1,0:T(8,128)S(1)}, u32[]{:S(2)}, u32[]{:S(2)}) collective-permute-start(f32[128,256]{1,0:T(8,128)S(1)} %get-tuple-element.65), channel_id=1, source_target_pairs={{0,16},{16,0},{32,48},{48,32},{64,80},{80,64},{96,112},{112,96},{1... | collective-permute-start | bytes 393224 | tf_op jit(solution)/shard_map/ppermute | solution.py:135
  152.0 8.7 %collective-permute-start.15 = (f32[128,256]{1,0:T(8,128)S(1)}, f32[128,256]{1,0:T(8,128)S(1)}, u32[]{:S(2)}, u32[]{:S(2)}) collective-permute-start(f32[128,256]{1,0:T(8,128)S(1)} %get-tuple-element.66), channel_id=1, source_target_pairs={{16,32},{32,16},{48,64},{64,48},{80,96},{96,80},{112,128},{128,112... | collective-permute-start | bytes 393224 | tf_op jit(solution)/shard_map/ppermute | solution.py:135
  156.0 9.1 %collective-permute-start.16 = (f32[128,256]{1,0:T(8,128)S(1)}, f32[128,256]{1,0:T(8,128)S(1)}, u32[]{:S(2)}, u32[]{:S(2)}) collective-permute-start(f32[128,256]{1,0:T(8,128)S(1)} %get-tuple-element.67), channel_id=1, source_target_pairs={{0,1},{1,0},{2,3},{3,2},{4,5},{5,4},{6,7},{7,6},{8,9},{9,8},{10,11... | collective-permute-start | bytes 393224 | tf_op jit(solution)/shard_map/ppermute | solution.py:135
  158.1 11.0 %collective-permute-start.17 = (f32[128,256]{1,0:T(8,128)S(1)}, f32[128,256]{1,0:T(8,128)S(1)}, u32[]{:S(2)}, u32[]{:S(2)}) collective-permute-start(f32[128,256]{1,0:T(8,128)S(1)} %get-tuple-element.68), channel_id=1, source_target_pairs={{1,2},{2,1},{3,4},{4,3},{5,6},{6,5},{7,8},{8,7},{9,10},{10,9},{11,... | collective-permute-start | bytes 393224 | tf_op jit(solution)/shard_map/ppermute | solution.py:135
  (17 other events, 35.7 us)

commit v2 on v1

v2 whole, which is shorter than its diff:
```python
import jax
import jax.numpy as jnp
from jax import lax
from jax.experimental import pallas as pl
from jax.experimental.pallas import tpu as pltpu
from jax.sharding import PartitionSpec as P

ITERS = 2
CHUNKS = 4
VMEM_LIMIT = 32 * 1024 * 1024
F32 = jnp.float32
BF16 = jnp.bfloat16


def dot(a, b):
    return jnp.dot(a, b, preferred_element_type=F32)


def halves(v):
    high = v.astype(BF16)
    return high, (v - high.astype(F32)).astype(BF16)


def pick(onehot, v):
    high, low = halves(v)
    return dot(onehot, high) + dot(onehot, low)


def live_of(length_ref, n):
    return (lax.broadcasted_iota(jnp.int32, (n, 1), 0) < length_ref[0]).astype(F32)


def onehot(rows, shape, axis):
    spot = lax.broadcasted_iota(jnp.int32, shape, axis)
    return (rows == spot).astype(F32).astype(BF16)


def store_faces(faces, refs):
    share = refs[0].shape[0]
    for j, ref in enumerate(refs):
        ref[...] = faces[j * share : (j + 1) * share]


def load_faces(refs):
    return jnp.concatenate([ref[...] for ref in refs], axis=0)


def chunks(n):
    return [slice(j * (n // CHUNKS), (j + 1) * (n // CHUNKS)) for j in range(CHUNKS)]


def chunk_copies(source, target, sems):
    return [
        pltpu.make_async_copy(source.at[part], target.at[part], sems.at[j])
        for j, part in enumerate(chunks(target.shape[0]))
    ]


def begin_kernel(length, rows, loads, resid, take, f0, f1, f2, f3, sems):
    n = resid.shape[0]
    copies = chunk_copies(loads, resid, sems)
    for copy in copies:
        copy.start()
    take[...] = onehot(rows[...], take.shape, 1)
    for copy in copies:
        copy.wait()
    resid[...] = resid[...] * live_of(length, n)
    store_faces(pick(take[...], resid[...]), (f0, f1, f2, f3))


def tables_kernel(rows, coarse, put, coarse_high, coarse_low):
    put[...] = onehot(rows[...], put.shape, 0)
    high, low = halves(coarse[...])
    coarse_high[...] = high
    coarse_low[...] = low


def coarse_in_kernel(resid, f0, f1, f2, f3, put, basis, assembled, coarse_in, token):
    token[...] = jnp.zeros_like(token)
    received = load_faces((f0, f1, f2, f3))
    assembled[...] = (resid[...] + pick(put[...], received)).astype(BF16)
    block = dot(basis[...], assembled[...])
    for j in range(coarse_in.shape[0]):
        coarse_in[j] = block


def local_kernel(inverse, assembled, take, local, local_faces, token):
    local[...] = dot(inverse[...], assembled[...])
    local_faces[...] = pick(take[...], local[...])
    token[...] = jnp.zeros_like(token)


def coarse_kernel(core, high, low, gathered, after, after_too, keep, send):
    groups, modes, loads = gathered.shape
    g_high, g_low = halves(gathered[...].reshape(groups * modes, loads))
    out = dot(high[...], g_high) + dot(high[...], g_low) + dot(low[...], g_high)
    pairs = out.reshape(-1, 2, modes, loads)
    even = pairs[:, 0].reshape(keep.shape)
    odd = pairs[:, 1].reshape(keep.shape)
    first = core[0] == 0
    keep[...] = jnp.where(first, even, odd)
    send[...] = jnp.where(first, odd, even)


def rows_kernel(after, take, offdiag, basis_t, diag_row, offdiag_rows, basis_rows, diag_rows, token):
    token[...] = after[...]
    basis_rows[...] = dot(take[...], basis_t[...]).astype(BF16)
    diag_rows[...] = jnp.sum(take[...].astype(F32) * diag_row[...], axis=1, keepdims=True)
    offdiag_rows[...] = dot(take[...], offdiag[...]).astype(BF16)


def columns_kernel(after, offdiag, put, offdiag_columns, token):
    token[...] = after[...]
    offdiag_columns[...] = dot(offdiag[...], put[...]).astype(BF16)


def sent_kernel(parts, local_faces, basis_rows, coarse_out, f0, f1, f2, f3):
    total = jnp.sum(parts[...], axis=0)
    coarse_out[...] = total
    high, low = halves(total)
    rows = basis_rows[...]
    store_faces(local_faces[...] + dot(rows, high) + dot(rows, low), (f0, f1, f2, f3))


def correct(length, local, basis_t, coarse_out):
    high, low = halves(coarse_out[...])
    spread = dot(basis_t[...], high) + dot(basis_t[...], low)
    return live_of(length, local.shape[0]) * (local[...] + spread)


def correction_kernel(length, local, basis_t, coarse_out, correction):
    correction[...] = correct(length, local, basis_t, coarse_out)


def increment_kernel(correction, r0, r1, r2, r3, put, offdiag_rows, diag_rows, c0, c1, c2, c3, p0, p1, p2, p3,
                     increment, g0, g1, g2, g3):
    received = load_faces((r0, r1, r2, r3))
    increment[...] = correction[...] + pick(put[...], received)
    there = load_faces((c0, c1, c2, c3)) + received
    applied = dot(offdiag_rows[...], increment[...].astype(BF16)) + diag_rows[...] * there
    store_faces(load_faces((p0, p1, p2, p3)) - applied, (g0, g1, g2, g3))


def residual_kernel(length, increment, diag, resid, offdiag, resid_out):
    applied = dot(offdiag[...], increment[...].astype(BF16)) + diag[...] * increment[...]
    resid_out[...] = resid[...] - live_of(length, resid.shape[0]) * applied


def own_kernel(length, local, basis_t, coarse_out, before, diag, resid, offdiag,
               solution, resid_out):
    correction = correct(length, local, basis_t, coarse_out)
    solution[...] = before[...] + correction
    applied = dot(offdiag[...], correction.astype(BF16)) + diag[...] * correction
    resid_out[...] = resid[...] - live_of(length, resid.shape[0]) * applied


def finish_kernel(length, r0, r1, r2, r3, put, offdiag_columns, diag, own, own_resid,
                  solution, resid_out, total, rest, total_sems, rest_sems):
    n = own.shape[0]
    totals = chunk_copies(total, solution, total_sems)
    rests = chunk_copies(rest, resid_out, rest_sems)
    high, low = halves(load_faces((r0, r1, r2, r3)))
    live = live_of(length, n)
    for part, leave, leave_too in zip(chunks(n), totals, rests):
        added = dot(put[part], high) + dot(put[part], low)
        total[part] = own[part] + added
        leave.start()
        applied = dot(offdiag_columns[part], high) + diag[part] * added
        rest[part] = own_resid[part] - live[part] * applied
        leave_too.start()
    for copy in totals + rests:
        copy.wait()


def call(kernel, outs, args, places, out_places="", scratch=(), flops=0):
    size = lambda a: a.size * a.dtype.itemsize
    kinds = dict(s=pltpu.SMEM, v=pltpu.VMEM, h=pltpu.HBM)
    out_places = out_places or "v" * len(outs)
    return pl.pallas_call(
        kernel,
        out_shape=outs,
        in_specs=[pl.BlockSpec(memory_space=kinds[c]) for c in places],
        out_specs=[pl.BlockSpec(memory_space=kinds[c]) for c in out_places],
        scratch_shapes=list(scratch),
        compiler_params=pltpu.CompilerParams(vmem_limit_bytes=VMEM_LIMIT),
        cost_estimate=pl.CostEstimate(
            flops=flops,
            bytes_accessed=sum(size(a) for a in args) + sum(size(a) for a in outs),
            transcendentals=0,
        ),
    )(*args)


def like(*shape, dtype=F32):
    return jax.ShapeDtypeStruct(shape, dtype)


def swap(array, axis, odd):
    size = lax.axis_size(axis)
    pairs = [(i, ((i + odd) ^ 1) - odd) for i in range(size)]
    return lax.ppermute(array, axis, [(i, j) for i, j in pairs if 0 <= j < size])


def exchange(faces):
    return (
        swap(faces[0], "grid", 0),
        swap(faces[1], "grid", 1),
        swap(faces[2], "sub", 1),
        swap(faces[3], "sub", 0),
    )


def body(
    load_parts,
    iface_len,
    face_rows,
    face_count,
    local_inverse,
    schur_offdiag,
    schur_diag,
    mode_basis,
    coarse_inverse,
):
    loads = load_parts[0]
    inverse = local_inverse[0]
    offdiag = schur_offdiag[0]
    diag = schur_diag[0][:, None]
    basis = mode_basis[0]
    basis_t = basis.T
    n, nloads = loads.shape
    modes = basis.shape[0]
    share = face_rows.shape[2]
    nsub = lax.axis_size("sub")
    ngrid = lax.axis_size("grid")
    core = lax.rem(lax.axis_index("sub"), 2)
    column = lax.rem(lax.axis_index("grid"), 2)

    usable = jnp.arange(share)[None, :] < face_count[0][:, None]
    rows = jnp.where(usable, face_rows[0], -1)
    rows_grid = jnp.where(column == 0, rows[2:], rows[:1:-1])
    rows_sub = jnp.where(core == 0, rows[1::-1], rows[:2])
    rows = jnp.concatenate([rows_grid, rows_sub], axis=0).reshape(-1)
    nrows = rows.shape[0]
    core = core[None]

    face = like(share, nloads)
    block = like(n, nloads)
    gather_flops = 4 * nrows * n * nloads
    square_flops = 2 * n * n * nloads

    order = coarse_inverse.shape
    sems = pltpu.SemaphoreType.DMA((CHUNKS,))
    mark = like(8, 128)
    resid, take, *sent = call(
        begin_kernel,
        [block, like(nrows, n, dtype=BF16)] + [face] * 4,
        (iface_len, rows[:, None], loads),
        "svh",
        scratch=[sems],
        flops=gather_flops,
    )
    put, coarse_high, coarse_low = call(
        tables_kernel,
        [like(n, nrows, dtype=BF16), like(*order, dtype=BF16), like(*order, dtype=BF16)],
        (rows[None, :], coarse_inverse),
        "vv",
    )
    solution = None
    for sweep in range(ITERS):
        received = exchange(sent)
        assembled, coarse_in, after = call(
            coarse_in_kernel,
            [like(n, nloads, dtype=BF16), like(ngrid, modes, nloads), mark],
            (resid, *received, put, basis),
            "v" * 7,
            flops=gather_flops,
        )
        gathered = lax.all_to_all(coarse_in, "grid", 0, 0)
        local, local_faces, ahead = call(
            local_kernel,
            [block, like(nrows, nloads), mark],
            (inverse, assembled, take),
            "vvv",
            flops=square_flops + gather_flops,
        )
        if sweep == 0:
            offdiag_rows, basis_rows, diag_rows, ahead_too = call(
                rows_kernel,
                [like(nrows, n, dtype=BF16), like(nrows, modes, dtype=BF16), like(nrows, 1), mark],
                (after, take, offdiag, basis_t, schur_diag),
                "vvvvv",
                flops=2 * nrows * n * n,
            )
        else:
            offdiag_columns, ahead_too = call(
                columns_kernel,
                [like(n, nrows, dtype=BF16), mark],
                (after, offdiag, put),
                "vvv",
                flops=2 * nrows * n * n,
            )
        keep, send = call(
            coarse_kernel,
            [like(order[0] // 2, nloads)] * 2,
            (core, coarse_high, coarse_low, gathered, ahead, ahead_too),
            "svvvvv",
            flops=6 * order[0] * order[1] * nloads,
        )
        other = swap(send, "sub", 0)
        parts = (keep + other).reshape(nsub // 2, modes, nloads)
        groups = [list(range(i, nsub, 2)) for i in range(2)]
        parts = lax.all_to_all(parts, "sub", 0, 0, axis_index_groups=groups)
        coarse_out, *corrected = call(
            sent_kernel,
            [like(modes, nloads)] + [face] * 4,
            (parts, local_faces, basis_rows),
            "vvv",
        )
        received = exchange(corrected)
        if sweep < ITERS - 1:
            (correction,) = call(
                correction_kernel, [block], (iface_len, local, basis_t, coarse_out), "svvv"
            )
            increment, *sent = call(
                increment_kernel,
                [block] + [face] * 4,
                (correction, *received, put, offdiag_rows, diag_rows, *corrected, *sent),
                "v" * 16,
                flops=2 * gather_flops,
            )
            (resid,) = call(
                residual_kernel,
                [block],
                (iface_len, increment, diag, resid, offdiag),
                "svvvv",
                flops=square_flops,
            )
            solution = increment if solution is None else solution + increment
        else:
            own, own_resid = call(
                own_kernel,
                [block, block],
                (iface_len, local, basis_t, coarse_out, solution, diag, resid, offdiag),
                "svvvvvvv",
                flops=square_flops,
            )
            solution, resid = call(
                finish_kernel,
                [block, block],
                (iface_len, *received, put, offdiag_columns, diag, own, own_resid),
                "s" + "v" * 9,
                "hh",
                [pltpu.VMEM((n, nloads), F32)] * 2 + [sems] * 2,
                flops=2 * gather_flops,
            )
    return (solution[None], resid[None])


def solution(mesh):
    in_specs = (
        P(("sub", "grid"), None, None),
        P(("sub", "grid")),
        P(("sub", "grid"), None, None),
        P(("sub", "grid"), None),
        P(("sub", "grid"), None, None),
        P(("sub", "grid"), None, None),
        P(("sub", "grid"), None),
        P(("sub", "grid"), None, None),
        P("grid", "sub"),
    )
    out_specs = (P(("sub", "grid"), None, None), P(("sub", "grid"), None, None))
    return jax.shard_map(body, mesh=mesh, in_specs=in_specs, out_specs=out_specs, check_vma=False)
```

time: 177 us -> 158 us (0.89)
  blocking collectives: 51 us -> 23.1 us
  local copies, waits for them, and re-layouts: 20.5 us -> 31.1 us
  waiting for transfers between devices: 35.2 us -> 27.8 us
  Pallas kernels: 18.9 us -> 25.2 us
    all_to_all x2, blocking collectives: 51 us -> 23.1 us  [body(): parts = lax.all_to_all(parts, 'sub', 0, 0, axis_index_groups=groups)]
    ppermute x18, waiting for transfers between devices: 32.6 us -> 20.4 us  [swap(): lax.ppermute(array, axis, [(i, j) for i, j in pairs if 0 <= j < size])]
    unnamed x59 -> x97, local copies, waits for them, and re-layouts: 20.1 us -> 30.6 us
    pallas_call x12 -> x17, Pallas kernels: 18.9 us -> 25.2 us  [call(): pl.pallas_call(kernel, out_shape=outs, in_specs=[pl.BlockSpec(memory_spac...]
    all_to_all x2, waiting for transfers between devices: 2.53 us -> 7.38 us  [body(): gathered = lax.all_to_all(coarse_in, 'grid', 0, 0)]
    all_to_all x2, starting transfers between devices: 11.1 us -> 15.4 us  [body(): gathered = lax.all_to_all(coarse_in, 'grid', 0, 0)]
    ppermute x18, starting transfers between devices: 34.7 us -> 31.8 us  [swap(): lax.ppermute(array, axis, [(i, j) for i, j in pairs if 0 <= j < size])]
  transfers between devices with their start and end apart: 20 -> 20, of which waited for: 12 -> 11; matrix products, arithmetic and copies ran while one was open for 1% -> 0% of each run, Pallas kernels for 1% -> 8%
where the time goes in v2:
time: 158 us; the launch traced here: 157 us
  starting transfers between devices  47.2 us (30%)
  local copies, waits for them, and re-layouts  31.1 us (20%)
  waiting for transfers between devices  27.8 us (18%)
  Pallas kernels  25.2 us (16%)
  blocking collectives  23.1 us (15%)
  between operations  2.03 us (1%)
    ppermute x18, starting transfers between devices, swap(): lax.ppermute(array, axis, [(i, j) for i, j in pairs if 0 <= j < size])  31.8 us
    unnamed x97, local copies, waits for them, and re-layouts  30.6 us
    pallas_call x17, Pallas kernels, call(): pl.pallas_call(kernel, out_shape=outs, in_specs=[pl.BlockSpec(memory_spac...  25.2 us
    all_to_all x2, blocking collectives, body(): parts = lax.all_to_all(parts, 'sub', 0, 0, axis_index_groups=groups)  23.1 us
    ppermute x18, waiting for transfers between devices, swap(): lax.ppermute(array, axis, [(i, j) for i, j in pairs if 0 <= j < size])  20.4 us
    all_to_all x2, starting transfers between devices, body(): gathered = lax.all_to_all(coarse_in, 'grid', 0, 0)  15.4 us
    all_to_all x2, waiting for transfers between devices, body(): gathered = lax.all_to_all(coarse_in, 'grid', 0, 0)  7.38 us
  transfers between devices with their start and end apart: 20, of which 11 were waited for; matrix products, arithmetic and copies ran while one was open for 0% of the time, Pallas kernels for 8%

profile of v2, /device:TPU:72, one launch (start us, length us, event | category | flops | bytes accessed | tf_op | source)
XLA Modules:
  0.0 157.2 jit_solution(17755555150002743702)
XLA Ops:
  6.2 7.8 %collective-permute-start.1 = (f32[128,256]{1,0:T(8,128)S(1)}, f32[128,256]{1,0:T(8,128)S(1)}, u32[]{:S(2)}, u32[]{:S(2)}) collective-permute-start(f32[128,256]{1,0:T(8,128)S(1)} %get-tuple-element.56.p1), channel_id=1, source_target_pairs={{1,2},{2,1},{3,4},{4,3},{5,6},{6,5},{7,8},{8,7},{9,10},{10,9},{11,... | collective-permute-start | bytes 393224 | tf_op jit(solution)/shard_map/ppermute | solution.py:201
  14.1 1.9 %collective-permute-start.2 = (f32[128,256]{1,0:T(8,128)S(1)}, f32[128,256]{1,0:T(8,128)S(1)}, u32[]{:S(2)}, u32[]{:S(2)}) collective-permute-start(f32[128,256]{1,0:T(8,128)S(1)} %get-tuple-element.57.p2), channel_id=1, source_target_pairs={{16,32},{32,16},{48,64},{64,48},{80,96},{96,80},{112,128},{128,112... | collective-permute-start | bytes 393224 | tf_op jit(solution)/shard_map/ppermute | solution.py:201
  17.6 1.7 %collective-permute-done.1.f1 = f32[128,256]{1,0:T(8,128)S(1)} collective-permute-done((f32[128,256]{1,0:T(8,128)S(1)}, f32[128,256]{1,0:T(8,128)S(1)}, u32[]{:S(2)}, u32[]{:S(2)}) %collective-permute-start.1) | collective-permute-done | bytes 131104 | tf_op jit(solution)/shard_map/ppermute | solution.py:201
  19.3 2.6 %collective-permute-done.2.f2 = f32[128,256]{1,0:T(8,128)S(1)} collective-permute-done((f32[128,256]{1,0:T(8,128)S(1)}, f32[128,256]{1,0:T(8,128)S(1)}, u32[]{:S(2)}, u32[]{:S(2)}) %collective-permute-start.2) | collective-permute-done | bytes 131104 | tf_op jit(solution)/shard_map/ppermute | solution.py:201
  24.6 8.1 %all-to-all-start = ((f32[16,32,256]{2,1,0:T(8,128)}), f32[16,32,256]{2,1,0:T(8,128)S(1)}, u32[]{:S(2)}, u32[]{:S(2)}) async-start(f32[16,32,256]{2,1,0:T(8,128)} %copy-done.27), calls=%async_computation | async-start | bytes 1048576 | tf_op jit(solution)/shard_map/all_to_all | solution.py:278
  33.0 1.7 %copy-done.38 = bf16[1,1152,1152]{2,1,0:T(8,128)(2,1)S(1)} copy-done((bf16[1,1152,1152]{2,1,0:T(8,128)(2,1)S(1)}, bf16[1,1152,1152]{2,1,0:T(8,128)(2,1)}, u32[]{:S(2)}) %copy-start.38) | copy-done | bytes 2654232
  37.0 2.9 %shard_map.107 = (f32[1152,256]{1,0:T(8,128)S(1)}, f32[512,256]{1,0:T(8,128)S(1)}, f32[8,128]{1,0:T(8,128)S(1)}) custom-call(bf16[1152,1152]{1,0:T(8,128)(2,1)S(1)} %bitcast.30, bf16[1152,256]{1,0:T(8,128)(2,1)S(1)} %copy-done.42, bf16[512,1152]{1,0:T(8,128)(2,1)S(1)} %copy-done.46), custom_call_target="tpu_custom_call" | custom-call | flops 1283457024 | bytes 6131712 | tf_op jit(solution)/shard_map/pallas_call | solution.py:179
  41.8 2.2 %shard_map.108 = (bf16[512,1152]{1,0:T(8,128)(2,1)S(1)}, bf16[512,32]{1,0:T(8,128)(2,1)S(1)}, f32[512,1]{1,0:T(8,128)S(1)}, f32[8,128]{1,0:T(8,128)S(1)}) custom-call(f32[8,128]{1,0:T(8,128)S(1)} %get-tuple-element.65.after, bf16[512,1152]{1,0:T(8,128)(2,1)S(1)} %copy-done.46, bf16[1152,1152]{1,0:T(8,128)(2,1)S(1)} %bitcast.18, ...), custom_call_target="tpu_custom_call" | custom-call | flops 1358954496 | bytes 5134848 | tf_op jit(solution)/shard_map/pallas_call | solution.py:179
  45.0 4.4 %all-to-all-done.gathered = f32[16,32,256]{2,1,0:T(8,128)S(1)} async-done(((f32[16,32,256]{2,1,0:T(8,128)}), f32[16,32,256]{2,1,0:T(8,128)S(1)}, u32[]{:S(2)}, u32[]{:S(2)}) %all-to-all-start) | async-done | bytes 524320 | tf_op jit(solution)/shard_map/all_to_all | solution.py:278
  51.7 10.8 %all_to_all.20.parts = f32[8,32,256]{2,1,0:T(8,128)S(1)} all-to-all(f32[8,32,256]{2,1,0:T(8,128)S(1)} %bitcast.33), channel_id=1, replica_groups={{0,32,64,96,128,160,192,224},{16,48,80,112,144,176,208,240},{1,33,65,97..., dimensions={0} | all-to-all | bytes 524288 | tf_op jit(solution)/shard_map/all_to_all | solution.py:312
  64.4 2.2 %collective-permute-start.6 = (f32[128,256]{1,0:T(8,128)S(1)}, f32[128,256]{1,0:T(8,128)S(1)}, u32[]{:S(2)}, u32[]{:S(2)}) collective-permute-start(f32[128,256]{1,0:T(8,128)S(1)} %get-tuple-element.73.c1), channel_id=1, source_target_pairs={{1,2},{2,1},{3,4},{4,3},{5,6},{6,5},{7,8},{8,7},{9,10},{10,9},{11,... | collective-permute-start | bytes 393224 | tf_op jit(solution)/shard_map/ppermute | solution.py:201
  66.6 1.9 %collective-permute-start.7 = (f32[128,256]{1,0:T(8,128)S(1)}, f32[128,256]{1,0:T(8,128)S(1)}, u32[]{:S(2)}, u32[]{:S(2)}) collective-permute-start(f32[128,256]{1,0:T(8,128)S(1)} %get-tuple-element.74.c2), channel_id=1, source_target_pairs={{16,32},{32,16},{48,64},{64,48},{80,96},{96,80},{112,128},{128,112... | collective-permute-start | bytes 393224 | tf_op jit(solution)/shard_map/ppermute | solution.py:201
  70.3 4.6 %collective-permute-done.6.r1 = f32[128,256]{1,0:T(8,128)S(1)} collective-permute-done((f32[128,256]{1,0:T(8,128)S(1)}, f32[128,256]{1,0:T(8,128)S(1)}, u32[]{:S(2)}, u32[]{:S(2)}) %collective-permute-start.6) | collective-permute-done | bytes 131104 | tf_op jit(solution)/shard_map/ppermute | solution.py:201
  74.9 2.3 %collective-permute-done.7.r2 = f32[128,256]{1,0:T(8,128)S(1)} collective-permute-done((f32[128,256]{1,0:T(8,128)S(1)}, f32[128,256]{1,0:T(8,128)S(1)}, u32[]{:S(2)}, u32[]{:S(2)}) %collective-permute-start.7) | collective-permute-done | bytes 131104 | tf_op jit(solution)/shard_map/ppermute | solution.py:201
  77.3 2.4 %shard_map.112 = (f32[1152,256]{1,0:T(8,128)S(1)}, f32[128,256]{1,0:T(8,128)}, f32[128,256]{1,0:T(8,128)}, f32[128,256]{1,0:T(8,128)}, f32[128,256]{1,0:T(8,128)}) custom-call(f32[1152,256]{1,0:T(8,128)S(1)} %shard_map.111.correction, f32[128,256]{1,0:T(8,128)S(1)} %collective-permute-done.5.r0, f32[128,256]{1,0:T(8,128)S(1)} %collective-permute-done.6.r1, ...), custom_call_target="tpu_custom_call" | custom-call | flops 1207959552 | bytes 6817792 | tf_op jit(solution)/shard_map/pallas_call | solution.py:179
  80.7 3.4 %collective-permute-start.10 = (f32[128,256]{1,0:T(8,128)}, f32[128,256]{1,0:T(8,128)}, u32[]{:S(2)}, u32[]{:S(2)}) collective-permute-start(f32[128,256]{1,0:T(8,128)} %get-tuple-element.80), channel_id=1, source_target_pairs={{1,2},{2,1},{3,4},{4,3},{5,6},{6,5},{7,8},{8,7},{9,10},{10,9},{11,... | collective-permute-start | bytes 393224 | tf_op jit(solution)/shard_map/ppermute | solution.py:201
  84.1 1.9 %collective-permute-start.11 = (f32[128,256]{1,0:T(8,128)}, f32[128,256]{1,0:T(8,128)}, u32[]{:S(2)}, u32[]{:S(2)}) collective-permute-start(f32[128,256]{1,0:T(8,128)} %get-tuple-element.81), channel_id=1, source_target_pairs={{16,32},{32,16},{48,64},{64,48},{80,96},{96,80},{112,128},{128,112... | collective-permute-start | bytes 393224 | tf_op jit(solution)/shard_map/ppermute | solution.py:201
  86.7 1.7 %copy-done.1 = bf16[1,1152,1152]{2,1,0:T(8,128)(2,1)S(1)} copy-done((bf16[1,1152,1152]{2,1,0:T(8,128)(2,1)S(1)}, bf16[1,1152,1152]{2,1,0:T(8,128)(2,1)}, u32[]{:S(2)}) %copy-start.1) | copy-done | bytes 2654232
  92.0 3.3 %collective-permute-done.11.f2 = f32[128,256]{1,0:T(8,128)} collective-permute-done((f32[128,256]{1,0:T(8,128)}, f32[128,256]{1,0:T(8,128)}, u32[]{:S(2)}, u32[]{:S(2)}) %collective-permute-start.11) | collective-permute-done | bytes 131104 | tf_op jit(solution)/shard_map/ppermute | solution.py:201
  95.3 2.1 %shard_map.114 = (bf16[1152,256]{1,0:T(8,128)(2,1)S(1)}, f32[16,32,256]{2,1,0:T(8,128)S(1)}, f32[8,128]{1,0:T(8,128)S(1)}) custom-call(f32[1152,256]{1,0:T(8,128)S(1)} %shard_map.113.resid, f32[128,256]{1,0:T(8,128)} %collective-permute-done.9.f0, f32[128,256]{1,0:T(8,128)} %collective-permute-done.10.f1, f32[128,256]{1,0:T(8,128)} %collective-permute-done.11.f2, ...), custom_call_target="tpu_custom_call" | custom-call | flops 603979776 | bytes 4075520 | tf_op jit(solution)/shard_map/pallas_call | solution.py:179
  99.1 7.3 %all-to-all-start.2 = ((f32[16,32,256]{2,1,0:T(8,128)}), f32[16,32,256]{2,1,0:T(8,128)}, u32[]{:S(2)}, u32[]{:S(2)}) async-start(f32[16,32,256]{2,1,0:T(8,128)} %copy-done.28), calls=%async_computation.2 | async-start | bytes 1048576 | tf_op jit(solution)/shard_map/all_to_all | solution.py:278
  106.3 1.7 %copy-done.39 = bf16[1,1152,1152]{2,1,0:T(8,128)(2,1)S(1)} copy-done((bf16[1,1152,1152]{2,1,0:T(8,128)(2,1)S(1)}, bf16[1,1152,1152]{2,1,0:T(8,128)(2,1)}, u32[]{:S(2)}) %copy-start.39) | copy-done | bytes 2654232
  110.4 2.9 %shard_map.115 = (f32[1152,256]{1,0:T(8,128)S(1)}, f32[512,256]{1,0:T(8,128)S(1)}, f32[8,128]{1,0:T(8,128)S(1)}) custom-call(bf16[1152,1152]{1,0:T(8,128)(2,1)S(1)} %bitcast.31, bf16[1152,256]{1,0:T(8,128)(2,1)S(1)} %copy-done.44, bf16[512,1152]{1,0:T(8,128)(2,1)S(1)} %copy-done.47), custom_call_target="tpu_custom_call" | custom-call | flops 1283457024 | bytes 6131712 | tf_op jit(solution)/shard_map/pallas_call | solution.py:179
  117.9 3.0 %all-to-all-done.2.gathered = f32[16,32,256]{2,1,0:T(8,128)} async-done(((f32[16,32,256]{2,1,0:T(8,128)}), f32[16,32,256]{2,1,0:T(8,128)}, u32[]{:S(2)}, u32[]{:S(2)}) %all-to-all-start.2) | async-done | bytes 524320 | tf_op jit(solution)/shard_map/all_to_all | solution.py:278
  122.9 1.8 %shard_map.117 = (f32[256,256]{1,0:T(8,128)S(1)}, f32[256,256]{1,0:T(8,128)S(1)}) custom-call(s32[1]{0:T(128)} %bitcast.core, bf16[512,512]{1,0:T(8,128)(2,1)S(1)} %copy-done.10, bf16[512,512]{1,0:T(8,128)(2,1)S(1)} %copy-done.12, f32[16,32,256]{2,1,0:T(8,128)} %all-to-all-done.2.gathered, f32[8,128]{1,0:T(8,128)S(1)} %get-tuple-element.85.after, ...), custom_call_target="tpu_custom_call" | custom-call | flops 402653184 | bytes 2105348 | tf_op jit(solution)/shard_map/pallas_call | solution.py:179
  126.4 12.4 %all_to_all.21.parts = f32[8,32,256]{2,1,0:T(8,128)S(1)} all-to-all(f32[8,32,256]{2,1,0:T(8,128)S(1)} %bitcast.34), channel_id=1, replica_groups={{0,32,64,96,128,160,192,224},{16,48,80,112,144,176,208,240},{1,33,65,97..., dimensions={0} | all-to-all | bytes 524288 | tf_op jit(solution)/shard_map/all_to_all | solution.py:312
  140.1 2.1 %collective-permute-start.14 = (f32[128,256]{1,0:T(8,128)S(1)}, f32[128,256]{1,0:T(8,128)S(1)}, u32[]{:S(2)}, u32[]{:S(2)}) collective-permute-start(f32[128,256]{1,0:T(8,128)S(1)} %get-tuple-element.91), channel_id=1, source_target_pairs={{0,1},{1,0},{2,3},{3,2},{4,5},{5,4},{6,7},{7,6},{8,9},{9,8},{10,11... | collective-permute-start | bytes 393224 | tf_op jit(solution)/shard_map/ppermute | solution.py:201
  142.1 2.6 %collective-permute-start.15 = (f32[128,256]{1,0:T(8,128)S(1)}, f32[128,256]{1,0:T(8,128)S(1)}, u32[]{:S(2)}, u32[]{:S(2)}) collective-permute-start(f32[128,256]{1,0:T(8,128)S(1)} %get-tuple-element.92), channel_id=1, source_target_pairs={{1,2},{2,1},{3,4},{4,3},{5,6},{6,5},{7,8},{8,7},{9,10},{10,9},{11,... | collective-permute-start | bytes 393224 | tf_op jit(solution)/shard_map/ppermute | solution.py:201
  144.7 1.9 %collective-permute-start.16 = (f32[128,256]{1,0:T(8,128)S(1)}, f32[128,256]{1,0:T(8,128)S(1)}, u32[]{:S(2)}, u32[]{:S(2)}) collective-permute-start(f32[128,256]{1,0:T(8,128)S(1)} %get-tuple-element.93), channel_id=1, source_target_pairs={{16,32},{32,16},{48,64},{64,48},{80,96},{96,80},{112,128},{128,112... | collective-permute-start | bytes 393224 | tf_op jit(solution)/shard_map/ppermute | solution.py:201
  150.5 1.8 %shard_map.119 = (f32[1152,256]{1,0:T(8,128)S(1)}, f32[1152,256]{1,0:T(8,128)S(1)}) custom-call(s32[1]{0:T(128)S(6)} %copy.22.length, f32[1152,256]{1,0:T(8,128)S(1)} %copy-done.14, bf16[1152,32]{1,0:T(8,128)(2,1)S(1)} %bitcast.24, f32[32,256]{1,0:T(8,128)S(1)} %get-tuple-element.97.coarse_out, f32[1152,256]{1,0:T(8,128)S(1)} %copy-done.6, ...), custom_call_target="tpu_custom_call" | custom-call | flops 679477248 | bytes 8663556 | tf_op jit(solution)/shard_map/pallas_call | solution.py:179
  152.6 2.5 %collective-permute-done.16.r2 = f32[128,256]{1,0:T(8,128)S(1)} collective-permute-done((f32[128,256]{1,0:T(8,128)S(1)}, f32[128,256]{1,0:T(8,128)S(1)}, u32[]{:S(2)}, u32[]{:S(2)}) %collective-permute-start.16) | collective-permute-done | bytes 131104 | tf_op jit(solution)/shard_map/ppermute | solution.py:201
  155.1 2.0 %shard_map.120 = (f32[1152,256]{1,0:T(8,128)}, f32[1152,256]{1,0:T(8,128)}) custom-call(s32[1]{0:T(128)S(6)} %copy.22.length, f32[128,256]{1,0:T(8,128)S(1)} %collective-permute-done.14.r0, f32[128,256]{1,0:T(8,128)S(1)} %collective-permute-done.15.r1, f32[128,256]{1,0:T(8,128)S(1)} %collective-permute-done.16.r2, ...), custom_call_target="tpu_custom_call" | custom-call | flops 1207959552 | bytes 7606788 | tf_op jit(solution)/shard_map/pallas_call | solution.py:179
  (134 shorter events, 43.2 us)
Async XLA Ops:
  1.6 15.6 %copy-start.21 = (f32[512,512]{1,0:T(8,128)S(1)}, f32[512,512]{1,0:T(8,128)}, u32[]{:S(2)}) copy-start(f32[512,512]{1,0:T(8,128)} %coarse.1) | copy-start | bytes 3145732
  3.7 18.3 %copy-start.22 = (bf16[1,32,1152]{2,1,0:T(8,128)(2,1)S(1)}, bf16[1,32,1152]{2,1,0:T(8,128)(2,1)}, u32[]{:S(2)}) copy-start(bf16[1,32,1152]{2,1,0:T(8,128)(2,1)} %param.16) | copy-start | bytes 221188
  6.1 16.9 %copy-start.7 = (f32[1152,256]{1,0:T(8,128)}, f32[1152,256]{1,0:T(8,128)S(1)}, u32[]{:S(2)}) copy-start(f32[1152,256]{1,0:T(8,128)S(1)} %get-tuple-element.54.resid) | copy-start | bytes 3538948
  6.1 16.9 %copy-start.29 = (f32[128,256]{1,0:T(8,128)}, f32[128,256]{1,0:T(8,128)S(1)}, u32[]{:S(2)}) copy-start(f32[128,256]{1,0:T(8,128)S(1)} %get-tuple-element.55.p0) | copy-start | bytes 393220
  6.1 16.9 %copy-start.31 = (f32[128,256]{1,0:T(8,128)}, f32[128,256]{1,0:T(8,128)S(1)}, u32[]{:S(2)}) copy-start(f32[128,256]{1,0:T(8,128)S(1)} %get-tuple-element.56.p1) | copy-start | bytes 393220
  6.1 16.9 %copy-start.33 = (f32[128,256]{1,0:T(8,128)}, f32[128,256]{1,0:T(8,128)S(1)}, u32[]{:S(2)}) copy-start(f32[128,256]{1,0:T(8,128)S(1)} %get-tuple-element.57.p2) | copy-start | bytes 393220
  6.1 16.9 %copy-start.35 = (f32[128,256]{1,0:T(8,128)}, f32[128,256]{1,0:T(8,128)S(1)}, u32[]{:S(2)}) copy-start(f32[128,256]{1,0:T(8,128)S(1)} %get-tuple-element.58.p3) | copy-start | bytes 393220
  6.1 11.5 %collective-permute-start = (f32[128,256]{1,0:T(8,128)S(1)}, f32[128,256]{1,0:T(8,128)S(1)}, u32[]{:S(2)}, u32[]{:S(2)}) collective-permute-start(f32[128,256]{1,0:T(8,128)S(1)} %get-tuple-element.55.p0), channel_id=1, source_target_pairs={{0,1},{1,0},{2,3},{3,2},{4,5},{5,4},{6,7},{7,6},{8,9},{9,8},{10,11... | collective-permute-start | bytes 393224 | tf_op jit(solution)/shard_map/ppermute | solution.py:201
  6.2 13.1 %collective-permute-start.1 = (f32[128,256]{1,0:T(8,128)S(1)}, f32[128,256]{1,0:T(8,128)S(1)}, u32[]{:S(2)}, u32[]{:S(2)}) collective-permute-start(f32[128,256]{1,0:T(8,128)S(1)} %get-tuple-element.56.p1), channel_id=1, source_target_pairs={{1,2},{2,1},{3,4},{4,3},{5,6},{6,5},{7,8},{8,7},{9,10},{10,9},{11,... | collective-permute-start | bytes 393224 | tf_op jit(solution)/shard_map/ppermute | solution.py:201
  14.1 7.9 %collective-permute-start.2 = (f32[128,256]{1,0:T(8,128)S(1)}, f32[128,256]{1,0:T(8,128)S(1)}, u32[]{:S(2)}, u32[]{:S(2)}) collective-permute-start(f32[128,256]{1,0:T(8,128)S(1)} %get-tuple-element.57.p2), channel_id=1, source_target_pairs={{16,32},{32,16},{48,64},{64,48},{80,96},{96,80},{112,128},{128,112... | collective-permute-start | bytes 393224 | tf_op jit(solution)/shard_map/ppermute | solution.py:201
  16.0 5.9 %collective-permute-start.3 = (f32[128,256]{1,0:T(8,128)S(1)}, f32[128,256]{1,0:T(8,128)S(1)}, u32[]{:S(2)}, u32[]{:S(2)}) collective-permute-start(f32[128,256]{1,0:T(8,128)S(1)} %get-tuple-element.58.p3), channel_id=1, source_target_pairs={{0,16},{16,0},{32,48},{48,32},{64,80},{80,64},{96,112},{112,96},{1... | collective-permute-start | bytes 393224 | tf_op jit(solution)/shard_map/ppermute | solution.py:201
  17.6 31.9 %copy-start.9 = (bf16[512,512]{1,0:T(8,128)(2,1)}, bf16[512,512]{1,0:T(8,128)(2,1)S(1)}, u32[]{:S(2)}) copy-start(bf16[512,512]{1,0:T(8,128)(2,1)S(1)} %get-tuple-element.52.high) | copy-start | bytes 1572868
  17.6 31.9 %copy-start.11 = (bf16[512,512]{1,0:T(8,128)(2,1)}, bf16[512,512]{1,0:T(8,128)(2,1)S(1)}, u32[]{:S(2)}) copy-start(bf16[512,512]{1,0:T(8,128)(2,1)S(1)} %get-tuple-element.53.low) | copy-start | bytes 1572868
  24.6 24.8 %all-to-all-start = ((f32[16,32,256]{2,1,0:T(8,128)}), f32[16,32,256]{2,1,0:T(8,128)S(1)}, u32[]{:S(2)}, u32[]{:S(2)}) async-start(f32[16,32,256]{2,1,0:T(8,128)} %copy-done.27), calls=%async_computation | async-start | bytes 1048576 | tf_op jit(solution)/shard_map/all_to_all | solution.py:278
  49.4 13.0 %copy-start.26 = (f32[512,256]{1,0:T(8,128)S(1)}, f32[512,256]{1,0:T(8,128)}, u32[]{:S(2)}) copy-start(f32[512,256]{1,0:T(8,128)} %copy-done.25) | copy-start | bytes 1572868
  50.0 19.8 %copy-start.16 = (f32[1152,256]{1,0:T(8,128)S(1)}, f32[1152,256]{1,0:T(8,128)}, u32[]{:S(2)}) copy-start(f32[1152,256]{1,0:T(8,128)} %copy-done.15) | copy-start | bytes 3538948
  50.1 1.6 %collective-permute-start.4 = (f32[256,256]{1,0:T(8,128)S(1)}, f32[256,256]{1,0:T(8,128)S(1)}, u32[]{:S(2)}, u32[]{:S(2)}) collective-permute-start(f32[256,256]{1,0:T(8,128)S(1)} %get-tuple-element.68), channel_id=1, source_target_pairs={{0,16},{16,0},{32,48},{48,32},{64,80},{80,64},{96,112},{112,96},{1... | collective-permute-start | bytes 786440 | tf_op jit(solution)/shard_map/ppermute | solution.py:201
  62.8 7.5 %collective-permute-start.5 = (f32[128,256]{1,0:T(8,128)S(1)}, f32[128,256]{1,0:T(8,128)S(1)}, u32[]{:S(2)}, u32[]{:S(2)}) collective-permute-start(f32[128,256]{1,0:T(8,128)S(1)} %get-tuple-element.72.c0), channel_id=1, source_target_pairs={{0,1},{1,0},{2,3},{3,2},{4,5},{5,4},{6,7},{7,6},{8,9},{9,8},{10,11... | collective-permute-start | bytes 393224 | tf_op jit(solution)/shard_map/ppermute | solution.py:201
  64.4 10.5 %collective-permute-start.6 = (f32[128,256]{1,0:T(8,128)S(1)}, f32[128,256]{1,0:T(8,128)S(1)}, u32[]{:S(2)}, u32[]{:S(2)}) collective-permute-start(f32[128,256]{1,0:T(8,128)S(1)} %get-tuple-element.73.c1), channel_id=1, source_target_pairs={{1,2},{2,1},{3,4},{4,3},{5,6},{6,5},{7,8},{8,7},{9,10},{10,9},{11,... | collective-permute-start | bytes 393224 | tf_op jit(solution)/shard_map/ppermute | solution.py:201
  66.6 10.6 %collective-permute-start.7 = (f32[128,256]{1,0:T(8,128)S(1)}, f32[128,256]{1,0:T(8,128)S(1)}, u32[]{:S(2)}, u32[]{:S(2)}) collective-permute-start(f32[128,256]{1,0:T(8,128)S(1)} %get-tuple-element.74.c2), channel_id=1, source_target_pairs={{16,32},{32,16},{48,64},{64,48},{80,96},{96,80},{112,128},{128,112... | collective-permute-start | bytes 393224 | tf_op jit(solution)/shard_map/ppermute | solution.py:201
  68.6 8.7 %collective-permute-start.8 = (f32[128,256]{1,0:T(8,128)S(1)}, f32[128,256]{1,0:T(8,128)S(1)}, u32[]{:S(2)}, u32[]{:S(2)}) collective-permute-start(f32[128,256]{1,0:T(8,128)S(1)} %get-tuple-element.75.c3), channel_id=1, source_target_pairs={{0,16},{16,0},{32,48},{48,32},{64,80},{80,64},{96,112},{112,96},{1... | collective-permute-start | bytes 393224 | tf_op jit(solution)/shard_map/ppermute | solution.py:201
  80.7 11.3 %collective-permute-start.10 = (f32[128,256]{1,0:T(8,128)}, f32[128,256]{1,0:T(8,128)}, u32[]{:S(2)}, u32[]{:S(2)}) collective-permute-start(f32[128,256]{1,0:T(8,128)} %get-tuple-element.80), channel_id=1, source_target_pairs={{1,2},{2,1},{3,4},{4,3},{5,6},{6,5},{7,8},{8,7},{9,10},{10,9},{11,... | collective-permute-start | bytes 393224 | tf_op jit(solution)/shard_map/ppermute | solution.py:201
  84.1 11.2 %collective-permute-start.11 = (f32[128,256]{1,0:T(8,128)}, f32[128,256]{1,0:T(8,128)}, u32[]{:S(2)}, u32[]{:S(2)}) collective-permute-start(f32[128,256]{1,0:T(8,128)} %get-tuple-element.81), channel_id=1, source_target_pairs={{16,32},{32,16},{48,64},{64,48},{80,96},{96,80},{112,128},{128,112... | collective-permute-start | bytes 393224 | tf_op jit(solution)/shard_map/ppermute | solution.py:201
  86.0 9.3 %collective-permute-start.12 = (f32[128,256]{1,0:T(8,128)}, f32[128,256]{1,0:T(8,128)}, u32[]{:S(2)}, u32[]{:S(2)}) collective-permute-start(f32[128,256]{1,0:T(8,128)} %get-tuple-element.82), channel_id=1, source_target_pairs={{0,16},{16,0},{32,48},{48,32},{64,80},{80,64},{96,112},{112,96},{1... | collective-permute-start | bytes 393224 | tf_op jit(solution)/shard_map/ppermute | solution.py:201
  86.5 8.8 %collective-permute-start.9 = (f32[128,256]{1,0:T(8,128)}, f32[128,256]{1,0:T(8,128)}, u32[]{:S(2)}, u32[]{:S(2)}) collective-permute-start(f32[128,256]{1,0:T(8,128)} %get-tuple-element.79), channel_id=1, source_target_pairs={{0,1},{1,0},{2,3},{3,2},{4,5},{5,4},{6,7},{7,6},{8,9},{9,8},{10,11... | collective-permute-start | bytes 393224 | tf_op jit(solution)/shard_map/ppermute | solution.py:201
  99.1 21.8 %all-to-all-start.2 = ((f32[16,32,256]{2,1,0:T(8,128)}), f32[16,32,256]{2,1,0:T(8,128)}, u32[]{:S(2)}, u32[]{:S(2)}) async-start(f32[16,32,256]{2,1,0:T(8,128)} %copy-done.28), calls=%async_computation.2 | async-start | bytes 1048576 | tf_op jit(solution)/shard_map/all_to_all | solution.py:278
  122.9 25.0 %copy-start.3 = (bf16[1,1152,1152]{2,1,0:T(8,128)(2,1)S(1)}, bf16[1,1152,1152]{2,1,0:T(8,128)(2,1)}, u32[]{:S(2)}) copy-start(bf16[1,1152,1152]{2,1,0:T(8,128)(2,1)} %param.14) | copy-start | bytes 7962628
  124.7 1.6 %collective-permute-start.13 = (f32[256,256]{1,0:T(8,128)S(1)}, f32[256,256]{1,0:T(8,128)S(1)}, u32[]{:S(2)}, u32[]{:S(2)}) collective-permute-start(f32[256,256]{1,0:T(8,128)S(1)} %get-tuple-element.89), channel_id=1, source_target_pairs={{0,16},{16,0},{32,48},{48,32},{64,80},{80,64},{96,112},{112,96},{1... | collective-permute-start | bytes 786440 | tf_op jit(solution)/shard_map/ppermute | solution.py:201
  140.1 12.2 %collective-permute-start.14 = (f32[128,256]{1,0:T(8,128)S(1)}, f32[128,256]{1,0:T(8,128)S(1)}, u32[]{:S(2)}, u32[]{:S(2)}) collective-permute-start(f32[128,256]{1,0:T(8,128)S(1)} %get-tuple-element.91), channel_id=1, source_target_pairs={{0,1},{1,0},{2,3},{3,2},{4,5},{5,4},{6,7},{7,6},{8,9},{9,8},{10,11... | collective-permute-start | bytes 393224 | tf_op jit(solution)/shard_map/ppermute | solution.py:201
  142.1 10.5 %collective-permute-start.15 = (f32[128,256]{1,0:T(8,128)S(1)}, f32[128,256]{1,0:T(8,128)S(1)}, u32[]{:S(2)}, u32[]{:S(2)}) collective-permute-start(f32[128,256]{1,0:T(8,128)S(1)} %get-tuple-element.92), channel_id=1, source_target_pairs={{1,2},{2,1},{3,4},{4,3},{5,6},{6,5},{7,8},{8,7},{9,10},{10,9},{11,... | collective-permute-start | bytes 393224 | tf_op jit(solution)/shard_map/ppermute | solution.py:201
  144.7 10.3 %collective-permute-start.16 = (f32[128,256]{1,0:T(8,128)S(1)}, f32[128,256]{1,0:T(8,128)S(1)}, u32[]{:S(2)}, u32[]{:S(2)}) collective-permute-start(f32[128,256]{1,0:T(8,128)S(1)} %get-tuple-element.93), channel_id=1, source_target_pairs={{16,32},{32,16},{48,64},{64,48},{80,96},{96,80},{112,128},{128,112... | collective-permute-start | bytes 393224 | tf_op jit(solution)/shard_map/ppermute | solution.py:201
  146.7 8.4 %collective-permute-start.17 = (f32[128,256]{1,0:T(8,128)S(1)}, f32[128,256]{1,0:T(8,128)S(1)}, u32[]{:S(2)}, u32[]{:S(2)}) collective-permute-start(f32[128,256]{1,0:T(8,128)S(1)} %get-tuple-element.94), channel_id=1, source_target_pairs={{0,16},{16,0},{32,48},{48,32},{64,80},{80,64},{96,112},{112,96},{1... | collective-permute-start | bytes 393224 | tf_op jit(solution)/shard_map/ppermute | solution.py:201
  (36 other events, 86.3 us)

commit v3 on v2

--- a/solution.py
+++ b/solution.py
@@ -21,9 +21,18 @@
     return high, (v - high.astype(F32)).astype(BF16)
 
 
-def pick(onehot, v):
+def dot_t(a, b):
+    return lax.dot_general(a, b, (((0,), (0,)), ((), ())), preferred_element_type=F32)
+
+
+def place(put, v):
     high, low = halves(v)
-    return dot(onehot, high) + dot(onehot, low)
+    return dot(put, high) + dot(put, low)
+
+
+def take(put, v):
+    high, low = halves(v)
+    return dot_t(put, high) + dot_t(put, low)
 
 
 def live_of(length_ref, n):
@@ -56,44 +65,35 @@
     ]
 
 
-def begin_kernel(length, rows, loads, resid, take, f0, f1, f2, f3, sems):
-    n = resid.shape[0]
-    copies = chunk_copies(loads, resid, sems)
-    for copy in copies:
-        copy.start()
-    take[...] = onehot(rows[...], take.shape, 1)
-    for copy in copies:
-        copy.wait()
-    resid[...] = resid[...] * live_of(length, n)
-    store_faces(pick(take[...], resid[...]), (f0, f1, f2, f3))
-
-
-def tables_kernel(rows, coarse, put, coarse_high, coarse_low):
+def put_kernel(rows, put):
     put[...] = onehot(rows[...], put.shape, 0)
-    high, low = halves(coarse[...])
-    coarse_high[...] = high
-    coarse_low[...] = low
+
+
+def begin_kernel(length, loads, put, resid, f0, f1, f2, f3):
+    resid[...] = loads[...] * live_of(length, resid.shape[0])
+    store_faces(take(put[...], resid[...]), (f0, f1, f2, f3))
 
 
 def coarse_in_kernel(resid, f0, f1, f2, f3, put, basis, assembled, coarse_in, token):
     token[...] = jnp.zeros_like(token)
     received = load_faces((f0, f1, f2, f3))
-    assembled[...] = (resid[...] + pick(put[...], received)).astype(BF16)
+    assembled[...] = (resid[...] + place(put[...], received)).astype(BF16)
     block = dot(basis[...], assembled[...])
     for j in range(coarse_in.shape[0]):
         coarse_in[j] = block
 
 
-def local_kernel(inverse, assembled, take, local, local_faces, token):
+def local_kernel(inverse, assembled, put, local, local_faces, token):
     local[...] = dot(inverse[...], assembled[...])
-    local_faces[...] = pick(take[...], local[...])
+    local_faces[...] = take(put[...], local[...])
     token[...] = jnp.zeros_like(token)
 
 
-def coarse_kernel(core, high, low, gathered, after, after_too, keep, send):
+def coarse_kernel(core, coarse, gathered, after, after_too, keep, send):
     groups, modes, loads = gathered.shape
     g_high, g_low = halves(gathered[...].reshape(groups * modes, loads))
-    out = dot(high[...], g_high) + dot(high[...], g_low) + dot(low[...], g_high)
+    high, low = halves(coarse[...])
+    out = dot(high, g_high) + dot(high, g_low) + dot(low, g_high)
     pairs = out.reshape(-1, 2, modes, loads)
     even = pairs[:, 0].reshape(keep.shape)
     odd = pairs[:, 1].reshape(keep.shape)
@@ -102,16 +102,12 @@
     send[...] = jnp.where(first, odd, even)
 
 
-def rows_kernel(after, take, offdiag, basis_t, diag_row, offdiag_rows, basis_rows, diag_rows, token):
+def rows_kernel(after, put, offdiag, basis_t, diag, offdiag_rows, basis_rows, diag_rows, token):
     token[...] = after[...]
-    basis_rows[...] = dot(take[...], basis_t[...]).astype(BF16)
-    diag_rows[...] = jnp.sum(take[...].astype(F32) * diag_row[...], axis=1, keepdims=True)
-    offdiag_rows[...] = dot(take[...], offdiag[...]).astype(BF16)
-
-
-def columns_kernel(after, offdiag, put, offdiag_columns, token):
-    token[...] = after[...]
-    offdiag_columns[...] = dot(offdiag[...], put[...]).astype(BF16)
+    basis_rows[...] = dot_t(put[...], basis_t[...]).astype(BF16)
+    wide = jnp.broadcast_to(diag[...], (diag.shape[0], 128))
+    diag_rows[...] = take(put[...], wide)
+    offdiag_rows[...] = dot_t(put[...], offdiag[...]).astype(BF16)
 
 
 def sent_kernel(parts, local_faces, basis_rows, coarse_out, f0, f1, f2, f3):
@@ -135,15 +131,19 @@
 def increment_kernel(correction, r0, r1, r2, r3, put, offdiag_rows, diag_rows, c0, c1, c2, c3, p0, p1, p2, p3,
                      increment, g0, g1, g2, g3):
     received = load_faces((r0, r1, r2, r3))
-    increment[...] = correction[...] + pick(put[...], received)
+    increment[...] = correction[...] + place(put[...], received)
     there = load_faces((c0, c1, c2, c3)) + received
-    applied = dot(offdiag_rows[...], increment[...].astype(BF16)) + diag_rows[...] * there
+    applied = dot(offdiag_rows[...], increment[...].astype(BF16)) + diag_rows[:, :1] * there
     store_faces(load_faces((p0, p1, p2, p3)) - applied, (g0, g1, g2, g3))
 
 
-def residual_kernel(length, increment, diag, resid, offdiag, resid_out):
+def residual_kernel(length, increment, diag, resid, offdiag, put, resid_out, solution, offdiag_columns, sem):
+    leave = pltpu.make_async_copy(increment, solution, sem)
+    leave.start()
     applied = dot(offdiag[...], increment[...].astype(BF16)) + diag[...] * increment[...]
     resid_out[...] = resid[...] - live_of(length, resid.shape[0]) * applied
+    offdiag_columns[...] = dot(offdiag[...], put[...]).astype(BF16)
+    leave.wait()
 
 
 def own_kernel(length, local, basis_t, coarse_out, before, diag, resid, offdiag,
@@ -251,19 +251,9 @@
     order = coarse_inverse.shape
     sems = pltpu.SemaphoreType.DMA((CHUNKS,))
     mark = like(8, 128)
-    resid, take, *sent = call(
-        begin_kernel,
-        [block, like(nrows, n, dtype=BF16)] + [face] * 4,
-        (iface_len, rows[:, None], loads),
-        "svh",
-        scratch=[sems],
-        flops=gather_flops,
-    )
-    put, coarse_high, coarse_low = call(
-        tables_kernel,
-        [like(n, nrows, dtype=BF16), like(*order, dtype=BF16), like(*order, dtype=BF16)],
-        (rows[None, :], coarse_inverse),
-        "vv",
+    (put,) = call(put_kernel, [like(n, nrows, dtype=BF16)], (rows[None, :],), "v")
+    resid, *sent = call(
+        begin_kernel, [block] + [face] * 4, (iface_len, loads, put), "svv", flops=gather_flops
     )
     solution = None
     for sweep in range(ITERS):
@@ -279,31 +269,23 @@
         local, local_faces, ahead = call(
             local_kernel,
             [block, like(nrows, nloads), mark],
-            (inverse, assembled, take),
+            (inverse, assembled, put),
             "vvv",
             flops=square_flops + gather_flops,
         )
         if sweep == 0:
             offdiag_rows, basis_rows, diag_rows, ahead_too = call(
                 rows_kernel,
-                [like(nrows, n, dtype=BF16), like(nrows, modes, dtype=BF16), like(nrows, 1), mark],
-                (after, take, offdiag, basis_t, schur_diag),
+                [like(nrows, n, dtype=BF16), like(nrows, modes, dtype=BF16), like(nrows, 128), mark],
+                (after, put, offdiag, basis_t, diag),
                 "vvvvv",
-                flops=2 * nrows * n * n,
-            )
-        else:
-            offdiag_columns, ahead_too = call(
-                columns_kernel,
-                [like(n, nrows, dtype=BF16), mark],
-                (after, offdiag, put),
-                "vvv",
                 flops=2 * nrows * n * n,
             )
         keep, send = call(
             coarse_kernel,
             [like(order[0] // 2, nloads)] * 2,
-            (core, coarse_high, coarse_low, gathered, ahead, ahead_too),
-            "svvvvv",
+            (core, coarse_inverse, gathered, ahead, ahead_too),
+            "svvvv",
             flops=6 * order[0] * order[1] * nloads,
         )
         other = swap(send, "sub", 0)
@@ -328,14 +310,16 @@
                 "v" * 16,
                 flops=2 * gather_flops,
             )
-            (resid,) = call(
+            assert solution is None
+            resid, solution, offdiag_columns = call(
                 residual_kernel,
-                [block],
-                (iface_len, increment, diag, resid, offdiag),
-                "svvvv",
+                [block, block, like(n, nrows, dtype=BF16)],
+                (iface_len, increment, diag, resid, offdiag, put),
+                "svvvvv",
+                "vhv",
+                [pltpu.SemaphoreType.DMA],
                 flops=square_flops,
             )
-            solution = increment if solution is None else solution + increment
         else:
             own, own_resid = call(
                 own_kernel,

time: 158 us -> 150 us (0.949)
  local copies, waits for them, and re-layouts: 31.1 us -> 18.2 us
  waiting for transfers between devices: 27.8 us -> 31.9 us
    unnamed x97 -> x75, local copies, waits for them, and re-layouts: 30.6 us -> 17.9 us
    all_to_all x2, waiting for transfers between devices: 7.38 us -> 12.2 us  [body(): gathered = lax.all_to_all(coarse_in, 'grid', 0, 0)]
    ppermute x18, starting transfers between devices: 31.8 us -> 33.5 us  [swap(): lax.ppermute(array, axis, [(i, j) for i, j in pairs if 0 <= j < size])]
    pallas_call x17 -> x16, Pallas kernels: 25.2 us -> 25.9 us  [call(): pl.pallas_call(kernel, out_shape=outs, in_specs=[pl.BlockSpec(memory_spac...]
  transfers between devices with their start and end apart: 20 -> 20, of which waited for: 11 -> 12; matrix products, arithmetic and copies ran while one was open for 0% -> 0% of each run, Pallas kernels for 8% -> 9%
where the time goes in v3:
time: 150 us
  starting transfers between devices  48.3 us (32%)
  waiting for transfers between devices  31.9 us (21%)
  Pallas kernels  25.9 us (17%)
  blocking collectives  22.4 us (15%)
  local copies, waits for them, and re-layouts  18.2 us (12%)
  between operations  1.97 us (1%)
    ppermute x18, starting transfers between devices, swap(): lax.ppermute(array, axis, [(i, j) for i, j in pairs if 0 <= j < size])  33.5 us
    pallas_call x16, Pallas kernels, call(): pl.pallas_call(kernel, out_shape=outs, in_specs=[pl.BlockSpec(memory_spac...  25.9 us
    all_to_all x2, blocking collectives, body(): parts = lax.all_to_all(parts, 'sub', 0, 0, axis_index_groups=groups)  22.4 us
    ppermute x18, waiting for transfers between devices, swap(): lax.ppermute(array, axis, [(i, j) for i, j in pairs if 0 <= j < size])  19.7 us
    unnamed x75, local copies, waits for them, and re-layouts  17.9 us
    all_to_all x2, starting transfers between devices, body(): gathered = lax.all_to_all(coarse_in, 'grid', 0, 0)  14.8 us
    all_to_all x2, waiting for transfers between devices, body(): gathered = lax.all_to_all(coarse_in, 'grid', 0, 0)  12.2 us
  transfers between devices with their start and end apart: 20, of which 12 were waited for; matrix products, arithmetic and copies ran while one was open for 0% of the time, Pallas kernels for 9%

profile of v3, /device:TPU:72, one launch (start us, length us, event | category | flops | bytes accessed | tf_op | source)
XLA Modules:
  0.0 149.5 jit_solution(11691250317276168964)
XLA Ops:
  3.5 7.8 %collective-permute-start.1 = (f32[128,256]{1,0:T(8,128)S(1)}, f32[128,256]{1,0:T(8,128)S(1)}, u32[]{:S(2)}, u32[]{:S(2)}) collective-permute-start(f32[128,256]{1,0:T(8,128)S(1)} %get-tuple-element.50.p1), channel_id=1, source_target_pairs={{1,2},{2,1},{3,4},{4,3},{5,6},{6,5},{7,8},{8,7},{9,10},{10,9},{11,... | collective-permute-start | bytes 393224 | tf_op jit(solution)/shard_map/ppermute | solution.py:201
  11.3 1.9 %collective-permute-start.2 = (f32[128,256]{1,0:T(8,128)S(1)}, f32[128,256]{1,0:T(8,128)S(1)}, u32[]{:S(2)}, u32[]{:S(2)}) collective-permute-start(f32[128,256]{1,0:T(8,128)S(1)} %get-tuple-element.51.p2), channel_id=1, source_target_pairs={{16,32},{32,16},{48,64},{64,48},{80,96},{96,80},{112,128},{128,112... | collective-permute-start | bytes 393224 | tf_op jit(solution)/shard_map/ppermute | solution.py:201
  16.6 2.6 %collective-permute-done.2.f2 = f32[128,256]{1,0:T(8,128)S(1)} collective-permute-done((f32[128,256]{1,0:T(8,128)S(1)}, f32[128,256]{1,0:T(8,128)S(1)}, u32[]{:S(2)}, u32[]{:S(2)}) %collective-permute-start.2) | collective-permute-done | bytes 131104 | tf_op jit(solution)/shard_map/ppermute | solution.py:201
  19.2 1.8 %shard_map.106 = (bf16[1152,256]{1,0:T(8,128)(2,1)S(1)}, f32[16,32,256]{2,1,0:T(8,128)}, f32[8,128]{1,0:T(8,128)S(1)}) custom-call(f32[1152,256]{1,0:T(8,128)S(1)} %get-tuple-element.48.resid, f32[128,256]{1,0:T(8,128)S(1)} %collective-permute-done.f0, f32[128,256]{1,0:T(8,128)S(1)} %collective-permute-done.1.f1, f32[128,256]{1,0:T(8,128)S(1)} %collective-permute-done.2.f2, ...), custom_call_target="tpu_custom_call" | custom-call | flops 603979776 | bytes 4075520 | tf_op jit(solution)/shard_map/pallas_call | solution.py:179
  21.0 8.2 %all-to-all-start = ((f32[16,32,256]{2,1,0:T(8,128)}), f32[16,32,256]{2,1,0:T(8,128)}, u32[]{:S(2)}, u32[]{:S(2)}) async-start(f32[16,32,256]{2,1,0:T(8,128)} %get-tuple-element.55), calls=%async_computation | async-start | bytes 1048576 | tf_op jit(solution)/shard_map/all_to_all | solution.py:268
  29.8 1.7 %copy-done.32 = bf16[1,1152,1152]{2,1,0:T(8,128)(2,1)S(1)} copy-done((bf16[1,1152,1152]{2,1,0:T(8,128)(2,1)S(1)}, bf16[1,1152,1152]{2,1,0:T(8,128)(2,1)}, u32[]{:S(2)}) %copy-start.32) | copy-done | bytes 2654232
  31.5 2.9 %shard_map.107 = (f32[1152,256]{1,0:T(8,128)S(1)}, f32[512,256]{1,0:T(8,128)S(1)}, f32[8,128]{1,0:T(8,128)S(1)}) custom-call(bf16[1152,1152]{1,0:T(8,128)(2,1)S(1)} %bitcast.27, bf16[1152,256]{1,0:T(8,128)(2,1)S(1)} %get-tuple-element.53.assembled, bf16[1152,512]{1,0:T(8,128)(2,1)S(1)} %shard_map.104.put), custom_call_target="tpu_custom_call" | custom-call | flops 1283457024 | bytes 6131712 | tf_op jit(solution)/shard_map/pallas_call | solution.py:179
  36.2 3.0 %shard_map.108 = (bf16[512,1152]{1,0:T(8,128)(2,1)S(1)}, bf16[512,32]{1,0:T(8,128)(2,1)S(1)}, f32[512,128]{1,0:T(8,128)S(1)}, f32[8,128]{1,0:T(8,128)S(1)}) custom-call(f32[8,128]{1,0:T(8,128)S(1)} %get-tuple-element.57.after, bf16[1152,512]{1,0:T(8,128)(2,1)S(1)} %shard_map.104.put, bf16[1152,1152]{1,0:T(8,128)(2,1)S(1)} %bitcast.17, ...), custom_call_target="tpu_custom_call" | custom-call | flops 1358954496 | bytes 5394944 | tf_op jit(solution)/shard_map/pallas_call | solution.py:179
  41.0 5.1 %all-to-all-done.gathered = f32[16,32,256]{2,1,0:T(8,128)} async-done(((f32[16,32,256]{2,1,0:T(8,128)}), f32[16,32,256]{2,1,0:T(8,128)}, u32[]{:S(2)}, u32[]{:S(2)}) %all-to-all-start) | async-done | bytes 524320 | tf_op jit(solution)/shard_map/all_to_all | solution.py:268
  46.1 1.7 %shard_map.109 = (f32[256,256]{1,0:T(8,128)S(1)}, f32[256,256]{1,0:T(8,128)S(1)}) custom-call(s32[1]{0:T(128)} %bitcast.core, f32[512,512]{1,0:T(8,128)S(1)} %copy-done.5, f32[16,32,256]{2,1,0:T(8,128)} %all-to-all-done.gathered, f32[8,128]{1,0:T(8,128)S(1)} %get-tuple-element.56.after, f32[8,128]{1,0:T(8,128)S(1)} %get-tuple-element.58.after_too), custom_call_target="tpu_custom_call" | custom-call | flops 402653184 | bytes 2105348 | tf_op jit(solution)/shard_map/pallas_call | solution.py:179
  49.5 10.8 %all_to_all.20.parts = f32[8,32,256]{2,1,0:T(8,128)S(1)} all-to-all(f32[8,32,256]{2,1,0:T(8,128)S(1)} %bitcast.29), channel_id=1, replica_groups={{0,32,64,96,128,160,192,224},{16,48,80,112,144,176,208,240},{1,33,65,97..., dimensions={0} | all-to-all | bytes 524288 | tf_op jit(solution)/shard_map/all_to_all | solution.py:294
  62.2 2.2 %collective-permute-start.6 = (f32[128,256]{1,0:T(8,128)S(1)}, f32[128,256]{1,0:T(8,128)S(1)}, u32[]{:S(2)}, u32[]{:S(2)}) collective-permute-start(f32[128,256]{1,0:T(8,128)S(1)} %get-tuple-element.65.c1), channel_id=1, source_target_pairs={{1,2},{2,1},{3,4},{4,3},{5,6},{6,5},{7,8},{8,7},{9,10},{10,9},{11,... | collective-permute-start | bytes 393224 | tf_op jit(solution)/shard_map/ppermute | solution.py:201
  64.4 1.9 %collective-permute-start.7 = (f32[128,256]{1,0:T(8,128)S(1)}, f32[128,256]{1,0:T(8,128)S(1)}, u32[]{:S(2)}, u32[]{:S(2)}) collective-permute-start(f32[128,256]{1,0:T(8,128)S(1)} %get-tuple-element.66.c2), channel_id=1, source_target_pairs={{16,32},{32,16},{48,64},{64,48},{80,96},{96,80},{112,128},{128,112... | collective-permute-start | bytes 393224 | tf_op jit(solution)/shard_map/ppermute | solution.py:201
  68.2 4.4 %collective-permute-done.6.r1 = f32[128,256]{1,0:T(8,128)S(1)} collective-permute-done((f32[128,256]{1,0:T(8,128)S(1)}, f32[128,256]{1,0:T(8,128)S(1)}, u32[]{:S(2)}, u32[]{:S(2)}) %collective-permute-start.6) | collective-permute-done | bytes 131104 | tf_op jit(solution)/shard_map/ppermute | solution.py:201
  72.7 2.3 %collective-permute-done.7.r2 = f32[128,256]{1,0:T(8,128)S(1)} collective-permute-done((f32[128,256]{1,0:T(8,128)S(1)}, f32[128,256]{1,0:T(8,128)S(1)}, u32[]{:S(2)}, u32[]{:S(2)}) %collective-permute-start.7) | collective-permute-done | bytes 131104 | tf_op jit(solution)/shard_map/ppermute | solution.py:201
  75.0 1.7 %shard_map.112 = (f32[1152,256]{1,0:T(8,128)S(1)}, f32[128,256]{1,0:T(8,128)S(1)}, f32[128,256]{1,0:T(8,128)S(1)}, f32[128,256]{1,0:T(8,128)S(1)}, f32[128,256]{1,0:T(8,128)S(1)}) custom-call(f32[1152,256]{1,0:T(8,128)S(1)} %shard_map.111.correction, f32[128,256]{1,0:T(8,128)S(1)} %collective-permute-done.5.r0, f32[128,256]{1,0:T(8,128)S(1)} %collective-permute-done.6.r1, ...), custom_call_target="tpu_custom_call" | custom-call | flops 1207959552 | bytes 7077888 | tf_op jit(solution)/shard_map/pallas_call | solution.py:179
  76.8 4.2 %collective-permute-start.10 = (f32[128,256]{1,0:T(8,128)S(1)}, f32[128,256]{1,0:T(8,128)S(1)}, u32[]{:S(2)}, u32[]{:S(2)}) collective-permute-start(f32[128,256]{1,0:T(8,128)S(1)} %get-tuple-element.73), channel_id=1, source_target_pairs={{1,2},{2,1},{3,4},{4,3},{5,6},{6,5},{7,8},{8,7},{9,10},{10,9},{11,... | collective-permute-start | bytes 393224 | tf_op jit(solution)/shard_map/ppermute | solution.py:201
  81.1 1.9 %collective-permute-start.11 = (f32[128,256]{1,0:T(8,128)S(1)}, f32[128,256]{1,0:T(8,128)S(1)}, u32[]{:S(2)}, u32[]{:S(2)}) collective-permute-start(f32[128,256]{1,0:T(8,128)S(1)} %get-tuple-element.74), channel_id=1, source_target_pairs={{16,32},{32,16},{48,64},{64,48},{80,96},{96,80},{112,128},{128,112... | collective-permute-start | bytes 393224 | tf_op jit(solution)/shard_map/ppermute | solution.py:201
  83.3 2.7 %shard_map.113 = (f32[1152,256]{1,0:T(8,128)S(1)}, f32[1152,256]{1,0:T(8,128)S(1)}, bf16[1152,512]{1,0:T(8,128)(2,1)S(1)}) custom-call(s32[1]{0:T(128)S(6)} %copy.22.length, f32[1152,256]{1,0:T(8,128)S(1)} %get-tuple-element.70.increment, f32[1152,1]{1,0:T(8,128)S(1)} %copy.16.diag, f32[1152,256]{1,0:T(8,128)S(1)} %copy-done.4, ...), custom_call_target="tpu_custom_call" | custom-call | flops 679477248 | bytes 9736708 | tf_op jit(solution)/shard_map/pallas_call | solution.py:179
  86.7 3.0 %collective-permute-done.11.f2 = f32[128,256]{1,0:T(8,128)S(1)} collective-permute-done((f32[128,256]{1,0:T(8,128)S(1)}, f32[128,256]{1,0:T(8,128)S(1)}, u32[]{:S(2)}, u32[]{:S(2)}) %collective-permute-start.11) | collective-permute-done | bytes 131104 | tf_op jit(solution)/shard_map/ppermute | solution.py:201
  92.8 6.6 %all-to-all-start.2 = ((f32[16,32,256]{2,1,0:T(8,128)}), f32[16,32,256]{2,1,0:T(8,128)}, u32[]{:S(2)}, u32[]{:S(2)}) async-start(f32[16,32,256]{2,1,0:T(8,128)} %copy-done.23), calls=%async_computation.2 | async-start | bytes 1048576 | tf_op jit(solution)/shard_map/all_to_all | solution.py:268
  99.4 1.7 %copy-done.33 = bf16[1,1152,1152]{2,1,0:T(8,128)(2,1)S(1)} copy-done((bf16[1,1152,1152]{2,1,0:T(8,128)(2,1)S(1)}, bf16[1,1152,1152]{2,1,0:T(8,128)(2,1)}, u32[]{:S(2)}) %copy-start.33) | copy-done | bytes 2654232
  102.2 2.9 %shard_map.115 = (f32[1152,256]{1,0:T(8,128)S(1)}, f32[512,256]{1,0:T(8,128)S(1)}, f32[8,128]{1,0:T(8,128)S(1)}) custom-call(bf16[1152,1152]{1,0:T(8,128)(2,1)S(1)} %bitcast.28, bf16[1152,256]{1,0:T(8,128)(2,1)S(1)} %copy-done.35, bf16[1152,512]{1,0:T(8,128)(2,1)S(1)} %shard_map.104.put), custom_call_target="tpu_custom_call" | custom-call | flops 1283457024 | bytes 6131712 | tf_op jit(solution)/shard_map/pallas_call | solution.py:179
  106.9 7.1 %all-to-all-done.2.gathered = f32[16,32,256]{2,1,0:T(8,128)} async-done(((f32[16,32,256]{2,1,0:T(8,128)}), f32[16,32,256]{2,1,0:T(8,128)}, u32[]{:S(2)}, u32[]{:S(2)}) %all-to-all-start.2) | async-done | bytes 524320 | tf_op jit(solution)/shard_map/all_to_all | solution.py:268
  115.2 1.8 %shard_map.116 = (f32[256,256]{1,0:T(8,128)S(1)}, f32[256,256]{1,0:T(8,128)S(1)}) custom-call(s32[1]{0:T(128)} %bitcast.core, f32[512,512]{1,0:T(8,128)S(1)} %copy-done.6, f32[16,32,256]{2,1,0:T(8,128)} %all-to-all-done.2.gathered, f32[8,128]{1,0:T(8,128)S(1)} %get-tuple-element.78.after, f32[8,128]{1,0:T(8,128)S(1)} %get-tuple-element.58.after_too), custom_call_target="tpu_custom_call" | custom-call | flops 402653184 | bytes 2105348 | tf_op jit(solution)/shard_map/pallas_call | solution.py:179
  118.7 11.6 %all_to_all.21.parts = f32[8,32,256]{2,1,0:T(8,128)S(1)} all-to-all(f32[8,32,256]{2,1,0:T(8,128)S(1)} %bitcast.30), channel_id=1, replica_groups={{0,32,64,96,128,160,192,224},{16,48,80,112,144,176,208,240},{1,33,65,97..., dimensions={0} | all-to-all | bytes 524288 | tf_op jit(solution)/shard_map/all_to_all | solution.py:294
  131.6 2.8 %collective-permute-start.14 = (f32[128,256]{1,0:T(8,128)S(1)}, f32[128,256]{1,0:T(8,128)S(1)}, u32[]{:S(2)}, u32[]{:S(2)}) collective-permute-start(f32[128,256]{1,0:T(8,128)S(1)} %get-tuple-element.82), channel_id=1, source_target_pairs={{0,1},{1,0},{2,3},{3,2},{4,5},{5,4},{6,7},{7,6},{8,9},{9,8},{10,11... | collective-permute-start | bytes 393224 | tf_op jit(solution)/shard_map/ppermute | solution.py:201
  134.4 2.7 %collective-permute-start.15 = (f32[128,256]{1,0:T(8,128)S(1)}, f32[128,256]{1,0:T(8,128)S(1)}, u32[]{:S(2)}, u32[]{:S(2)}) collective-permute-start(f32[128,256]{1,0:T(8,128)S(1)} %get-tuple-element.83), channel_id=1, source_target_pairs={{1,2},{2,1},{3,4},{4,3},{5,6},{6,5},{7,8},{8,7},{9,10},{10,9},{11,... | collective-permute-start | bytes 393224 | tf_op jit(solution)/shard_map/ppermute | solution.py:201
  137.1 1.9 %collective-permute-start.16 = (f32[128,256]{1,0:T(8,128)S(1)}, f32[128,256]{1,0:T(8,128)S(1)}, u32[]{:S(2)}, u32[]{:S(2)}) collective-permute-start(f32[128,256]{1,0:T(8,128)S(1)} %get-tuple-element.84), channel_id=1, source_target_pairs={{16,32},{32,16},{48,64},{64,48},{80,96},{96,80},{112,128},{128,112... | collective-permute-start | bytes 393224 | tf_op jit(solution)/shard_map/ppermute | solution.py:201
  142.8 1.8 %shard_map.118 = (f32[1152,256]{1,0:T(8,128)S(1)}, f32[1152,256]{1,0:T(8,128)S(1)}) custom-call(s32[1]{0:T(128)S(6)} %copy.22.length, f32[1152,256]{1,0:T(8,128)S(1)} %copy-done.10, bf16[1152,32]{1,0:T(8,128)(2,1)S(1)} %bitcast.22, f32[32,256]{1,0:T(8,128)S(1)} %get-tuple-element.88.coarse_out, f32[1152,256]{1,0:T(8,128)S(1)} %copy-done.8, ...), custom_call_target="tpu_custom_call" | custom-call | flops 679477248 | bytes 8663556 | tf_op jit(solution)/shard_map/pallas_call | solution.py:179
  144.9 2.5 %collective-permute-done.16.r2 = f32[128,256]{1,0:T(8,128)S(1)} collective-permute-done((f32[128,256]{1,0:T(8,128)S(1)}, f32[128,256]{1,0:T(8,128)S(1)}, u32[]{:S(2)}, u32[]{:S(2)}) %collective-permute-start.16) | collective-permute-done | bytes 131104 | tf_op jit(solution)/shard_map/ppermute | solution.py:201
  147.3 2.0 %shard_map.119 = (f32[1152,256]{1,0:T(8,128)}, f32[1152,256]{1,0:T(8,128)}) custom-call(s32[1]{0:T(128)S(6)} %copy.22.length, f32[128,256]{1,0:T(8,128)S(1)} %collective-permute-done.14.r0, f32[128,256]{1,0:T(8,128)S(1)} %collective-permute-done.15.r1, f32[128,256]{1,0:T(8,128)S(1)} %collective-permute-done.16.r2, ...), custom_call_target="tpu_custom_call" | custom-call | flops 1207959552 | bytes 7606788 | tf_op jit(solution)/shard_map/pallas_call | solution.py:179
  (110 shorter events, 30.1 us)
Async XLA Ops:
  2.5 16.7 %copy-start.18 = (bf16[1,32,1152]{2,1,0:T(8,128)(2,1)S(1)}, bf16[1,32,1152]{2,1,0:T(8,128)(2,1)}, u32[]{:S(2)}) copy-start(bf16[1,32,1152]{2,1,0:T(8,128)(2,1)} %param.16) | copy-start | bytes 221188
  3.4 17.7 %copy-start.3 = (f32[1152,256]{1,0:T(8,128)}, f32[1152,256]{1,0:T(8,128)S(1)}, u32[]{:S(2)}) copy-start(f32[1152,256]{1,0:T(8,128)S(1)} %get-tuple-element.48.resid) | copy-start | bytes 3538948
  3.4 17.7 %copy-start.26 = (f32[128,256]{1,0:T(8,128)}, f32[128,256]{1,0:T(8,128)S(1)}, u32[]{:S(2)}) copy-start(f32[128,256]{1,0:T(8,128)S(1)} %get-tuple-element.50.p1) | copy-start | bytes 393220
  3.4 12.3 %collective-permute-start = (f32[128,256]{1,0:T(8,128)S(1)}, f32[128,256]{1,0:T(8,128)S(1)}, u32[]{:S(2)}, u32[]{:S(2)}) collective-permute-start(f32[128,256]{1,0:T(8,128)S(1)} %get-tuple-element.49.p0), channel_id=1, source_target_pairs={{0,1},{1,0},{2,3},{3,2},{4,5},{5,4},{6,7},{7,6},{8,9},{9,8},{10,11... | collective-permute-start | bytes 393224 | tf_op jit(solution)/shard_map/ppermute | solution.py:201
  3.5 13.1 %collective-permute-start.1 = (f32[128,256]{1,0:T(8,128)S(1)}, f32[128,256]{1,0:T(8,128)S(1)}, u32[]{:S(2)}, u32[]{:S(2)}) collective-permute-start(f32[128,256]{1,0:T(8,128)S(1)} %get-tuple-element.50.p1), channel_id=1, source_target_pairs={{1,2},{2,1},{3,4},{4,3},{5,6},{6,5},{7,8},{8,7},{9,10},{10,9},{11,... | collective-permute-start | bytes 393224 | tf_op jit(solution)/shard_map/ppermute | solution.py:201
  11.3 7.9 %collective-permute-start.2 = (f32[128,256]{1,0:T(8,128)S(1)}, f32[128,256]{1,0:T(8,128)S(1)}, u32[]{:S(2)}, u32[]{:S(2)}) collective-permute-start(f32[128,256]{1,0:T(8,128)S(1)} %get-tuple-element.51.p2), channel_id=1, source_target_pairs={{16,32},{32,16},{48,64},{64,48},{80,96},{96,80},{112,128},{128,112... | collective-permute-start | bytes 393224 | tf_op jit(solution)/shard_map/ppermute | solution.py:201
  13.9 5.3 %collective-permute-start.3 = (f32[128,256]{1,0:T(8,128)S(1)}, f32[128,256]{1,0:T(8,128)S(1)}, u32[]{:S(2)}, u32[]{:S(2)}) collective-permute-start(f32[128,256]{1,0:T(8,128)S(1)} %get-tuple-element.52.p3), channel_id=1, source_target_pairs={{0,16},{16,0},{32,48},{48,32},{64,80},{80,64},{96,112},{112,96},{1... | collective-permute-start | bytes 393224 | tf_op jit(solution)/shard_map/ppermute | solution.py:201
  21.0 8.5 %copy-start.36 = (f32[1,1152]{1,0:T(1,128)S(1)}, f32[1,1152]{1,0:T(1,128)}, u32[]{:S(2)}) copy-start(f32[1,1152]{1,0:T(1,128)} %param.15) | copy-start | bytes 13828
  21.0 25.0 %all-to-all-start = ((f32[16,32,256]{2,1,0:T(8,128)}), f32[16,32,256]{2,1,0:T(8,128)}, u32[]{:S(2)}, u32[]{:S(2)}) async-start(f32[16,32,256]{2,1,0:T(8,128)} %get-tuple-element.55), calls=%async_computation | async-start | bytes 1048576 | tf_op jit(solution)/shard_map/all_to_all | solution.py:268
  36.2 9.8 %copy-start.5 = (f32[512,512]{1,0:T(8,128)S(1)}, f32[512,512]{1,0:T(8,128)}, u32[]{:S(2)}) copy-start(f32[512,512]{1,0:T(8,128)} %coarse.3) | copy-start | bytes 3145732
  46.1 14.2 %copy-start.20 = (f32[512,256]{1,0:T(8,128)S(1)}, f32[512,256]{1,0:T(8,128)}, u32[]{:S(2)}) copy-start(f32[512,256]{1,0:T(8,128)} %copy-done.19) | copy-start | bytes 1572868
  47.8 20.0 %copy-start.13 = (f32[1152,256]{1,0:T(8,128)S(1)}, f32[1152,256]{1,0:T(8,128)}, u32[]{:S(2)}) copy-start(f32[1152,256]{1,0:T(8,128)} %copy-done.12) | copy-start | bytes 3538948
  47.8 1.6 %collective-permute-start.4 = (f32[256,256]{1,0:T(8,128)S(1)}, f32[256,256]{1,0:T(8,128)S(1)}, u32[]{:S(2)}, u32[]{:S(2)}) collective-permute-start(f32[256,256]{1,0:T(8,128)S(1)} %get-tuple-element.60), channel_id=1, source_target_pairs={{0,16},{16,0},{32,48},{48,32},{64,80},{80,64},{96,112},{112,96},{1... | collective-permute-start | bytes 786440 | tf_op jit(solution)/shard_map/ppermute | solution.py:201
  60.5 7.7 %collective-permute-start.5 = (f32[128,256]{1,0:T(8,128)S(1)}, f32[128,256]{1,0:T(8,128)S(1)}, u32[]{:S(2)}, u32[]{:S(2)}) collective-permute-start(f32[128,256]{1,0:T(8,128)S(1)} %get-tuple-element.64.c0), channel_id=1, source_target_pairs={{0,1},{1,0},{2,3},{3,2},{4,5},{5,4},{6,7},{7,6},{8,9},{9,8},{10,11... | collective-permute-start | bytes 393224 | tf_op jit(solution)/shard_map/ppermute | solution.py:201
  62.2 10.5 %collective-permute-start.6 = (f32[128,256]{1,0:T(8,128)S(1)}, f32[128,256]{1,0:T(8,128)S(1)}, u32[]{:S(2)}, u32[]{:S(2)}) collective-permute-start(f32[128,256]{1,0:T(8,128)S(1)} %get-tuple-element.65.c1), channel_id=1, source_target_pairs={{1,2},{2,1},{3,4},{4,3},{5,6},{6,5},{7,8},{8,7},{9,10},{10,9},{11,... | collective-permute-start | bytes 393224 | tf_op jit(solution)/shard_map/ppermute | solution.py:201
  64.4 10.6 %collective-permute-start.7 = (f32[128,256]{1,0:T(8,128)S(1)}, f32[128,256]{1,0:T(8,128)S(1)}, u32[]{:S(2)}, u32[]{:S(2)}) collective-permute-start(f32[128,256]{1,0:T(8,128)S(1)} %get-tuple-element.66.c2), channel_id=1, source_target_pairs={{16,32},{32,16},{48,64},{64,48},{80,96},{96,80},{112,128},{128,112... | collective-permute-start | bytes 393224 | tf_op jit(solution)/shard_map/ppermute | solution.py:201
  66.3 8.7 %collective-permute-start.8 = (f32[128,256]{1,0:T(8,128)S(1)}, f32[128,256]{1,0:T(8,128)S(1)}, u32[]{:S(2)}, u32[]{:S(2)}) collective-permute-start(f32[128,256]{1,0:T(8,128)S(1)} %get-tuple-element.67.c3), channel_id=1, source_target_pairs={{0,16},{16,0},{32,48},{48,32},{64,80},{80,64},{96,112},{112,96},{1... | collective-permute-start | bytes 393224 | tf_op jit(solution)/shard_map/ppermute | solution.py:201
  67.8 7.2 %copy-start.29 = (f32[128,256]{1,0:T(8,128)S(1)}, f32[128,256]{1,0:T(8,128)}, u32[]{:S(2)}) copy-start(f32[128,256]{1,0:T(8,128)} %copy-done.28) | copy-start | bytes 393220
  67.8 7.2 %copy-start.31 = (f32[128,256]{1,0:T(8,128)S(1)}, f32[128,256]{1,0:T(8,128)}, u32[]{:S(2)}) copy-start(f32[128,256]{1,0:T(8,128)} %copy-done.30) | copy-start | bytes 393220
  75.0 8.3 %copy-start.1 = (bf16[1,1152,1152]{2,1,0:T(8,128)(2,1)S(1)}, bf16[1,1152,1152]{2,1,0:T(8,128)(2,1)}, u32[]{:S(2)}) copy-start(bf16[1,1152,1152]{2,1,0:T(8,128)(2,1)} %param.14) | copy-start | bytes 7962628
  75.0 8.3 %copy-start.4 = (f32[1152,256]{1,0:T(8,128)S(1)}, f32[1152,256]{1,0:T(8,128)}, u32[]{:S(2)}) copy-start(f32[1152,256]{1,0:T(8,128)} %copy-done.3) | copy-start | bytes 3538948
  76.7 10.0 %collective-permute-start.9 = (f32[128,256]{1,0:T(8,128)S(1)}, f32[128,256]{1,0:T(8,128)S(1)}, u32[]{:S(2)}, u32[]{:S(2)}) collective-permute-start(f32[128,256]{1,0:T(8,128)S(1)} %get-tuple-element.72), channel_id=1, source_target_pairs={{0,1},{1,0},{2,3},{3,2},{4,5},{5,4},{6,7},{7,6},{8,9},{9,8},{10,11... | collective-permute-start | bytes 393224 | tf_op jit(solution)/shard_map/ppermute | solution.py:201
  76.8 9.9 %collective-permute-start.10 = (f32[128,256]{1,0:T(8,128)S(1)}, f32[128,256]{1,0:T(8,128)S(1)}, u32[]{:S(2)}, u32[]{:S(2)}) collective-permute-start(f32[128,256]{1,0:T(8,128)S(1)} %get-tuple-element.73), channel_id=1, source_target_pairs={{1,2},{2,1},{3,4},{4,3},{5,6},{6,5},{7,8},{8,7},{9,10},{10,9},{11,... | collective-permute-start | bytes 393224 | tf_op jit(solution)/shard_map/ppermute | solution.py:201
  81.1 8.6 %collective-permute-start.11 = (f32[128,256]{1,0:T(8,128)S(1)}, f32[128,256]{1,0:T(8,128)S(1)}, u32[]{:S(2)}, u32[]{:S(2)}) collective-permute-start(f32[128,256]{1,0:T(8,128)S(1)} %get-tuple-element.74), channel_id=1, source_target_pairs={{16,32},{32,16},{48,64},{64,48},{80,96},{96,80},{112,128},{128,112... | collective-permute-start | bytes 393224 | tf_op jit(solution)/shard_map/ppermute | solution.py:201
  83.0 6.7 %collective-permute-start.12 = (f32[128,256]{1,0:T(8,128)S(1)}, f32[128,256]{1,0:T(8,128)S(1)}, u32[]{:S(2)}, u32[]{:S(2)}) collective-permute-start(f32[128,256]{1,0:T(8,128)S(1)} %get-tuple-element.75), channel_id=1, source_target_pairs={{0,16},{16,0},{32,48},{48,32},{64,80},{80,64},{96,112},{112,96},{1... | collective-permute-start | bytes 393224 | tf_op jit(solution)/shard_map/ppermute | solution.py:201
  92.8 21.2 %all-to-all-start.2 = ((f32[16,32,256]{2,1,0:T(8,128)}), f32[16,32,256]{2,1,0:T(8,128)}, u32[]{:S(2)}, u32[]{:S(2)}) async-start(f32[16,32,256]{2,1,0:T(8,128)} %copy-done.23), calls=%async_computation.2 | async-start | bytes 1048576 | tf_op jit(solution)/shard_map/all_to_all | solution.py:268
  115.2 25.0 %copy-start.2 = (bf16[1,1152,1152]{2,1,0:T(8,128)(2,1)S(1)}, bf16[1,1152,1152]{2,1,0:T(8,128)(2,1)}, u32[]{:S(2)}) copy-start(bf16[1,1152,1152]{2,1,0:T(8,128)(2,1)} %param.14) | copy-start | bytes 7962628
  117.0 1.6 %collective-permute-start.13 = (f32[256,256]{1,0:T(8,128)S(1)}, f32[256,256]{1,0:T(8,128)S(1)}, u32[]{:S(2)}, u32[]{:S(2)}) collective-permute-start(f32[256,256]{1,0:T(8,128)S(1)} %get-tuple-element.80), channel_id=1, source_target_pairs={{0,16},{16,0},{32,48},{48,32},{64,80},{80,64},{96,112},{112,96},{1... | collective-permute-start | bytes 786440 | tf_op jit(solution)/shard_map/ppermute | solution.py:201
  131.6 12.9 %collective-permute-start.14 = (f32[128,256]{1,0:T(8,128)S(1)}, f32[128,256]{1,0:T(8,128)S(1)}, u32[]{:S(2)}, u32[]{:S(2)}) collective-permute-start(f32[128,256]{1,0:T(8,128)S(1)} %get-tuple-element.82), channel_id=1, source_target_pairs={{0,1},{1,0},{2,3},{3,2},{4,5},{5,4},{6,7},{7,6},{8,9},{9,8},{10,11... | collective-permute-start | bytes 393224 | tf_op jit(solution)/shard_map/ppermute | solution.py:201
  134.4 10.5 %collective-permute-start.15 = (f32[128,256]{1,0:T(8,128)S(1)}, f32[128,256]{1,0:T(8,128)S(1)}, u32[]{:S(2)}, u32[]{:S(2)}) collective-permute-start(f32[128,256]{1,0:T(8,128)S(1)} %get-tuple-element.83), channel_id=1, source_target_pairs={{1,2},{2,1},{3,4},{4,3},{5,6},{6,5},{7,8},{8,7},{9,10},{10,9},{11,... | collective-permute-start | bytes 393224 | tf_op jit(solution)/shard_map/ppermute | solution.py:201
  137.1 10.2 %collective-permute-start.16 = (f32[128,256]{1,0:T(8,128)S(1)}, f32[128,256]{1,0:T(8,128)S(1)}, u32[]{:S(2)}, u32[]{:S(2)}) collective-permute-start(f32[128,256]{1,0:T(8,128)S(1)} %get-tuple-element.84), channel_id=1, source_target_pairs={{16,32},{32,16},{48,64},{64,48},{80,96},{96,80},{112,128},{128,112... | collective-permute-start | bytes 393224 | tf_op jit(solution)/shard_map/ppermute | solution.py:201
  139.0 8.3 %collective-permute-start.17 = (f32[128,256]{1,0:T(8,128)S(1)}, f32[128,256]{1,0:T(8,128)S(1)}, u32[]{:S(2)}, u32[]{:S(2)}) collective-permute-start(f32[128,256]{1,0:T(8,128)S(1)} %get-tuple-element.85), channel_id=1, source_target_pairs={{0,16},{16,0},{32,48},{48,32},{64,80},{80,64},{96,112},{112,96},{1... | collective-permute-start | bytes 393224 | tf_op jit(solution)/shard_map/ppermute | solution.py:201
  (25 other events, 60.7 us)

commit v4 on v3

--- a/solution.py
+++ b/solution.py
@@ -89,7 +89,17 @@
     token[...] = jnp.zeros_like(token)
 
 
-def coarse_kernel(core, coarse, gathered, after, after_too, keep, send):
+def late_local_kernel(after, inverse, assembled, local, token):
+    token[...] = after[...]
+    local[...] = dot(inverse[...], assembled[...])
+
+
+def sum_kernel(keep, other, after, out):
+    out[...] = (keep[...] + other[...]).reshape(out.shape)
+
+
+def coarse_kernel(core, coarse, gathered, after, after_too, keep, send, token):
+    token[...] = after[...]
     groups, modes, loads = gathered.shape
     g_high, g_low = halves(gathered[...].reshape(groups * modes, loads))
     high, low = halves(coarse[...])
@@ -110,6 +120,14 @@
     offdiag_rows[...] = dot_t(put[...], offdiag[...]).astype(BF16)
 
 
+def late_sent_kernel(parts, local, put, basis_rows, coarse_out, f0, f1, f2, f3):
+    total = jnp.sum(parts[...], axis=0)
+    coarse_out[...] = total
+    high, low = halves(total)
+    rows = basis_rows[...]
+    store_faces(take(put[...], local[...]) + dot(rows, high) + dot(rows, low), (f0, f1, f2, f3))
+
+
 def sent_kernel(parts, local_faces, basis_rows, coarse_out, f0, f1, f2, f3):
     total = jnp.sum(parts[...], axis=0)
     coarse_out[...] = total
@@ -137,11 +155,11 @@
     store_faces(load_faces((p0, p1, p2, p3)) - applied, (g0, g1, g2, g3))
 
 
-def residual_kernel(length, increment, diag, resid, offdiag, put, resid_out, solution, offdiag_columns, sem):
+def residual_kernel(length, increment, diag, loads, offdiag, put, resid_out, solution, offdiag_columns, sem):
     leave = pltpu.make_async_copy(increment, solution, sem)
     leave.start()
     applied = dot(offdiag[...], increment[...].astype(BF16)) + diag[...] * increment[...]
-    resid_out[...] = resid[...] - live_of(length, resid.shape[0]) * applied
+    resid_out[...] = (loads[...] - applied) * live_of(length, loads.shape[0])
     offdiag_columns[...] = dot(offdiag[...], put[...]).astype(BF16)
     leave.wait()
 
@@ -266,38 +284,52 @@
             flops=gather_flops,
         )
         gathered = lax.all_to_all(coarse_in, "grid", 0, 0)
-        local, local_faces, ahead = call(
-            local_kernel,
-            [block, like(nrows, nloads), mark],
-            (inverse, assembled, put),
-            "vvv",
-            flops=square_flops + gather_flops,
-        )
         if sweep == 0:
-            offdiag_rows, basis_rows, diag_rows, ahead_too = call(
+            local, local_faces, ahead = call(
+                local_kernel,
+                [block, like(nrows, nloads), mark],
+                (inverse, assembled, put),
+                "vvv",
+                flops=square_flops + gather_flops,
+            )
+            offdiag_rows, basis_rows, diag_rows, after = call(
                 rows_kernel,
                 [like(nrows, n, dtype=BF16), like(nrows, modes, dtype=BF16), like(nrows, 128), mark],
                 (after, put, offdiag, basis_t, diag),
                 "vvvvv",
                 flops=2 * nrows * n * n,
             )
-        keep, send = call(
+        else:
+            ahead = after
+        keep, send, after = call(
             coarse_kernel,
-            [like(order[0] // 2, nloads)] * 2,
-            (core, coarse_inverse, gathered, ahead, ahead_too),
+            [like(order[0] // 2, nloads)] * 2 + [mark],
+            (core, coarse_inverse, gathered, after, ahead),
             "svvvv",
             flops=6 * order[0] * order[1] * nloads,
         )
         other = swap(send, "sub", 0)
-        parts = (keep + other).reshape(nsub // 2, modes, nloads)
         groups = [list(range(i, nsub, 2)) for i in range(2)]
+        if sweep == 0:
+            parts = (keep + other).reshape(nsub // 2, modes, nloads)
+        else:
+            local, after = call(
+                late_local_kernel, [block, mark], (after, inverse, assembled), "vvv", flops=square_flops
+            )
+            (parts,) = call(sum_kernel, [like(nsub // 2, modes, nloads)], (keep, other, after), "vvv")
         parts = lax.all_to_all(parts, "sub", 0, 0, axis_index_groups=groups)
-        coarse_out, *corrected = call(
-            sent_kernel,
-            [like(modes, nloads)] + [face] * 4,
-            (parts, local_faces, basis_rows),
-            "vvv",
-        )
+        if sweep == 0:
+            coarse_out, *corrected = call(
+                sent_kernel, [like(modes, nloads)] + [face] * 4, (parts, local_faces, basis_rows), "vvv"
+            )
+        else:
+            coarse_out, *corrected = call(
+                late_sent_kernel,
+                [like(modes, nloads)] + [face] * 4,
+                (parts, local, put, basis_rows),
+                "vvvv",
+                flops=gather_flops,
+            )
         received = exchange(corrected)
         if sweep < ITERS - 1:
             (correction,) = call(
@@ -314,7 +346,7 @@
             resid, solution, offdiag_columns = call(
                 residual_kernel,
                 [block, block, like(n, nrows, dtype=BF16)],
-                (iface_len, increment, diag, resid, offdiag, put),
+                (iface_len, increment, diag, loads, offdiag, put),
                 "svvvvv",
                 "vhv",
                 [pltpu.SemaphoreType.DMA],

time: 150 us -> 148 us (0.987)
  blocking collectives: 22.4 us -> 43.8 us
  local copies, waits for them, and re-layouts: 18.2 us -> 8.98 us
  starting transfers between devices: 48.3 us -> 41.6 us
  waiting for transfers between devices: 31.9 us -> 26.4 us
  Pallas kernels: 25.9 us -> 23.6 us
    all_to_all x0 -> x1, blocking collectives: none -> 20.9 us  [body(): gathered = lax.all_to_all(coarse_in, 'grid', 0, 0)]
    unnamed x75 -> x55, local copies, waits for them, and re-layouts: 17.9 us -> 8.67 us
    all_to_all x2 -> x1, waiting for transfers between devices: 12.2 us -> 4.01 us  [body(): gathered = lax.all_to_all(coarse_in, 'grid', 0, 0)]
    all_to_all x2 -> x1, starting transfers between devices: 14.8 us -> 8.23 us  [body(): gathered = lax.all_to_all(coarse_in, 'grid', 0, 0)]
    ppermute x18, waiting for transfers between devices: 19.7 us -> 22.4 us  [swap(): lax.ppermute(array, axis, [(i, j) for i, j in pairs if 0 <= j < size])]
    pallas_call x16 -> x17, Pallas kernels: 25.9 us -> 23.6 us  [call(): pl.pallas_call(kernel, out_shape=outs, in_specs=[pl.BlockSpec(memory_spac...]
  transfers between devices with their start and end apart: 20 -> 19, of which waited for: 12 -> 11; matrix products, arithmetic and copies ran while one was open for 0% -> 0% of each run, Pallas kernels for 9% -> 8%
where the time goes in v4:
time: 148 us; the launch traced here: 147 us
  blocking collectives  43.8 us (30%)
  starting transfers between devices  41.6 us (28%)
  waiting for transfers between devices  26.4 us (18%)
  Pallas kernels  23.6 us (16%)
  local copies, waits for them, and re-layouts  8.98 us (6%)
  between operations  1.96 us (1%)
    ppermute x18, starting transfers between devices, swap(): lax.ppermute(array, axis, [(i, j) for i, j in pairs if 0 <= j < size])  33.3 us
    pallas_call x17, Pallas kernels, call(): pl.pallas_call(kernel, out_shape=outs, in_specs=[pl.BlockSpec(memory_spac...  23.6 us
    all_to_all x2, blocking collectives, body(): parts = lax.all_to_all(parts, 'sub', 0, 0, axis_index_groups=groups)  22.9 us
    ppermute x18, waiting for transfers between devices, swap(): lax.ppermute(array, axis, [(i, j) for i, j in pairs if 0 <= j < size])  22.4 us
    all_to_all x1, blocking collectives, body(): gathered = lax.all_to_all(coarse_in, 'grid', 0, 0)  20.9 us
    unnamed x55, local copies, waits for them, and re-layouts  8.67 us
    all_to_all x1, starting transfers between devices, body(): gathered = lax.all_to_all(coarse_in, 'grid', 0, 0)  8.23 us
    all_to_all x1, waiting for transfers between devices, body(): gathered = lax.all_to_all(coarse_in, 'grid', 0, 0)  4.01 us
  transfers between devices with their start and end apart: 19, of which 11 were waited for; matrix products, arithmetic and copies ran while one was open for 0% of the time, Pallas kernels for 8%

profile of v4, /device:TPU:72, one launch (start us, length us, event | category | flops | bytes accessed | tf_op | source)
XLA Modules:
  0.0 147.1 jit_solution(7062565996368792151)
XLA Ops:
  3.5 7.8 %collective-permute-start.1 = (f32[128,256]{1,0:T(8,128)S(1)}, f32[128,256]{1,0:T(8,128)S(1)}, u32[]{:S(2)}, u32[]{:S(2)}) collective-permute-start(f32[128,256]{1,0:T(8,128)S(1)} %get-tuple-element.51.p1), channel_id=1, source_target_pairs={{1,2},{2,1},{3,4},{4,3},{5,6},{6,5},{7,8},{8,7},{9,10},{10,9},{11,... | collective-permute-start | bytes 393224 | tf_op jit(solution)/shard_map/ppermute | solution.py:219
  11.3 1.9 %collective-permute-start.2 = (f32[128,256]{1,0:T(8,128)S(1)}, f32[128,256]{1,0:T(8,128)S(1)}, u32[]{:S(2)}, u32[]{:S(2)}) collective-permute-start(f32[128,256]{1,0:T(8,128)S(1)} %get-tuple-element.52.p2), channel_id=1, source_target_pairs={{16,32},{32,16},{48,64},{64,48},{80,96},{96,80},{112,128},{128,112... | collective-permute-start | bytes 393224 | tf_op jit(solution)/shard_map/ppermute | solution.py:219
  14.5 2.1 %collective-permute-done.1.f1 = f32[128,256]{1,0:T(8,128)S(1)} collective-permute-done((f32[128,256]{1,0:T(8,128)S(1)}, f32[128,256]{1,0:T(8,128)S(1)}, u32[]{:S(2)}, u32[]{:S(2)}) %collective-permute-start.1) | collective-permute-done | bytes 131104 | tf_op jit(solution)/shard_map/ppermute | solution.py:219
  16.6 2.6 %collective-permute-done.2.f2 = f32[128,256]{1,0:T(8,128)S(1)} collective-permute-done((f32[128,256]{1,0:T(8,128)S(1)}, f32[128,256]{1,0:T(8,128)S(1)}, u32[]{:S(2)}, u32[]{:S(2)}) %collective-permute-start.2) | collective-permute-done | bytes 131104 | tf_op jit(solution)/shard_map/ppermute | solution.py:219
  19.2 1.8 %shard_map.106 = (bf16[1152,256]{1,0:T(8,128)(2,1)S(1)}, f32[16,32,256]{2,1,0:T(8,128)}, f32[8,128]{1,0:T(8,128)S(1)}) custom-call(f32[1152,256]{1,0:T(8,128)S(1)} %get-tuple-element.49.resid, f32[128,256]{1,0:T(8,128)S(1)} %collective-permute-done.f0, f32[128,256]{1,0:T(8,128)S(1)} %collective-permute-done.1.f1, f32[128,256]{1,0:T(8,128)S(1)} %collective-permute-done.2.f2, ...), custom_call_target="tpu_custom_call" | custom-call | flops 603979776 | bytes 4075520 | tf_op jit(solution)/shard_map/pallas_call | solution.py:197
  21.9 8.2 %all-to-all-start = ((f32[16,32,256]{2,1,0:T(8,128)}), f32[16,32,256]{2,1,0:T(8,128)}, u32[]{:S(2)}, u32[]{:S(2)}) async-start(f32[16,32,256]{2,1,0:T(8,128)} %get-tuple-element.56), calls=%async_computation | async-start | bytes 1048576 | tf_op jit(solution)/shard_map/all_to_all | solution.py:286
  30.6 1.7 %copy-done.5 = bf16[1,1152,1152]{2,1,0:T(8,128)(2,1)S(1)} copy-done((bf16[1,1152,1152]{2,1,0:T(8,128)(2,1)S(1)}, bf16[1,1152,1152]{2,1,0:T(8,128)(2,1)}, u32[]{:S(2)}) %copy-start.5) | copy-done | bytes 2654232
  33.4 2.9 %shard_map.107 = (f32[1152,256]{1,0:T(8,128)S(1)}, f32[512,256]{1,0:T(8,128)S(1)}, f32[8,128]{1,0:T(8,128)S(1)}) custom-call(bf16[1152,1152]{1,0:T(8,128)(2,1)S(1)} %bitcast.24, bf16[1152,256]{1,0:T(8,128)(2,1)S(1)} %copy-done.25, bf16[1152,512]{1,0:T(8,128)(2,1)S(1)} %shard_map.104.put), custom_call_target="tpu_custom_call" | custom-call | flops 1283457024 | bytes 6131712 | tf_op jit(solution)/shard_map/pallas_call | solution.py:197
  38.1 3.0 %shard_map.108 = (bf16[512,1152]{1,0:T(8,128)(2,1)S(1)}, bf16[512,32]{1,0:T(8,128)(2,1)S(1)}, f32[512,128]{1,0:T(8,128)S(1)}, f32[8,128]{1,0:T(8,128)S(1)}) custom-call(f32[8,128]{1,0:T(8,128)S(1)} %get-tuple-element.57.after, bf16[1152,512]{1,0:T(8,128)(2,1)S(1)} %shard_map.104.put, bf16[1152,1152]{1,0:T(8,128)(2,1)S(1)} %bitcast.16, ...), custom_call_target="tpu_custom_call" | custom-call | flops 1358954496 | bytes 5394944 | tf_op jit(solution)/shard_map/pallas_call | solution.py:197
  42.9 4.0 %all-to-all-done.gathered = f32[16,32,256]{2,1,0:T(8,128)} async-done(((f32[16,32,256]{2,1,0:T(8,128)}), f32[16,32,256]{2,1,0:T(8,128)}, u32[]{:S(2)}, u32[]{:S(2)}) %all-to-all-start) | async-done | bytes 524320 | tf_op jit(solution)/shard_map/all_to_all | solution.py:286
  48.1 2.2 %shard_map.109 = (f32[256,256]{1,0:T(8,128)S(1)}, f32[256,256]{1,0:T(8,128)S(1)}, f32[8,128]{1,0:T(8,128)}) custom-call(s32[1]{0:T(128)} %bitcast.core, f32[512,512]{1,0:T(8,128)S(1)} %copy-done.3, f32[16,32,256]{2,1,0:T(8,128)} %all-to-all-done.gathered, f32[8,128]{1,0:T(8,128)S(1)} %get-tuple-element.58.after, f32[8,128]{1,0:T(8,128)S(1)} %get-tuple-element.59.after_too), custom_call_target="tpu_custom_call" | custom-call | flops 402653184 | bytes 2109444 | tf_op jit(solution)/shard_map/pallas_call | solution.py:197
  50.3 1.5 %collective-permute-done.4 = f32[256,256]{1,0:T(8,128)S(1)} collective-permute-done((f32[256,256]{1,0:T(8,128)S(1)}, f32[256,256]{1,0:T(8,128)S(1)}, u32[]{:S(2)}, u32[]{:S(2)}) %collective-permute-start.4) | collective-permute-done | bytes 262176 | tf_op jit(solution)/shard_map/ppermute | solution.py:219
  51.9 10.8 %all_to_all.20.parts = f32[8,32,256]{2,1,0:T(8,128)S(1)} all-to-all(f32[8,32,256]{2,1,0:T(8,128)S(1)} %bitcast.29), channel_id=1, replica_groups={{0,32,64,96,128,160,192,224},{16,48,80,112,144,176,208,240},{1,33,65,97..., dimensions={0} | all-to-all | bytes 524288 | tf_op jit(solution)/shard_map/all_to_all | solution.py:320
  63.0 1.7 %collective-permute-start.5 = (f32[128,256]{1,0:T(8,128)S(1)}, f32[128,256]{1,0:T(8,128)S(1)}, u32[]{:S(2)}, u32[]{:S(2)}) collective-permute-start(f32[128,256]{1,0:T(8,128)S(1)} %get-tuple-element.65.c0), channel_id=1, source_target_pairs={{0,1},{1,0},{2,3},{3,2},{4,5},{5,4},{6,7},{7,6},{8,9},{9,8},{10,11... | collective-permute-start | bytes 393224 | tf_op jit(solution)/shard_map/ppermute | solution.py:219
  64.7 2.2 %collective-permute-start.6 = (f32[128,256]{1,0:T(8,128)S(1)}, f32[128,256]{1,0:T(8,128)S(1)}, u32[]{:S(2)}, u32[]{:S(2)}) collective-permute-start(f32[128,256]{1,0:T(8,128)S(1)} %get-tuple-element.66.c1), channel_id=1, source_target_pairs={{1,2},{2,1},{3,4},{4,3},{5,6},{6,5},{7,8},{8,7},{9,10},{10,9},{11,... | collective-permute-start | bytes 393224 | tf_op jit(solution)/shard_map/ppermute | solution.py:219
  66.9 1.9 %collective-permute-start.7 = (f32[128,256]{1,0:T(8,128)S(1)}, f32[128,256]{1,0:T(8,128)S(1)}, u32[]{:S(2)}, u32[]{:S(2)}) collective-permute-start(f32[128,256]{1,0:T(8,128)S(1)} %get-tuple-element.67.c2), channel_id=1, source_target_pairs={{16,32},{32,16},{48,64},{64,48},{80,96},{96,80},{112,128},{128,112... | collective-permute-start | bytes 393224 | tf_op jit(solution)/shard_map/ppermute | solution.py:219
  70.7 4.4 %collective-permute-done.6.r1 = f32[128,256]{1,0:T(8,128)S(1)} collective-permute-done((f32[128,256]{1,0:T(8,128)S(1)}, f32[128,256]{1,0:T(8,128)S(1)}, u32[]{:S(2)}, u32[]{:S(2)}) %collective-permute-start.6) | collective-permute-done | bytes 131104 | tf_op jit(solution)/shard_map/ppermute | solution.py:219
  75.1 2.1 %collective-permute-done.7.r2 = f32[128,256]{1,0:T(8,128)S(1)} collective-permute-done((f32[128,256]{1,0:T(8,128)S(1)}, f32[128,256]{1,0:T(8,128)S(1)}, u32[]{:S(2)}, u32[]{:S(2)}) %collective-permute-start.7) | collective-permute-done | bytes 131104 | tf_op jit(solution)/shard_map/ppermute | solution.py:219
  77.3 1.7 %shard_map.112 = (f32[1152,256]{1,0:T(8,128)S(1)}, f32[128,256]{1,0:T(8,128)S(1)}, f32[128,256]{1,0:T(8,128)S(1)}, f32[128,256]{1,0:T(8,128)S(1)}, f32[128,256]{1,0:T(8,128)S(1)}) custom-call(f32[1152,256]{1,0:T(8,128)S(1)} %shard_map.111.correction, f32[128,256]{1,0:T(8,128)S(1)} %collective-permute-done.5.r0, f32[128,256]{1,0:T(8,128)S(1)} %collective-permute-done.6.r1, ...), custom_call_target="tpu_custom_call" | custom-call | flops 1207959552 | bytes 7077888 | tf_op jit(solution)/shard_map/pallas_call | solution.py:197
  79.1 4.5 %collective-permute-start.10 = (f32[128,256]{1,0:T(8,128)S(1)}, f32[128,256]{1,0:T(8,128)S(1)}, u32[]{:S(2)}, u32[]{:S(2)}) collective-permute-start(f32[128,256]{1,0:T(8,128)S(1)} %get-tuple-element.74), channel_id=1, source_target_pairs={{1,2},{2,1},{3,4},{4,3},{5,6},{6,5},{7,8},{8,7},{9,10},{10,9},{11,... | collective-permute-start | bytes 393224 | tf_op jit(solution)/shard_map/ppermute | solution.py:219
  83.6 1.9 %collective-permute-start.11 = (f32[128,256]{1,0:T(8,128)S(1)}, f32[128,256]{1,0:T(8,128)S(1)}, u32[]{:S(2)}, u32[]{:S(2)}) collective-permute-start(f32[128,256]{1,0:T(8,128)S(1)} %get-tuple-element.75), channel_id=1, source_target_pairs={{16,32},{32,16},{48,64},{64,48},{80,96},{96,80},{112,128},{128,112... | collective-permute-start | bytes 393224 | tf_op jit(solution)/shard_map/ppermute | solution.py:219
  85.8 2.7 %shard_map.113 = (f32[1152,256]{1,0:T(8,128)S(1)}, f32[1152,256]{1,0:T(8,128)S(1)}, bf16[1152,512]{1,0:T(8,128)(2,1)S(1)}) custom-call(s32[1]{0:T(128)S(6)} %copy.22.length, f32[1152,256]{1,0:T(8,128)S(1)} %get-tuple-element.71.increment, f32[1152,1]{1,0:T(8,128)S(1)} %copy.16.diag, f32[1152,256]{1,0:T(8,128)S(1)} %bitcast.20, ...), custom_call_target="tpu_custom_call" | custom-call | flops 679477248 | bytes 9736708 | tf_op jit(solution)/shard_map/pallas_call | solution.py:197
  88.8 3.4 %collective-permute-done.11.f2 = f32[128,256]{1,0:T(8,128)S(1)} collective-permute-done((f32[128,256]{1,0:T(8,128)S(1)}, f32[128,256]{1,0:T(8,128)S(1)}, u32[]{:S(2)}, u32[]{:S(2)}) %collective-permute-start.11) | collective-permute-done | bytes 131104 | tf_op jit(solution)/shard_map/ppermute | solution.py:219
  93.2 20.9 %all_to_all.21.gathered = f32[16,32,256]{2,1,0:T(8,128)S(1)} all-to-all(f32[16,32,256]{2,1,0:T(8,128)S(1)} %get-tuple-element.77), channel_id=1, replica_groups=mesh['sub'=16,'grid'=16] {'grid'}, dimensions={0} | all-to-all | bytes 1048576 | tf_op jit(solution)/shard_map/all_to_all | solution.py:286
  116.4 12.2 %all_to_all.22.parts = f32[8,32,256]{2,1,0:T(8,128)S(1)} all-to-all(f32[8,32,256]{2,1,0:T(8,128)S(1)} %shard_map.117), channel_id=1, replica_groups={{0,32,64,96,128,160,192,224},{16,48,80,112,144,176,208,240},{1,33,65,97..., dimensions={0} | all-to-all | bytes 524288 | tf_op jit(solution)/shard_map/all_to_all | solution.py:320
  129.6 2.4 %collective-permute-start.14 = (f32[128,256]{1,0:T(8,128)S(1)}, f32[128,256]{1,0:T(8,128)S(1)}, u32[]{:S(2)}, u32[]{:S(2)}) collective-permute-start(f32[128,256]{1,0:T(8,128)S(1)} %get-tuple-element.85), channel_id=1, source_target_pairs={{0,1},{1,0},{2,3},{3,2},{4,5},{5,4},{6,7},{7,6},{8,9},{9,8},{10,11... | collective-permute-start | bytes 393224 | tf_op jit(solution)/shard_map/ppermute | solution.py:219
  132.0 2.6 %collective-permute-start.15 = (f32[128,256]{1,0:T(8,128)S(1)}, f32[128,256]{1,0:T(8,128)S(1)}, u32[]{:S(2)}, u32[]{:S(2)}) collective-permute-start(f32[128,256]{1,0:T(8,128)S(1)} %get-tuple-element.86), channel_id=1, source_target_pairs={{1,2},{2,1},{3,4},{4,3},{5,6},{6,5},{7,8},{8,7},{9,10},{10,9},{11,... | collective-permute-start | bytes 393224 | tf_op jit(solution)/shard_map/ppermute | solution.py:219
  134.6 1.9 %collective-permute-start.16 = (f32[128,256]{1,0:T(8,128)S(1)}, f32[128,256]{1,0:T(8,128)S(1)}, u32[]{:S(2)}, u32[]{:S(2)}) collective-permute-start(f32[128,256]{1,0:T(8,128)S(1)} %get-tuple-element.87), channel_id=1, source_target_pairs={{16,32},{32,16},{48,64},{64,48},{80,96},{96,80},{112,128},{128,112... | collective-permute-start | bytes 393224 | tf_op jit(solution)/shard_map/ppermute | solution.py:219
  137.8 1.7 %shard_map.119 = (f32[1152,256]{1,0:T(8,128)S(1)}, f32[1152,256]{1,0:T(8,128)S(1)}) custom-call(s32[1]{0:T(128)S(6)} %copy.22.length, f32[1152,256]{1,0:T(8,128)S(1)} %get-tuple-element.84.local, bf16[1152,32]{1,0:T(8,128)(2,1)S(1)} %bitcast.23, f32[32,256]{1,0:T(8,128)S(1)} %get-tuple-element.90.coarse_out, f32[1152,256]{1,0:T(8,128)S(1)} %get-tuple-element.91.before, ...), custom_call_target="tpu_custom_call" | custom-call | flops 679477248 | bytes 8663556 | tf_op jit(solution)/shard_map/pallas_call | solution.py:197
  139.6 2.9 %collective-permute-done.15.r1 = f32[128,256]{1,0:T(8,128)S(1)} collective-permute-done((f32[128,256]{1,0:T(8,128)S(1)}, f32[128,256]{1,0:T(8,128)S(1)}, u32[]{:S(2)}, u32[]{:S(2)}) %collective-permute-start.15) | collective-permute-done | bytes 131104 | tf_op jit(solution)/shard_map/ppermute | solution.py:219
  142.4 2.5 %collective-permute-done.16.r2 = f32[128,256]{1,0:T(8,128)S(1)} collective-permute-done((f32[128,256]{1,0:T(8,128)S(1)}, f32[128,256]{1,0:T(8,128)S(1)}, u32[]{:S(2)}, u32[]{:S(2)}) %collective-permute-start.16) | collective-permute-done | bytes 131104 | tf_op jit(solution)/shard_map/ppermute | solution.py:219
  144.9 2.0 %shard_map.120 = (f32[1152,256]{1,0:T(8,128)}, f32[1152,256]{1,0:T(8,128)}) custom-call(s32[1]{0:T(128)S(6)} %copy.22.length, f32[128,256]{1,0:T(8,128)S(1)} %collective-permute-done.14.r0, f32[128,256]{1,0:T(8,128)S(1)} %collective-permute-done.15.r1, f32[128,256]{1,0:T(8,128)S(1)} %collective-permute-done.16.r2, ...), custom_call_target="tpu_custom_call" | custom-call | flops 1207959552 | bytes 7606788 | tf_op jit(solution)/shard_map/pallas_call | solution.py:197
  (89 shorter events, 18.8 us)
Async XLA Ops:
  2.5 16.7 %copy-start.11 = (bf16[1,32,1152]{2,1,0:T(8,128)(2,1)S(1)}, bf16[1,32,1152]{2,1,0:T(8,128)(2,1)}, u32[]{:S(2)}) copy-start(bf16[1,32,1152]{2,1,0:T(8,128)(2,1)} %param.16) | copy-start | bytes 221188
  3.3 17.7 %copy-start.16 = (f32[128,256]{1,0:T(8,128)}, f32[128,256]{1,0:T(8,128)S(1)}, u32[]{:S(2)}) copy-start(f32[128,256]{1,0:T(8,128)S(1)} %get-tuple-element.50.p0) | copy-start | bytes 393220
  3.4 17.7 %copy-start.18 = (f32[128,256]{1,0:T(8,128)}, f32[128,256]{1,0:T(8,128)S(1)}, u32[]{:S(2)}) copy-start(f32[128,256]{1,0:T(8,128)S(1)} %get-tuple-element.51.p1) | copy-start | bytes 393220
  3.4 17.7 %copy-start.20 = (f32[128,256]{1,0:T(8,128)}, f32[128,256]{1,0:T(8,128)S(1)}, u32[]{:S(2)}) copy-start(f32[128,256]{1,0:T(8,128)S(1)} %get-tuple-element.52.p2) | copy-start | bytes 393220
  3.4 17.7 %copy-start.22 = (f32[128,256]{1,0:T(8,128)}, f32[128,256]{1,0:T(8,128)S(1)}, u32[]{:S(2)}) copy-start(f32[128,256]{1,0:T(8,128)S(1)} %get-tuple-element.53.p3) | copy-start | bytes 393220
  3.4 11.1 %collective-permute-start = (f32[128,256]{1,0:T(8,128)S(1)}, f32[128,256]{1,0:T(8,128)S(1)}, u32[]{:S(2)}, u32[]{:S(2)}) collective-permute-start(f32[128,256]{1,0:T(8,128)S(1)} %get-tuple-element.50.p0), channel_id=1, source_target_pairs={{0,1},{1,0},{2,3},{3,2},{4,5},{5,4},{6,7},{7,6},{8,9},{9,8},{10,11... | collective-permute-start | bytes 393224 | tf_op jit(solution)/shard_map/ppermute | solution.py:219
  3.5 13.1 %collective-permute-start.1 = (f32[128,256]{1,0:T(8,128)S(1)}, f32[128,256]{1,0:T(8,128)S(1)}, u32[]{:S(2)}, u32[]{:S(2)}) collective-permute-start(f32[128,256]{1,0:T(8,128)S(1)} %get-tuple-element.51.p1), channel_id=1, source_target_pairs={{1,2},{2,1},{3,4},{4,3},{5,6},{6,5},{7,8},{8,7},{9,10},{10,9},{11,... | collective-permute-start | bytes 393224 | tf_op jit(solution)/shard_map/ppermute | solution.py:219
  11.3 7.9 %collective-permute-start.2 = (f32[128,256]{1,0:T(8,128)S(1)}, f32[128,256]{1,0:T(8,128)S(1)}, u32[]{:S(2)}, u32[]{:S(2)}) collective-permute-start(f32[128,256]{1,0:T(8,128)S(1)} %get-tuple-element.52.p2), channel_id=1, source_target_pairs={{16,32},{32,16},{48,64},{64,48},{80,96},{96,80},{112,128},{128,112... | collective-permute-start | bytes 393224 | tf_op jit(solution)/shard_map/ppermute | solution.py:219
  13.3 5.9 %collective-permute-start.3 = (f32[128,256]{1,0:T(8,128)S(1)}, f32[128,256]{1,0:T(8,128)S(1)}, u32[]{:S(2)}, u32[]{:S(2)}) collective-permute-start(f32[128,256]{1,0:T(8,128)S(1)} %get-tuple-element.53.p3), channel_id=1, source_target_pairs={{0,16},{16,0},{32,48},{48,32},{64,80},{80,64},{96,112},{112,96},{1... | collective-permute-start | bytes 393224 | tf_op jit(solution)/shard_map/ppermute | solution.py:219
  21.9 8.5 %copy-start.26 = (f32[1,1152]{1,0:T(1,128)S(1)}, f32[1,1152]{1,0:T(1,128)}, u32[]{:S(2)}) copy-start(f32[1,1152]{1,0:T(1,128)} %param.15) | copy-start | bytes 13828
  21.9 25.0 %all-to-all-start = ((f32[16,32,256]{2,1,0:T(8,128)}), f32[16,32,256]{2,1,0:T(8,128)}, u32[]{:S(2)}, u32[]{:S(2)}) async-start(f32[16,32,256]{2,1,0:T(8,128)} %get-tuple-element.56), calls=%async_computation | async-start | bytes 1048576 | tf_op jit(solution)/shard_map/all_to_all | solution.py:286
  48.1 14.5 %copy-start.13 = (f32[512,256]{1,0:T(8,128)S(1)}, f32[512,256]{1,0:T(8,128)}, u32[]{:S(2)}) copy-start(f32[512,256]{1,0:T(8,128)} %copy-done.12) | copy-start | bytes 1572868
  50.3 19.9 %copy-start.8 = (f32[1152,256]{1,0:T(8,128)S(1)}, f32[1152,256]{1,0:T(8,128)}, u32[]{:S(2)}) copy-start(f32[1152,256]{1,0:T(8,128)} %copy-done.7) | copy-start | bytes 3538948
  50.3 1.5 %collective-permute-start.4 = (f32[256,256]{1,0:T(8,128)S(1)}, f32[256,256]{1,0:T(8,128)S(1)}, u32[]{:S(2)}, u32[]{:S(2)}) collective-permute-start(f32[256,256]{1,0:T(8,128)S(1)} %get-tuple-element.61), channel_id=1, source_target_pairs={{0,16},{16,0},{32,48},{48,32},{64,80},{80,64},{96,112},{112,96},{1... | collective-permute-start | bytes 786440 | tf_op jit(solution)/shard_map/ppermute | solution.py:219
  63.0 7.7 %collective-permute-start.5 = (f32[128,256]{1,0:T(8,128)S(1)}, f32[128,256]{1,0:T(8,128)S(1)}, u32[]{:S(2)}, u32[]{:S(2)}) collective-permute-start(f32[128,256]{1,0:T(8,128)S(1)} %get-tuple-element.65.c0), channel_id=1, source_target_pairs={{0,1},{1,0},{2,3},{3,2},{4,5},{5,4},{6,7},{7,6},{8,9},{9,8},{10,11... | collective-permute-start | bytes 393224 | tf_op jit(solution)/shard_map/ppermute | solution.py:219
  64.7 10.5 %collective-permute-start.6 = (f32[128,256]{1,0:T(8,128)S(1)}, f32[128,256]{1,0:T(8,128)S(1)}, u32[]{:S(2)}, u32[]{:S(2)}) collective-permute-start(f32[128,256]{1,0:T(8,128)S(1)} %get-tuple-element.66.c1), channel_id=1, source_target_pairs={{1,2},{2,1},{3,4},{4,3},{5,6},{6,5},{7,8},{8,7},{9,10},{10,9},{11,... | collective-permute-start | bytes 393224 | tf_op jit(solution)/shard_map/ppermute | solution.py:219
  66.9 10.4 %collective-permute-start.7 = (f32[128,256]{1,0:T(8,128)S(1)}, f32[128,256]{1,0:T(8,128)S(1)}, u32[]{:S(2)}, u32[]{:S(2)}) collective-permute-start(f32[128,256]{1,0:T(8,128)S(1)} %get-tuple-element.67.c2), channel_id=1, source_target_pairs={{16,32},{32,16},{48,64},{64,48},{80,96},{96,80},{112,128},{128,112... | collective-permute-start | bytes 393224 | tf_op jit(solution)/shard_map/ppermute | solution.py:219
  68.8 8.4 %collective-permute-start.8 = (f32[128,256]{1,0:T(8,128)S(1)}, f32[128,256]{1,0:T(8,128)S(1)}, u32[]{:S(2)}, u32[]{:S(2)}) collective-permute-start(f32[128,256]{1,0:T(8,128)S(1)} %get-tuple-element.68.c3), channel_id=1, source_target_pairs={{0,16},{16,0},{32,48},{48,32},{64,80},{80,64},{96,112},{112,96},{1... | collective-permute-start | bytes 393224 | tf_op jit(solution)/shard_map/ppermute | solution.py:219
  70.2 7.0 %copy-start.19 = (f32[128,256]{1,0:T(8,128)S(1)}, f32[128,256]{1,0:T(8,128)}, u32[]{:S(2)}) copy-start(f32[128,256]{1,0:T(8,128)} %copy-done.18) | copy-start | bytes 393220
  70.2 7.0 %copy-start.21 = (f32[128,256]{1,0:T(8,128)S(1)}, f32[128,256]{1,0:T(8,128)}, u32[]{:S(2)}) copy-start(f32[128,256]{1,0:T(8,128)} %copy-done.20) | copy-start | bytes 393220
  77.3 8.5 %copy-start.1 = (bf16[1,1152,1152]{2,1,0:T(8,128)(2,1)S(1)}, bf16[1,1152,1152]{2,1,0:T(8,128)(2,1)}, u32[]{:S(2)}) copy-start(bf16[1,1152,1152]{2,1,0:T(8,128)(2,1)} %param.14) | copy-start | bytes 7962628
  79.0 9.8 %collective-permute-start.9 = (f32[128,256]{1,0:T(8,128)S(1)}, f32[128,256]{1,0:T(8,128)S(1)}, u32[]{:S(2)}, u32[]{:S(2)}) collective-permute-start(f32[128,256]{1,0:T(8,128)S(1)} %get-tuple-element.73), channel_id=1, source_target_pairs={{0,1},{1,0},{2,3},{3,2},{4,5},{5,4},{6,7},{7,6},{8,9},{9,8},{10,11... | collective-permute-start | bytes 393224 | tf_op jit(solution)/shard_map/ppermute | solution.py:219
  79.1 9.7 %collective-permute-start.10 = (f32[128,256]{1,0:T(8,128)S(1)}, f32[128,256]{1,0:T(8,128)S(1)}, u32[]{:S(2)}, u32[]{:S(2)}) collective-permute-start(f32[128,256]{1,0:T(8,128)S(1)} %get-tuple-element.74), channel_id=1, source_target_pairs={{1,2},{2,1},{3,4},{4,3},{5,6},{6,5},{7,8},{8,7},{9,10},{10,9},{11,... | collective-permute-start | bytes 393224 | tf_op jit(solution)/shard_map/ppermute | solution.py:219
  83.6 8.6 %collective-permute-start.11 = (f32[128,256]{1,0:T(8,128)S(1)}, f32[128,256]{1,0:T(8,128)S(1)}, u32[]{:S(2)}, u32[]{:S(2)}) collective-permute-start(f32[128,256]{1,0:T(8,128)S(1)} %get-tuple-element.75), channel_id=1, source_target_pairs={{16,32},{32,16},{48,64},{64,48},{80,96},{96,80},{112,128},{128,112... | collective-permute-start | bytes 393224 | tf_op jit(solution)/shard_map/ppermute | solution.py:219
  85.5 6.7 %collective-permute-start.12 = (f32[128,256]{1,0:T(8,128)S(1)}, f32[128,256]{1,0:T(8,128)S(1)}, u32[]{:S(2)}, u32[]{:S(2)}) collective-permute-start(f32[128,256]{1,0:T(8,128)S(1)} %get-tuple-element.76), channel_id=1, source_target_pairs={{0,16},{16,0},{32,48},{48,32},{64,80},{80,64},{96,112},{112,96},{1... | collective-permute-start | bytes 393224 | tf_op jit(solution)/shard_map/ppermute | solution.py:219
  92.2 21.9 %copy-start.4 = (f32[512,512]{1,0:T(8,128)S(1)}, f32[512,512]{1,0:T(8,128)}, u32[]{:S(2)}) copy-start(f32[512,512]{1,0:T(8,128)} %coarse.3) | copy-start | bytes 3145732
  92.2 22.6 %copy-start.6 = (bf16[1,1152,1152]{2,1,0:T(8,128)(2,1)S(1)}, bf16[1,1152,1152]{2,1,0:T(8,128)(2,1)}, u32[]{:S(2)}) copy-start(bf16[1,1152,1152]{2,1,0:T(8,128)(2,1)} %param.13) | copy-start | bytes 7962628
  114.7 1.6 %collective-permute-start.13 = (f32[256,256]{1,0:T(8,128)S(1)}, f32[256,256]{1,0:T(8,128)S(1)}, u32[]{:S(2)}, u32[]{:S(2)}) collective-permute-start(f32[256,256]{1,0:T(8,128)S(1)} %get-tuple-element.80), channel_id=1, source_target_pairs={{0,16},{16,0},{32,48},{48,32},{64,80},{80,64},{96,112},{112,96},{1... | collective-permute-start | bytes 786440 | tf_op jit(solution)/shard_map/ppermute | solution.py:219
  129.6 10.0 %collective-permute-start.14 = (f32[128,256]{1,0:T(8,128)S(1)}, f32[128,256]{1,0:T(8,128)S(1)}, u32[]{:S(2)}, u32[]{:S(2)}) collective-permute-start(f32[128,256]{1,0:T(8,128)S(1)} %get-tuple-element.85), channel_id=1, source_target_pairs={{0,1},{1,0},{2,3},{3,2},{4,5},{5,4},{6,7},{7,6},{8,9},{9,8},{10,11... | collective-permute-start | bytes 393224 | tf_op jit(solution)/shard_map/ppermute | solution.py:219
  132.0 10.5 %collective-permute-start.15 = (f32[128,256]{1,0:T(8,128)S(1)}, f32[128,256]{1,0:T(8,128)S(1)}, u32[]{:S(2)}, u32[]{:S(2)}) collective-permute-start(f32[128,256]{1,0:T(8,128)S(1)} %get-tuple-element.86), channel_id=1, source_target_pairs={{1,2},{2,1},{3,4},{4,3},{5,6},{6,5},{7,8},{8,7},{9,10},{10,9},{11,... | collective-permute-start | bytes 393224 | tf_op jit(solution)/shard_map/ppermute | solution.py:219
  134.6 10.3 %collective-permute-start.16 = (f32[128,256]{1,0:T(8,128)S(1)}, f32[128,256]{1,0:T(8,128)S(1)}, u32[]{:S(2)}, u32[]{:S(2)}) collective-permute-start(f32[128,256]{1,0:T(8,128)S(1)} %get-tuple-element.87), channel_id=1, source_target_pairs={{16,32},{32,16},{48,64},{64,48},{80,96},{96,80},{112,128},{128,112... | collective-permute-start | bytes 393224 | tf_op jit(solution)/shard_map/ppermute | solution.py:219
  136.5 8.4 %collective-permute-start.17 = (f32[128,256]{1,0:T(8,128)S(1)}, f32[128,256]{1,0:T(8,128)S(1)}, u32[]{:S(2)}, u32[]{:S(2)}) collective-permute-start(f32[128,256]{1,0:T(8,128)S(1)} %get-tuple-element.88), channel_id=1, source_target_pairs={{0,16},{16,0},{32,48},{48,32},{64,80},{80,64},{96,112},{112,96},{1... | collective-permute-start | bytes 393224 | tf_op jit(solution)/shard_map/ppermute | solution.py:219
  (14 other events, 43.0 us)

commit v5 on v4

--- a/solution.py
+++ b/solution.py
@@ -112,12 +112,13 @@
     send[...] = jnp.where(first, odd, even)
 
 
-def rows_kernel(after, put, offdiag, basis_t, diag, offdiag_rows, basis_rows, diag_rows, token):
+def rows_kernel(after, put, offdiag, basis_t, diag, offdiag_rows, basis_rows, diag_rows, offdiag_shared, token):
     token[...] = after[...]
     basis_rows[...] = dot_t(put[...], basis_t[...]).astype(BF16)
     wide = jnp.broadcast_to(diag[...], (diag.shape[0], 128))
     diag_rows[...] = take(put[...], wide)
     offdiag_rows[...] = dot_t(put[...], offdiag[...]).astype(BF16)
+    offdiag_shared[...] = dot(offdiag_rows[...], put[...]).astype(BF16)
 
 
 def late_sent_kernel(parts, local, put, basis_rows, coarse_out, f0, f1, f2, f3):
@@ -142,20 +143,23 @@
     return live_of(length, local.shape[0]) * (local[...] + spread)
 
 
-def correction_kernel(length, local, basis_t, coarse_out, correction):
+def correction_kernel(length, local, basis_t, coarse_out, offdiag_rows, correction, applied_rows):
     correction[...] = correct(length, local, basis_t, coarse_out)
-
-
-def increment_kernel(correction, r0, r1, r2, r3, put, offdiag_rows, diag_rows, c0, c1, c2, c3, p0, p1, p2, p3,
-                     increment, g0, g1, g2, g3):
+    applied_rows[...] = dot(offdiag_rows[...], correction[...].astype(BF16))
+
+
+def faces_kernel(applied_rows, r0, r1, r2, r3, offdiag_shared, diag_rows, c0, c1, c2, c3, p0, p1, p2, p3,
+                 g0, g1, g2, g3, token):
+    token[...] = jnp.zeros_like(token)
     received = load_faces((r0, r1, r2, r3))
-    increment[...] = correction[...] + place(put[...], received)
     there = load_faces((c0, c1, c2, c3)) + received
-    applied = dot(offdiag_rows[...], increment[...].astype(BF16)) + diag_rows[:, :1] * there
+    applied = applied_rows[...] + dot(offdiag_shared[...], received.astype(BF16)) + diag_rows[:, :1] * there
     store_faces(load_faces((p0, p1, p2, p3)) - applied, (g0, g1, g2, g3))
 
 
-def residual_kernel(length, increment, diag, loads, offdiag, put, resid_out, solution, offdiag_columns, sem):
+def residual_kernel(after, length, correction, r0, r1, r2, r3, diag, loads, offdiag, put,
+                    resid_out, solution, offdiag_columns, increment, sem):
+    increment[...] = correction[...] + place(put[...], load_faces((r0, r1, r2, r3)))
     leave = pltpu.make_async_copy(increment, solution, sem)
     leave.start()
     applied = dot(offdiag[...], increment[...].astype(BF16)) + diag[...] * increment[...]
@@ -292,9 +296,10 @@
                 "vvv",
                 flops=square_flops + gather_flops,
             )
-            offdiag_rows, basis_rows, diag_rows, after = call(
+            offdiag_rows, basis_rows, diag_rows, offdiag_shared, after = call(
                 rows_kernel,
-                [like(nrows, n, dtype=BF16), like(nrows, modes, dtype=BF16), like(nrows, 128), mark],
+                [like(nrows, n, dtype=BF16), like(nrows, modes, dtype=BF16), like(nrows, 128),
+                 like(nrows, nrows, dtype=BF16), mark],
                 (after, put, offdiag, basis_t, diag),
                 "vvvvv",
                 flops=2 * nrows * n * n,
@@ -332,24 +337,27 @@
             )
         received = exchange(corrected)
         if sweep < ITERS - 1:
-            (correction,) = call(
-                correction_kernel, [block], (iface_len, local, basis_t, coarse_out), "svvv"
-            )
-            increment, *sent = call(
-                increment_kernel,
-                [block] + [face] * 4,
-                (correction, *received, put, offdiag_rows, diag_rows, *corrected, *sent),
-                "v" * 16,
-                flops=2 * gather_flops,
+            correction, applied_rows = call(
+                correction_kernel,
+                [block, like(nrows, nloads)],
+                (iface_len, local, basis_t, coarse_out, offdiag_rows),
+                "svvvv",
+                flops=gather_flops // 2,
+            )
+            *sent, after = call(
+                faces_kernel,
+                [face] * 4 + [mark],
+                (applied_rows, *received, offdiag_shared, diag_rows, *corrected, *sent),
+                "v" * 15,
             )
             assert solution is None
             resid, solution, offdiag_columns = call(
                 residual_kernel,
                 [block, block, like(n, nrows, dtype=BF16)],
-                (iface_len, increment, diag, loads, offdiag, put),
-                "svvvvv",
+                (after, iface_len, correction, *received, diag, loads, offdiag, put),
+                "vs" + "v" * 9,
                 "vhv",
-                [pltpu.SemaphoreType.DMA],
+                [pltpu.VMEM((n, nloads), F32), pltpu.SemaphoreType.DMA],
                 flops=square_flops,
             )
         else:

time: 148 us -> 147 us (level)
  waiting for transfers between devices: 26.4 us -> 19.3 us
  Pallas kernels: 23.6 us -> 25.9 us
  blocking collectives: 43.8 us -> 46 us
  starting transfers between devices: 41.6 us -> 43.1 us
    ppermute x18, waiting for transfers between devices: 22.4 us -> 16.7 us  [swap(): lax.ppermute(array, axis, [(i, j) for i, j in pairs if 0 <= j < size])]
    all_to_all x1, blocking collectives: 20.9 us -> 25.5 us  [body(): gathered = lax.all_to_all(coarse_in, 'grid', 0, 0)]
    all_to_all x2, blocking collectives: 22.9 us -> 20.5 us  [body(): parts = lax.all_to_all(parts, 'sub', 0, 0, axis_index_groups=groups)]
    pallas_call x17, Pallas kernels: 23.6 us -> 25.9 us  [call(): pl.pallas_call(kernel, out_shape=outs, in_specs=[pl.BlockSpec(memory_spac...]
    ppermute x18, starting transfers between devices: 33.3 us -> 34.8 us  [swap(): lax.ppermute(array, axis, [(i, j) for i, j in pairs if 0 <= j < size])]
    unnamed x55 -> x59, local copies, waits for them, and re-layouts: 8.67 us -> 9.47 us
  transfers between devices with their start and end apart: 19 -> 19, of which waited for: 11 -> 9; matrix products, arithmetic and copies ran while one was open for 0% -> 0% of each run, Pallas kernels for 8% -> 10%
where the time goes in v5:
time: 147 us
  blocking collectives  46 us (31%)
  starting transfers between devices  43.1 us (29%)
  Pallas kernels  25.9 us (18%)
  waiting for transfers between devices  19.3 us (13%)
  local copies, waits for them, and re-layouts  9.78 us (7%)
  between operations  1.98 us (1%)
    ppermute x18, starting transfers between devices, swap(): lax.ppermute(array, axis, [(i, j) for i, j in pairs if 0 <= j < size])  34.8 us
    pallas_call x17, Pallas kernels, call(): pl.pallas_call(kernel, out_shape=outs, in_specs=[pl.BlockSpec(memory_spac...  25.9 us
    all_to_all x1, blocking collectives, body(): gathered = lax.all_to_all(coarse_in, 'grid', 0, 0)  25.5 us
    all_to_all x2, blocking collectives, body(): parts = lax.all_to_all(parts, 'sub', 0, 0, axis_index_groups=groups)  20.5 us
    ppermute x18, waiting for transfers between devices, swap(): lax.ppermute(array, axis, [(i, j) for i, j in pairs if 0 <= j < size])  16.7 us
    unnamed x59, local copies, waits for them, and re-layouts  9.47 us
    all_to_all x1, starting transfers between devices, body(): gathered = lax.all_to_all(coarse_in, 'grid', 0, 0)  8.23 us
  transfers between devices with their start and end apart: 19, of which 9 were waited for; matrix products, arithmetic and copies ran while one was open for 0% of the time, Pallas kernels for 10%

profile of v5, /device:TPU:72, one launch (start us, length us, event | category | flops | bytes accessed | tf_op | source)
XLA Modules:
  0.0 146.8 jit_solution(5523846303190286559)
XLA Ops:
  3.5 7.8 %collective-permute-start.1 = (f32[128,256]{1,0:T(8,128)S(1)}, f32[128,256]{1,0:T(8,128)S(1)}, u32[]{:S(2)}, u32[]{:S(2)}) collective-permute-start(f32[128,256]{1,0:T(8,128)S(1)} %get-tuple-element.54.p1), channel_id=1, source_target_pairs={{1,2},{2,1},{3,4},{4,3},{5,6},{6,5},{7,8},{8,7},{9,10},{10,9},{11,... | collective-permute-start | bytes 393224 | tf_op jit(solution)/shard_map/ppermute | solution.py:223
  11.3 1.9 %collective-permute-start.2 = (f32[128,256]{1,0:T(8,128)S(1)}, f32[128,256]{1,0:T(8,128)S(1)}, u32[]{:S(2)}, u32[]{:S(2)}) collective-permute-start(f32[128,256]{1,0:T(8,128)S(1)} %get-tuple-element.55.p2), channel_id=1, source_target_pairs={{16,32},{32,16},{48,64},{64,48},{80,96},{96,80},{112,128},{128,112... | collective-permute-start | bytes 393224 | tf_op jit(solution)/shard_map/ppermute | solution.py:223
  14.5 2.1 %collective-permute-done.1.f1 = f32[128,256]{1,0:T(8,128)S(1)} collective-permute-done((f32[128,256]{1,0:T(8,128)S(1)}, f32[128,256]{1,0:T(8,128)S(1)}, u32[]{:S(2)}, u32[]{:S(2)}) %collective-permute-start.1) | collective-permute-done | bytes 131104 | tf_op jit(solution)/shard_map/ppermute | solution.py:223
  16.6 2.6 %collective-permute-done.2.f2 = f32[128,256]{1,0:T(8,128)S(1)} collective-permute-done((f32[128,256]{1,0:T(8,128)S(1)}, f32[128,256]{1,0:T(8,128)S(1)}, u32[]{:S(2)}, u32[]{:S(2)}) %collective-permute-start.2) | collective-permute-done | bytes 131104 | tf_op jit(solution)/shard_map/ppermute | solution.py:223
  19.2 1.8 %shard_map.106 = (bf16[1152,256]{1,0:T(8,128)(2,1)S(1)}, f32[16,32,256]{2,1,0:T(8,128)}, f32[8,128]{1,0:T(8,128)S(1)}) custom-call(f32[1152,256]{1,0:T(8,128)S(1)} %get-tuple-element.52.resid, f32[128,256]{1,0:T(8,128)S(1)} %collective-permute-done.f0, f32[128,256]{1,0:T(8,128)S(1)} %collective-permute-done.1.f1, f32[128,256]{1,0:T(8,128)S(1)} %collective-permute-done.2.f2, ...), custom_call_target="tpu_custom_call" | custom-call | flops 603979776 | bytes 4075520 | tf_op jit(solution)/shard_map/pallas_call | solution.py:201
  21.9 8.2 %all-to-all-start = ((f32[16,32,256]{2,1,0:T(8,128)}), f32[16,32,256]{2,1,0:T(8,128)}, u32[]{:S(2)}, u32[]{:S(2)}) async-start(f32[16,32,256]{2,1,0:T(8,128)} %get-tuple-element.59), calls=%async_computation | async-start | bytes 1048576 | tf_op jit(solution)/shard_map/all_to_all | solution.py:290
  30.6 1.7 %copy-done.5 = bf16[1,1152,1152]{2,1,0:T(8,128)(2,1)S(1)} copy-done((bf16[1,1152,1152]{2,1,0:T(8,128)(2,1)S(1)}, bf16[1,1152,1152]{2,1,0:T(8,128)(2,1)}, u32[]{:S(2)}) %copy-start.5) | copy-done | bytes 2654232
  33.4 2.9 %shard_map.107 = (f32[1152,256]{1,0:T(8,128)S(1)}, f32[512,256]{1,0:T(8,128)S(1)}, f32[8,128]{1,0:T(8,128)S(1)}) custom-call(bf16[1152,1152]{1,0:T(8,128)(2,1)S(1)} %bitcast.24, bf16[1152,256]{1,0:T(8,128)(2,1)S(1)} %copy-done.27, bf16[1152,512]{1,0:T(8,128)(2,1)S(1)} %shard_map.104.put), custom_call_target="tpu_custom_call" | custom-call | flops 1283457024 | bytes 6131712 | tf_op jit(solution)/shard_map/pallas_call | solution.py:201
  38.1 3.7 %shard_map.108 = (bf16[512,1152]{1,0:T(8,128)(2,1)S(1)}, bf16[512,32]{1,0:T(8,128)(2,1)S(1)}, f32[512,128]{1,0:T(8,128)S(1)}, bf16[512,512]{1,0:T(8,128)(2,1)S(1)}, f32[8,128]{1,0:T(8,128)S(1)}) custom-call(f32[8,128]{1,0:T(8,128)S(1)} %get-tuple-element.60.after, bf16[1152,512]{1,0:T(8,128)(2,1)S(1)} %shard_map.104.put, bf16[1152,1152]{1,0:T(8,128)(2,1)S(1)} %bitcast.16, ...), custom_call_target="tpu_custom_call" | custom-call | flops 1358954496 | bytes 5919232 | tf_op jit(solution)/shard_map/pallas_call | solution.py:201
  44.4 2.5 %all-to-all-done.gathered = f32[16,32,256]{2,1,0:T(8,128)} async-done(((f32[16,32,256]{2,1,0:T(8,128)}), f32[16,32,256]{2,1,0:T(8,128)}, u32[]{:S(2)}, u32[]{:S(2)}) %all-to-all-start) | async-done | bytes 524320 | tf_op jit(solution)/shard_map/all_to_all | solution.py:290
  48.1 2.3 %shard_map.109 = (f32[256,256]{1,0:T(8,128)S(1)}, f32[256,256]{1,0:T(8,128)S(1)}, f32[8,128]{1,0:T(8,128)}) custom-call(s32[1]{0:T(128)} %bitcast.core, f32[512,512]{1,0:T(8,128)S(1)} %copy-done.3, f32[16,32,256]{2,1,0:T(8,128)} %all-to-all-done.gathered, f32[8,128]{1,0:T(8,128)S(1)} %get-tuple-element.61.after, f32[8,128]{1,0:T(8,128)S(1)} %get-tuple-element.62.after_too), custom_call_target="tpu_custom_call" | custom-call | flops 402653184 | bytes 2109444 | tf_op jit(solution)/shard_map/pallas_call | solution.py:201
  50.4 1.5 %collective-permute-done.4 = f32[256,256]{1,0:T(8,128)S(1)} collective-permute-done((f32[256,256]{1,0:T(8,128)S(1)}, f32[256,256]{1,0:T(8,128)S(1)}, u32[]{:S(2)}, u32[]{:S(2)}) %collective-permute-start.4) | collective-permute-done | bytes 262176 | tf_op jit(solution)/shard_map/ppermute | solution.py:223
  52.0 10.8 %all_to_all.20.parts = f32[8,32,256]{2,1,0:T(8,128)S(1)} all-to-all(f32[8,32,256]{2,1,0:T(8,128)S(1)} %bitcast.29), channel_id=1, replica_groups={{0,32,64,96,128,160,192,224},{16,48,80,112,144,176,208,240},{1,33,65,97..., dimensions={0} | all-to-all | bytes 524288 | tf_op jit(solution)/shard_map/all_to_all | solution.py:325
  63.1 1.7 %collective-permute-start.5 = (f32[128,256]{1,0:T(8,128)S(1)}, f32[128,256]{1,0:T(8,128)S(1)}, u32[]{:S(2)}, u32[]{:S(2)}) collective-permute-start(f32[128,256]{1,0:T(8,128)S(1)} %get-tuple-element.70.c0), channel_id=1, source_target_pairs={{0,1},{1,0},{2,3},{3,2},{4,5},{5,4},{6,7},{7,6},{8,9},{9,8},{10,11... | collective-permute-start | bytes 393224 | tf_op jit(solution)/shard_map/ppermute | solution.py:223
  64.7 2.2 %collective-permute-start.6 = (f32[128,256]{1,0:T(8,128)S(1)}, f32[128,256]{1,0:T(8,128)S(1)}, u32[]{:S(2)}, u32[]{:S(2)}) collective-permute-start(f32[128,256]{1,0:T(8,128)S(1)} %get-tuple-element.71.c1), channel_id=1, source_target_pairs={{1,2},{2,1},{3,4},{4,3},{5,6},{6,5},{7,8},{8,7},{9,10},{10,9},{11,... | collective-permute-start | bytes 393224 | tf_op jit(solution)/shard_map/ppermute | solution.py:223
  67.0 1.9 %collective-permute-start.7 = (f32[128,256]{1,0:T(8,128)S(1)}, f32[128,256]{1,0:T(8,128)S(1)}, u32[]{:S(2)}, u32[]{:S(2)}) collective-permute-start(f32[128,256]{1,0:T(8,128)S(1)} %get-tuple-element.72.c2), channel_id=1, source_target_pairs={{16,32},{32,16},{48,64},{64,48},{80,96},{96,80},{112,128},{128,112... | collective-permute-start | bytes 393224 | tf_op jit(solution)/shard_map/ppermute | solution.py:223
  68.9 1.4 collective-permute-start.8
  70.4 1.2 shard_map.111
  71.6 4.0 %collective-permute-done.6.r1 = f32[128,256]{1,0:T(8,128)S(1)} collective-permute-done((f32[128,256]{1,0:T(8,128)S(1)}, f32[128,256]{1,0:T(8,128)S(1)}, u32[]{:S(2)}, u32[]{:S(2)}) %collective-permute-start.6) | collective-permute-done | bytes 131104 | tf_op jit(solution)/shard_map/ppermute | solution.py:223
  77.2 5.0 %collective-permute-start.10 = (f32[128,256]{1,0:T(8,128)S(1)}, f32[128,256]{1,0:T(8,128)S(1)}, u32[]{:S(2)}, u32[]{:S(2)}) collective-permute-start(f32[128,256]{1,0:T(8,128)S(1)} %get-tuple-element.80), channel_id=1, source_target_pairs={{1,2},{2,1},{3,4},{4,3},{5,6},{6,5},{7,8},{8,7},{9,10},{10,9},{11,... | collective-permute-start | bytes 393224 | tf_op jit(solution)/shard_map/ppermute | solution.py:223
  82.3 1.9 %collective-permute-start.11 = (f32[128,256]{1,0:T(8,128)S(1)}, f32[128,256]{1,0:T(8,128)S(1)}, u32[]{:S(2)}, u32[]{:S(2)}) collective-permute-start(f32[128,256]{1,0:T(8,128)S(1)} %get-tuple-element.81), channel_id=1, source_target_pairs={{16,32},{32,16},{48,64},{64,48},{80,96},{96,80},{112,128},{128,112... | collective-permute-start | bytes 393224 | tf_op jit(solution)/shard_map/ppermute | solution.py:223
  84.5 4.8 %shard_map.113 = (f32[1152,256]{1,0:T(8,128)S(1)}, f32[1152,256]{1,0:T(8,128)S(1)}, bf16[1152,512]{1,0:T(8,128)(2,1)S(1)}) custom-call(f32[8,128]{1,0:T(8,128)S(1)} %get-tuple-element.76.after, s32[1]{0:T(128)S(6)} %copy.22.length, f32[1152,256]{1,0:T(8,128)S(1)} %get-tuple-element.77.correction, f32[128,256]{1,0:T(8,128)S(1)} %collective-permute-done.5.r0, ...), custom_call_target="tpu_custom_call" | custom-call | flops 679477248 | bytes 10265092 | tf_op jit(solution)/shard_map/pallas_call | solution.py:201
  91.0 25.5 %all_to_all.21.gathered = f32[16,32,256]{2,1,0:T(8,128)S(1)} all-to-all(f32[16,32,256]{2,1,0:T(8,128)S(1)} %get-tuple-element.83), channel_id=1, replica_groups=mesh['sub'=16,'grid'=16] {'grid'}, dimensions={0} | all-to-all | bytes 1048576 | tf_op jit(solution)/shard_map/all_to_all | solution.py:290
  118.8 9.7 %all_to_all.22.parts = f32[8,32,256]{2,1,0:T(8,128)S(1)} all-to-all(f32[8,32,256]{2,1,0:T(8,128)S(1)} %shard_map.117), channel_id=1, replica_groups={{0,32,64,96,128,160,192,224},{16,48,80,112,144,176,208,240},{1,33,65,97..., dimensions={0} | all-to-all | bytes 524288 | tf_op jit(solution)/shard_map/all_to_all | solution.py:325
  129.5 2.2 %collective-permute-start.14 = (f32[128,256]{1,0:T(8,128)S(1)}, f32[128,256]{1,0:T(8,128)S(1)}, u32[]{:S(2)}, u32[]{:S(2)}) collective-permute-start(f32[128,256]{1,0:T(8,128)S(1)} %get-tuple-element.91), channel_id=1, source_target_pairs={{0,1},{1,0},{2,3},{3,2},{4,5},{5,4},{6,7},{7,6},{8,9},{9,8},{10,11... | collective-permute-start | bytes 393224 | tf_op jit(solution)/shard_map/ppermute | solution.py:223
  131.6 2.7 %collective-permute-start.15 = (f32[128,256]{1,0:T(8,128)S(1)}, f32[128,256]{1,0:T(8,128)S(1)}, u32[]{:S(2)}, u32[]{:S(2)}) collective-permute-start(f32[128,256]{1,0:T(8,128)S(1)} %get-tuple-element.92), channel_id=1, source_target_pairs={{1,2},{2,1},{3,4},{4,3},{5,6},{6,5},{7,8},{8,7},{9,10},{10,9},{11,... | collective-permute-start | bytes 393224 | tf_op jit(solution)/shard_map/ppermute | solution.py:223
  134.4 1.9 %collective-permute-start.16 = (f32[128,256]{1,0:T(8,128)S(1)}, f32[128,256]{1,0:T(8,128)S(1)}, u32[]{:S(2)}, u32[]{:S(2)}) collective-permute-start(f32[128,256]{1,0:T(8,128)S(1)} %get-tuple-element.93), channel_id=1, source_target_pairs={{16,32},{32,16},{48,64},{64,48},{80,96},{96,80},{112,128},{128,112... | collective-permute-start | bytes 393224 | tf_op jit(solution)/shard_map/ppermute | solution.py:223
  136.3 1.2 collective-permute-start.17
  137.5 1.8 %shard_map.119 = (f32[1152,256]{1,0:T(8,128)S(1)}, f32[1152,256]{1,0:T(8,128)S(1)}) custom-call(s32[1]{0:T(128)S(6)} %copy.22.length, f32[1152,256]{1,0:T(8,128)S(1)} %get-tuple-element.90.local, bf16[1152,32]{1,0:T(8,128)(2,1)S(1)} %bitcast.23, f32[32,256]{1,0:T(8,128)S(1)} %get-tuple-element.96.coarse_out, f32[1152,256]{1,0:T(8,128)S(1)} %get-tuple-element.97.before, ...), custom_call_target="tpu_custom_call" | custom-call | flops 679477248 | bytes 8663556 | tf_op jit(solution)/shard_map/pallas_call | solution.py:201
  139.4 2.7 %collective-permute-done.15.r1 = f32[128,256]{1,0:T(8,128)S(1)} collective-permute-done((f32[128,256]{1,0:T(8,128)S(1)}, f32[128,256]{1,0:T(8,128)S(1)}, u32[]{:S(2)}, u32[]{:S(2)}) %collective-permute-start.15) | collective-permute-done | bytes 131104 | tf_op jit(solution)/shard_map/ppermute | solution.py:223
  142.1 2.5 %collective-permute-done.16.r2 = f32[128,256]{1,0:T(8,128)S(1)} collective-permute-done((f32[128,256]{1,0:T(8,128)S(1)}, f32[128,256]{1,0:T(8,128)S(1)}, u32[]{:S(2)}, u32[]{:S(2)}) %collective-permute-start.16) | collective-permute-done | bytes 131104 | tf_op jit(solution)/shard_map/ppermute | solution.py:223
  144.6 2.0 %shard_map.120 = (f32[1152,256]{1,0:T(8,128)}, f32[1152,256]{1,0:T(8,128)}) custom-call(s32[1]{0:T(128)S(6)} %copy.22.length, f32[128,256]{1,0:T(8,128)S(1)} %collective-permute-done.14.r0, f32[128,256]{1,0:T(8,128)S(1)} %collective-permute-done.15.r1, f32[128,256]{1,0:T(8,128)S(1)} %collective-permute-done.16.r2, ...), custom_call_target="tpu_custom_call" | custom-call | flops 1207959552 | bytes 7606788 | tf_op jit(solution)/shard_map/pallas_call | solution.py:201
  (93 shorter events, 18.2 us)
Async XLA Ops:
  2.5 16.7 %copy-start.11 = (bf16[1,32,1152]{2,1,0:T(8,128)(2,1)S(1)}, bf16[1,32,1152]{2,1,0:T(8,128)(2,1)}, u32[]{:S(2)}) copy-start(bf16[1,32,1152]{2,1,0:T(8,128)(2,1)} %param.16) | copy-start | bytes 221188
  3.3 17.7 %copy-start.18 = (f32[128,256]{1,0:T(8,128)}, f32[128,256]{1,0:T(8,128)S(1)}, u32[]{:S(2)}) copy-start(f32[128,256]{1,0:T(8,128)S(1)} %get-tuple-element.53.p0) | copy-start | bytes 393220
  3.4 17.7 %copy-start.20 = (f32[128,256]{1,0:T(8,128)}, f32[128,256]{1,0:T(8,128)S(1)}, u32[]{:S(2)}) copy-start(f32[128,256]{1,0:T(8,128)S(1)} %get-tuple-element.54.p1) | copy-start | bytes 393220
  3.4 17.7 %copy-start.22 = (f32[128,256]{1,0:T(8,128)}, f32[128,256]{1,0:T(8,128)S(1)}, u32[]{:S(2)}) copy-start(f32[128,256]{1,0:T(8,128)S(1)} %get-tuple-element.55.p2) | copy-start | bytes 393220
  3.4 17.7 %copy-start.24 = (f32[128,256]{1,0:T(8,128)}, f32[128,256]{1,0:T(8,128)S(1)}, u32[]{:S(2)}) copy-start(f32[128,256]{1,0:T(8,128)S(1)} %get-tuple-element.56.p3) | copy-start | bytes 393220
  3.4 11.1 %collective-permute-start = (f32[128,256]{1,0:T(8,128)S(1)}, f32[128,256]{1,0:T(8,128)S(1)}, u32[]{:S(2)}, u32[]{:S(2)}) collective-permute-start(f32[128,256]{1,0:T(8,128)S(1)} %get-tuple-element.53.p0), channel_id=1, source_target_pairs={{0,1},{1,0},{2,3},{3,2},{4,5},{5,4},{6,7},{7,6},{8,9},{9,8},{10,11... | collective-permute-start | bytes 393224 | tf_op jit(solution)/shard_map/ppermute | solution.py:223
  3.5 13.1 %collective-permute-start.1 = (f32[128,256]{1,0:T(8,128)S(1)}, f32[128,256]{1,0:T(8,128)S(1)}, u32[]{:S(2)}, u32[]{:S(2)}) collective-permute-start(f32[128,256]{1,0:T(8,128)S(1)} %get-tuple-element.54.p1), channel_id=1, source_target_pairs={{1,2},{2,1},{3,4},{4,3},{5,6},{6,5},{7,8},{8,7},{9,10},{10,9},{11,... | collective-permute-start | bytes 393224 | tf_op jit(solution)/shard_map/ppermute | solution.py:223
  11.3 7.9 %collective-permute-start.2 = (f32[128,256]{1,0:T(8,128)S(1)}, f32[128,256]{1,0:T(8,128)S(1)}, u32[]{:S(2)}, u32[]{:S(2)}) collective-permute-start(f32[128,256]{1,0:T(8,128)S(1)} %get-tuple-element.55.p2), channel_id=1, source_target_pairs={{16,32},{32,16},{48,64},{64,48},{80,96},{96,80},{112,128},{128,112... | collective-permute-start | bytes 393224 | tf_op jit(solution)/shard_map/ppermute | solution.py:223
  13.3 5.9 %collective-permute-start.3 = (f32[128,256]{1,0:T(8,128)S(1)}, f32[128,256]{1,0:T(8,128)S(1)}, u32[]{:S(2)}, u32[]{:S(2)}) collective-permute-start(f32[128,256]{1,0:T(8,128)S(1)} %get-tuple-element.56.p3), channel_id=1, source_target_pairs={{0,16},{16,0},{32,48},{48,32},{64,80},{80,64},{96,112},{112,96},{1... | collective-permute-start | bytes 393224 | tf_op jit(solution)/shard_map/ppermute | solution.py:223
  21.9 8.5 %copy-start.28 = (f32[1,1152]{1,0:T(1,128)S(1)}, f32[1,1152]{1,0:T(1,128)}, u32[]{:S(2)}) copy-start(f32[1,1152]{1,0:T(1,128)} %param.15) | copy-start | bytes 13828
  21.9 25.0 %all-to-all-start = ((f32[16,32,256]{2,1,0:T(8,128)}), f32[16,32,256]{2,1,0:T(8,128)}, u32[]{:S(2)}, u32[]{:S(2)}) async-start(f32[16,32,256]{2,1,0:T(8,128)} %get-tuple-element.59), calls=%async_computation | async-start | bytes 1048576 | tf_op jit(solution)/shard_map/all_to_all | solution.py:290
  48.1 14.6 %copy-start.13 = (f32[512,256]{1,0:T(8,128)S(1)}, f32[512,256]{1,0:T(8,128)}, u32[]{:S(2)}) copy-start(f32[512,256]{1,0:T(8,128)} %copy-done.12) | copy-start | bytes 1572868
  48.1 22.2 %copy-start.10 = (bf16[512,1152]{1,0:T(8,128)(2,1)S(1)}, bf16[512,1152]{1,0:T(8,128)(2,1)}, u32[]{:S(2)}) copy-start(bf16[512,1152]{1,0:T(8,128)(2,1)} %copy-done.9) | copy-start | bytes 3538948
  50.4 19.9 %copy-start.8 = (f32[1152,256]{1,0:T(8,128)S(1)}, f32[1152,256]{1,0:T(8,128)}, u32[]{:S(2)}) copy-start(f32[1152,256]{1,0:T(8,128)} %copy-done.7) | copy-start | bytes 3538948
  50.4 1.5 %collective-permute-start.4 = (f32[256,256]{1,0:T(8,128)S(1)}, f32[256,256]{1,0:T(8,128)S(1)}, u32[]{:S(2)}, u32[]{:S(2)}) collective-permute-start(f32[256,256]{1,0:T(8,128)S(1)} %get-tuple-element.64), channel_id=1, source_target_pairs={{0,16},{16,0},{32,48},{48,32},{64,80},{80,64},{96,112},{112,96},{1... | collective-permute-start | bytes 786440 | tf_op jit(solution)/shard_map/ppermute | solution.py:223
  63.1 8.6 %collective-permute-start.5 = (f32[128,256]{1,0:T(8,128)S(1)}, f32[128,256]{1,0:T(8,128)S(1)}, u32[]{:S(2)}, u32[]{:S(2)}) collective-permute-start(f32[128,256]{1,0:T(8,128)S(1)} %get-tuple-element.70.c0), channel_id=1, source_target_pairs={{0,1},{1,0},{2,3},{3,2},{4,5},{5,4},{6,7},{7,6},{8,9},{9,8},{10,11... | collective-permute-start | bytes 393224 | tf_op jit(solution)/shard_map/ppermute | solution.py:223
  64.7 10.9 %collective-permute-start.6 = (f32[128,256]{1,0:T(8,128)S(1)}, f32[128,256]{1,0:T(8,128)S(1)}, u32[]{:S(2)}, u32[]{:S(2)}) collective-permute-start(f32[128,256]{1,0:T(8,128)S(1)} %get-tuple-element.71.c1), channel_id=1, source_target_pairs={{1,2},{2,1},{3,4},{4,3},{5,6},{6,5},{7,8},{8,7},{9,10},{10,9},{11,... | collective-permute-start | bytes 393224 | tf_op jit(solution)/shard_map/ppermute | solution.py:223
  67.0 8.7 %collective-permute-start.7 = (f32[128,256]{1,0:T(8,128)S(1)}, f32[128,256]{1,0:T(8,128)S(1)}, u32[]{:S(2)}, u32[]{:S(2)}) collective-permute-start(f32[128,256]{1,0:T(8,128)S(1)} %get-tuple-element.72.c2), channel_id=1, source_target_pairs={{16,32},{32,16},{48,64},{64,48},{80,96},{96,80},{112,128},{128,112... | collective-permute-start | bytes 393224 | tf_op jit(solution)/shard_map/ppermute | solution.py:223
  68.9 6.8 %collective-permute-start.8 = (f32[128,256]{1,0:T(8,128)S(1)}, f32[128,256]{1,0:T(8,128)S(1)}, u32[]{:S(2)}, u32[]{:S(2)}) collective-permute-start(f32[128,256]{1,0:T(8,128)S(1)} %get-tuple-element.73.c3), channel_id=1, source_target_pairs={{0,16},{16,0},{32,48},{48,32},{64,80},{80,64},{96,112},{112,96},{1... | collective-permute-start | bytes 393224 | tf_op jit(solution)/shard_map/ppermute | solution.py:223
  70.3 5.4 %copy-start.19 = (f32[128,256]{1,0:T(8,128)S(1)}, f32[128,256]{1,0:T(8,128)}, u32[]{:S(2)}) copy-start(f32[128,256]{1,0:T(8,128)} %copy-done.18) | copy-start | bytes 393220
  75.7 8.7 %copy-start.1 = (bf16[1,1152,1152]{2,1,0:T(8,128)(2,1)S(1)}, bf16[1,1152,1152]{2,1,0:T(8,128)(2,1)}, u32[]{:S(2)}) copy-start(bf16[1,1152,1152]{2,1,0:T(8,128)(2,1)} %param.14) | copy-start | bytes 7962628
  76.1 13.2 %collective-permute-start.9 = (f32[128,256]{1,0:T(8,128)S(1)}, f32[128,256]{1,0:T(8,128)S(1)}, u32[]{:S(2)}, u32[]{:S(2)}) collective-permute-start(f32[128,256]{1,0:T(8,128)S(1)} %get-tuple-element.79), channel_id=1, source_target_pairs={{0,1},{1,0},{2,3},{3,2},{4,5},{5,4},{6,7},{7,6},{8,9},{9,8},{10,11... | collective-permute-start | bytes 393224 | tf_op jit(solution)/shard_map/ppermute | solution.py:223
  77.2 12.1 %collective-permute-start.10 = (f32[128,256]{1,0:T(8,128)S(1)}, f32[128,256]{1,0:T(8,128)S(1)}, u32[]{:S(2)}, u32[]{:S(2)}) collective-permute-start(f32[128,256]{1,0:T(8,128)S(1)} %get-tuple-element.80), channel_id=1, source_target_pairs={{1,2},{2,1},{3,4},{4,3},{5,6},{6,5},{7,8},{8,7},{9,10},{10,9},{11,... | collective-permute-start | bytes 393224 | tf_op jit(solution)/shard_map/ppermute | solution.py:223
  82.3 7.7 %collective-permute-start.11 = (f32[128,256]{1,0:T(8,128)S(1)}, f32[128,256]{1,0:T(8,128)S(1)}, u32[]{:S(2)}, u32[]{:S(2)}) collective-permute-start(f32[128,256]{1,0:T(8,128)S(1)} %get-tuple-element.81), channel_id=1, source_target_pairs={{16,32},{32,16},{48,64},{64,48},{80,96},{96,80},{112,128},{128,112... | collective-permute-start | bytes 393224 | tf_op jit(solution)/shard_map/ppermute | solution.py:223
  84.2 5.7 %collective-permute-start.12 = (f32[128,256]{1,0:T(8,128)S(1)}, f32[128,256]{1,0:T(8,128)S(1)}, u32[]{:S(2)}, u32[]{:S(2)}) collective-permute-start(f32[128,256]{1,0:T(8,128)S(1)} %get-tuple-element.82), channel_id=1, source_target_pairs={{0,16},{16,0},{32,48},{48,32},{64,80},{80,64},{96,112},{112,96},{1... | collective-permute-start | bytes 393224 | tf_op jit(solution)/shard_map/ppermute | solution.py:223
  89.9 26.6 %copy-start.4 = (f32[512,512]{1,0:T(8,128)S(1)}, f32[512,512]{1,0:T(8,128)}, u32[]{:S(2)}) copy-start(f32[512,512]{1,0:T(8,128)} %coarse.3) | copy-start | bytes 3145732
  89.9 27.3 %copy-start.6 = (bf16[1,1152,1152]{2,1,0:T(8,128)(2,1)S(1)}, bf16[1,1152,1152]{2,1,0:T(8,128)(2,1)}, u32[]{:S(2)}) copy-start(bf16[1,1152,1152]{2,1,0:T(8,128)(2,1)} %param.13) | copy-start | bytes 7962628
  117.1 1.6 %collective-permute-start.13 = (f32[256,256]{1,0:T(8,128)S(1)}, f32[256,256]{1,0:T(8,128)S(1)}, u32[]{:S(2)}, u32[]{:S(2)}) collective-permute-start(f32[256,256]{1,0:T(8,128)S(1)} %get-tuple-element.86), channel_id=1, source_target_pairs={{0,16},{16,0},{32,48},{48,32},{64,80},{80,64},{96,112},{112,96},{1... | collective-permute-start | bytes 786440 | tf_op jit(solution)/shard_map/ppermute | solution.py:223
  129.5 9.9 %collective-permute-start.14 = (f32[128,256]{1,0:T(8,128)S(1)}, f32[128,256]{1,0:T(8,128)S(1)}, u32[]{:S(2)}, u32[]{:S(2)}) collective-permute-start(f32[128,256]{1,0:T(8,128)S(1)} %get-tuple-element.91), channel_id=1, source_target_pairs={{0,1},{1,0},{2,3},{3,2},{4,5},{5,4},{6,7},{7,6},{8,9},{9,8},{10,11... | collective-permute-start | bytes 393224 | tf_op jit(solution)/shard_map/ppermute | solution.py:223
  131.6 10.5 %collective-permute-start.15 = (f32[128,256]{1,0:T(8,128)S(1)}, f32[128,256]{1,0:T(8,128)S(1)}, u32[]{:S(2)}, u32[]{:S(2)}) collective-permute-start(f32[128,256]{1,0:T(8,128)S(1)} %get-tuple-element.92), channel_id=1, source_target_pairs={{1,2},{2,1},{3,4},{4,3},{5,6},{6,5},{7,8},{8,7},{9,10},{10,9},{11,... | collective-permute-start | bytes 393224 | tf_op jit(solution)/shard_map/ppermute | solution.py:223
  134.4 10.2 %collective-permute-start.16 = (f32[128,256]{1,0:T(8,128)S(1)}, f32[128,256]{1,0:T(8,128)S(1)}, u32[]{:S(2)}, u32[]{:S(2)}) collective-permute-start(f32[128,256]{1,0:T(8,128)S(1)} %get-tuple-element.93), channel_id=1, source_target_pairs={{16,32},{32,16},{48,64},{64,48},{80,96},{96,80},{112,128},{128,112... | collective-permute-start | bytes 393224 | tf_op jit(solution)/shard_map/ppermute | solution.py:223
  136.3 8.3 %collective-permute-start.17 = (f32[128,256]{1,0:T(8,128)S(1)}, f32[128,256]{1,0:T(8,128)S(1)}, u32[]{:S(2)}, u32[]{:S(2)}) collective-permute-start(f32[128,256]{1,0:T(8,128)S(1)} %get-tuple-element.94), channel_id=1, source_target_pairs={{0,16},{16,0},{32,48},{48,32},{64,80},{80,64},{96,112},{112,96},{1... | collective-permute-start | bytes 393224 | tf_op jit(solution)/shard_map/ppermute | solution.py:223
  (16 other events, 42.6 us)

commit v6 on v5

--- a/solution.py
+++ b/solution.py
@@ -158,22 +158,22 @@
 
 
 def residual_kernel(after, length, correction, r0, r1, r2, r3, diag, loads, offdiag, put,
-                    resid_out, solution, offdiag_columns, increment, sem):
+                    resid_out, solution, increment, sem):
     increment[...] = correction[...] + place(put[...], load_faces((r0, r1, r2, r3)))
     leave = pltpu.make_async_copy(increment, solution, sem)
     leave.start()
     applied = dot(offdiag[...], increment[...].astype(BF16)) + diag[...] * increment[...]
     resid_out[...] = (loads[...] - applied) * live_of(length, loads.shape[0])
-    offdiag_columns[...] = dot(offdiag[...], put[...]).astype(BF16)
     leave.wait()
 
 
-def own_kernel(length, local, basis_t, coarse_out, before, diag, resid, offdiag,
-               solution, resid_out):
+def own_kernel(length, local, basis_t, coarse_out, before, diag, resid, offdiag, put,
+               solution, resid_out, offdiag_columns):
     correction = correct(length, local, basis_t, coarse_out)
     solution[...] = before[...] + correction
     applied = dot(offdiag[...], correction.astype(BF16)) + diag[...] * correction
     resid_out[...] = resid[...] - live_of(length, resid.shape[0]) * applied
+    offdiag_columns[...] = dot(offdiag[...], put[...]).astype(BF16)
 
 
 def finish_kernel(length, r0, r1, r2, r3, put, offdiag_columns, diag, own, own_resid,
@@ -351,21 +351,21 @@
                 "v" * 15,
             )
             assert solution is None
-            resid, solution, offdiag_columns = call(
+            resid, solution = call(
                 residual_kernel,
-                [block, block, like(n, nrows, dtype=BF16)],
+                [block, block],
                 (after, iface_len, correction, *received, diag, loads, offdiag, put),
                 "vs" + "v" * 9,
-                "vhv",
+                "vh",
                 [pltpu.VMEM((n, nloads), F32), pltpu.SemaphoreType.DMA],
                 flops=square_flops,
             )
         else:
-            own, own_resid = call(
+            own, own_resid, offdiag_columns = call(
                 own_kernel,
-                [block, block],
-                (iface_len, local, basis_t, coarse_out, solution, diag, resid, offdiag),
-                "svvvvvvv",
+                [block, block, like(n, nrows, dtype=BF16)],
+                (iface_len, local, basis_t, coarse_out, solution, diag, resid, offdiag, put),
+                "svvvvvvvv",
                 flops=square_flops,
             )
             solution, resid = call(

time: 147 us -> 147 us (level)
  no operation moved by 1% of the time
where the time goes in v6:
time: 147 us
  blocking collectives  45.3 us (31%)
  starting transfers between devices  43.9 us (30%)
  Pallas kernels  25.8 us (18%)
  waiting for transfers between devices  19.2 us (13%)
  local copies, waits for them, and re-layouts  9.78 us (7%)
  between operations  2 us (1%)
    ppermute x18, starting transfers between devices, swap(): lax.ppermute(array, axis, [(i, j) for i, j in pairs if 0 <= j < size])  35.6 us
    pallas_call x17, Pallas kernels, call(): pl.pallas_call(kernel, out_shape=outs, in_specs=[pl.BlockSpec(memory_spac...  25.8 us
    all_to_all x1, blocking collectives, body(): gathered = lax.all_to_all(coarse_in, 'grid', 0, 0)  24.7 us
    all_to_all x2, blocking collectives, body(): parts = lax.all_to_all(parts, 'sub', 0, 0, axis_index_groups=groups)  20.6 us
    ppermute x18, waiting for transfers between devices, swap(): lax.ppermute(array, axis, [(i, j) for i, j in pairs if 0 <= j < size])  16.6 us
    unnamed x59, local copies, waits for them, and re-layouts  9.47 us
    all_to_all x1, starting transfers between devices, body(): gathered = lax.all_to_all(coarse_in, 'grid', 0, 0)  8.23 us
  transfers between devices with their start and end apart: 19, of which 9 were waited for; matrix products, arithmetic and copies ran while one was open for 0% of the time, Pallas kernels for 10%

profile of v6, /device:TPU:72, one launch (start us, length us, event | category | flops | bytes accessed | tf_op | source)
XLA Modules:
  0.0 146.7 jit_solution(16730211604942217950)
XLA Ops:
  3.5 7.8 %collective-permute-start.1 = (f32[128,256]{1,0:T(8,128)S(1)}, f32[128,256]{1,0:T(8,128)S(1)}, u32[]{:S(2)}, u32[]{:S(2)}) collective-permute-start(f32[128,256]{1,0:T(8,128)S(1)} %get-tuple-element.54.p1), channel_id=1, source_target_pairs={{1,2},{2,1},{3,4},{4,3},{5,6},{6,5},{7,8},{8,7},{9,10},{10,9},{11,... | collective-permute-start | bytes 393224 | tf_op jit(solution)/shard_map/ppermute | solution.py:223
  11.3 1.9 %collective-permute-start.2 = (f32[128,256]{1,0:T(8,128)S(1)}, f32[128,256]{1,0:T(8,128)S(1)}, u32[]{:S(2)}, u32[]{:S(2)}) collective-permute-start(f32[128,256]{1,0:T(8,128)S(1)} %get-tuple-element.55.p2), channel_id=1, source_target_pairs={{16,32},{32,16},{48,64},{64,48},{80,96},{96,80},{112,128},{128,112... | collective-permute-start | bytes 393224 | tf_op jit(solution)/shard_map/ppermute | solution.py:223
  14.5 2.1 %collective-permute-done.1.f1 = f32[128,256]{1,0:T(8,128)S(1)} collective-permute-done((f32[128,256]{1,0:T(8,128)S(1)}, f32[128,256]{1,0:T(8,128)S(1)}, u32[]{:S(2)}, u32[]{:S(2)}) %collective-permute-start.1) | collective-permute-done | bytes 131104 | tf_op jit(solution)/shard_map/ppermute | solution.py:223
  16.6 2.6 %collective-permute-done.2.f2 = f32[128,256]{1,0:T(8,128)S(1)} collective-permute-done((f32[128,256]{1,0:T(8,128)S(1)}, f32[128,256]{1,0:T(8,128)S(1)}, u32[]{:S(2)}, u32[]{:S(2)}) %collective-permute-start.2) | collective-permute-done | bytes 131104 | tf_op jit(solution)/shard_map/ppermute | solution.py:223
  19.2 1.8 %shard_map.106 = (bf16[1152,256]{1,0:T(8,128)(2,1)S(1)}, f32[16,32,256]{2,1,0:T(8,128)}, f32[8,128]{1,0:T(8,128)S(1)}) custom-call(f32[1152,256]{1,0:T(8,128)S(1)} %get-tuple-element.52.resid, f32[128,256]{1,0:T(8,128)S(1)} %collective-permute-done.f0, f32[128,256]{1,0:T(8,128)S(1)} %collective-permute-done.1.f1, f32[128,256]{1,0:T(8,128)S(1)} %collective-permute-done.2.f2, ...), custom_call_target="tpu_custom_call" | custom-call | flops 603979776 | bytes 4075520 | tf_op jit(solution)/shard_map/pallas_call | solution.py:201
  21.9 8.2 %all-to-all-start = ((f32[16,32,256]{2,1,0:T(8,128)}), f32[16,32,256]{2,1,0:T(8,128)}, u32[]{:S(2)}, u32[]{:S(2)}) async-start(f32[16,32,256]{2,1,0:T(8,128)} %get-tuple-element.59), calls=%async_computation | async-start | bytes 1048576 | tf_op jit(solution)/shard_map/all_to_all | solution.py:290
  30.6 1.7 %copy-done.5 = bf16[1,1152,1152]{2,1,0:T(8,128)(2,1)S(1)} copy-done((bf16[1,1152,1152]{2,1,0:T(8,128)(2,1)S(1)}, bf16[1,1152,1152]{2,1,0:T(8,128)(2,1)}, u32[]{:S(2)}) %copy-start.5) | copy-done | bytes 2654232
  33.4 2.9 %shard_map.107 = (f32[1152,256]{1,0:T(8,128)S(1)}, f32[512,256]{1,0:T(8,128)S(1)}, f32[8,128]{1,0:T(8,128)S(1)}) custom-call(bf16[1152,1152]{1,0:T(8,128)(2,1)S(1)} %bitcast.24, bf16[1152,256]{1,0:T(8,128)(2,1)S(1)} %copy-done.27, bf16[1152,512]{1,0:T(8,128)(2,1)S(1)} %shard_map.104.put), custom_call_target="tpu_custom_call" | custom-call | flops 1283457024 | bytes 6131712 | tf_op jit(solution)/shard_map/pallas_call | solution.py:201
  38.1 3.7 %shard_map.108 = (bf16[512,1152]{1,0:T(8,128)(2,1)S(1)}, bf16[512,32]{1,0:T(8,128)(2,1)S(1)}, f32[512,128]{1,0:T(8,128)S(1)}, bf16[512,512]{1,0:T(8,128)(2,1)S(1)}, f32[8,128]{1,0:T(8,128)S(1)}) custom-call(f32[8,128]{1,0:T(8,128)S(1)} %get-tuple-element.60.after, bf16[1152,512]{1,0:T(8,128)(2,1)S(1)} %shard_map.104.put, bf16[1152,1152]{1,0:T(8,128)(2,1)S(1)} %bitcast.16, ...), custom_call_target="tpu_custom_call" | custom-call | flops 1358954496 | bytes 5919232 | tf_op jit(solution)/shard_map/pallas_call | solution.py:201
  44.4 2.5 %all-to-all-done.gathered = f32[16,32,256]{2,1,0:T(8,128)} async-done(((f32[16,32,256]{2,1,0:T(8,128)}), f32[16,32,256]{2,1,0:T(8,128)}, u32[]{:S(2)}, u32[]{:S(2)}) %all-to-all-start) | async-done | bytes 524320 | tf_op jit(solution)/shard_map/all_to_all | solution.py:290
  48.1 2.3 %shard_map.109 = (f32[256,256]{1,0:T(8,128)S(1)}, f32[256,256]{1,0:T(8,128)S(1)}, f32[8,128]{1,0:T(8,128)}) custom-call(s32[1]{0:T(128)} %bitcast.core, f32[512,512]{1,0:T(8,128)S(1)} %copy-done.3, f32[16,32,256]{2,1,0:T(8,128)} %all-to-all-done.gathered, f32[8,128]{1,0:T(8,128)S(1)} %get-tuple-element.61.after, f32[8,128]{1,0:T(8,128)S(1)} %get-tuple-element.62.after_too), custom_call_target="tpu_custom_call" | custom-call | flops 402653184 | bytes 2109444 | tf_op jit(solution)/shard_map/pallas_call | solution.py:201
  50.4 1.5 %collective-permute-done.4 = f32[256,256]{1,0:T(8,128)S(1)} collective-permute-done((f32[256,256]{1,0:T(8,128)S(1)}, f32[256,256]{1,0:T(8,128)S(1)}, u32[]{:S(2)}, u32[]{:S(2)}) %collective-permute-start.4) | collective-permute-done | bytes 262176 | tf_op jit(solution)/shard_map/ppermute | solution.py:223
  52.0 10.8 %all_to_all.20.parts = f32[8,32,256]{2,1,0:T(8,128)S(1)} all-to-all(f32[8,32,256]{2,1,0:T(8,128)S(1)} %bitcast.29), channel_id=1, replica_groups={{0,32,64,96,128,160,192,224},{16,48,80,112,144,176,208,240},{1,33,65,97..., dimensions={0} | all-to-all | bytes 524288 | tf_op jit(solution)/shard_map/all_to_all | solution.py:325
  63.1 1.7 %collective-permute-start.5 = (f32[128,256]{1,0:T(8,128)S(1)}, f32[128,256]{1,0:T(8,128)S(1)}, u32[]{:S(2)}, u32[]{:S(2)}) collective-permute-start(f32[128,256]{1,0:T(8,128)S(1)} %get-tuple-element.70.c0), channel_id=1, source_target_pairs={{0,1},{1,0},{2,3},{3,2},{4,5},{5,4},{6,7},{7,6},{8,9},{9,8},{10,11... | collective-permute-start | bytes 393224 | tf_op jit(solution)/shard_map/ppermute | solution.py:223
  64.7 2.2 %collective-permute-start.6 = (f32[128,256]{1,0:T(8,128)S(1)}, f32[128,256]{1,0:T(8,128)S(1)}, u32[]{:S(2)}, u32[]{:S(2)}) collective-permute-start(f32[128,256]{1,0:T(8,128)S(1)} %get-tuple-element.71.c1), channel_id=1, source_target_pairs={{1,2},{2,1},{3,4},{4,3},{5,6},{6,5},{7,8},{8,7},{9,10},{10,9},{11,... | collective-permute-start | bytes 393224 | tf_op jit(solution)/shard_map/ppermute | solution.py:223
  67.0 1.9 %collective-permute-start.7 = (f32[128,256]{1,0:T(8,128)S(1)}, f32[128,256]{1,0:T(8,128)S(1)}, u32[]{:S(2)}, u32[]{:S(2)}) collective-permute-start(f32[128,256]{1,0:T(8,128)S(1)} %get-tuple-element.72.c2), channel_id=1, source_target_pairs={{16,32},{32,16},{48,64},{64,48},{80,96},{96,80},{112,128},{128,112... | collective-permute-start | bytes 393224 | tf_op jit(solution)/shard_map/ppermute | solution.py:223
  68.9 1.4 collective-permute-start.8
  70.4 1.2 shard_map.111
  71.6 4.0 %collective-permute-done.6.r1 = f32[128,256]{1,0:T(8,128)S(1)} collective-permute-done((f32[128,256]{1,0:T(8,128)S(1)}, f32[128,256]{1,0:T(8,128)S(1)}, u32[]{:S(2)}, u32[]{:S(2)}) %collective-permute-start.6) | collective-permute-done | bytes 131104 | tf_op jit(solution)/shard_map/ppermute | solution.py:223
  77.2 5.0 %collective-permute-start.10 = (f32[128,256]{1,0:T(8,128)S(1)}, f32[128,256]{1,0:T(8,128)S(1)}, u32[]{:S(2)}, u32[]{:S(2)}) collective-permute-start(f32[128,256]{1,0:T(8,128)S(1)} %get-tuple-element.80), channel_id=1, source_target_pairs={{1,2},{2,1},{3,4},{4,3},{5,6},{6,5},{7,8},{8,7},{9,10},{10,9},{11,... | collective-permute-start | bytes 393224 | tf_op jit(solution)/shard_map/ppermute | solution.py:223
  82.3 1.9 %collective-permute-start.11 = (f32[128,256]{1,0:T(8,128)S(1)}, f32[128,256]{1,0:T(8,128)S(1)}, u32[]{:S(2)}, u32[]{:S(2)}) collective-permute-start(f32[128,256]{1,0:T(8,128)S(1)} %get-tuple-element.81), channel_id=1, source_target_pairs={{16,32},{32,16},{48,64},{64,48},{80,96},{96,80},{112,128},{128,112... | collective-permute-start | bytes 393224 | tf_op jit(solution)/shard_map/ppermute | solution.py:223
  84.5 3.2 %shard_map.113 = (f32[1152,256]{1,0:T(8,128)S(1)}, f32[1152,256]{1,0:T(8,128)S(1)}) custom-call(f32[8,128]{1,0:T(8,128)S(1)} %get-tuple-element.76.after, s32[1]{0:T(128)S(6)} %copy.22.length, f32[1152,256]{1,0:T(8,128)S(1)} %get-tuple-element.77.correction, f32[128,256]{1,0:T(8,128)S(1)} %collective-permute-done.5.r0, ...), custom_call_target="tpu_custom_call" | custom-call | flops 679477248 | bytes 9085444 | tf_op jit(solution)/shard_map/pallas_call | solution.py:201
  87.7 2.2 %collective-permute-done.11.f2 = f32[128,256]{1,0:T(8,128)S(1)} collective-permute-done((f32[128,256]{1,0:T(8,128)S(1)}, f32[128,256]{1,0:T(8,128)S(1)}, u32[]{:S(2)}, u32[]{:S(2)}) %collective-permute-start.11) | collective-permute-done | bytes 131104 | tf_op jit(solution)/shard_map/ppermute | solution.py:223
  91.0 24.7 %all_to_all.21.gathered = f32[16,32,256]{2,1,0:T(8,128)S(1)} all-to-all(f32[16,32,256]{2,1,0:T(8,128)S(1)} %get-tuple-element.83), channel_id=1, replica_groups=mesh['sub'=16,'grid'=16] {'grid'}, dimensions={0} | all-to-all | bytes 1048576 | tf_op jit(solution)/shard_map/all_to_all | solution.py:290
  117.9 9.9 %all_to_all.22.parts = f32[8,32,256]{2,1,0:T(8,128)S(1)} all-to-all(f32[8,32,256]{2,1,0:T(8,128)S(1)} %shard_map.117), channel_id=1, replica_groups={{0,32,64,96,128,160,192,224},{16,48,80,112,144,176,208,240},{1,33,65,97..., dimensions={0} | all-to-all | bytes 524288 | tf_op jit(solution)/shard_map/all_to_all | solution.py:325
  128.8 2.8 %collective-permute-start.14 = (f32[128,256]{1,0:T(8,128)S(1)}, f32[128,256]{1,0:T(8,128)S(1)}, u32[]{:S(2)}, u32[]{:S(2)}) collective-permute-start(f32[128,256]{1,0:T(8,128)S(1)} %get-tuple-element.91), channel_id=1, source_target_pairs={{0,1},{1,0},{2,3},{3,2},{4,5},{5,4},{6,7},{7,6},{8,9},{9,8},{10,11... | collective-permute-start | bytes 393224 | tf_op jit(solution)/shard_map/ppermute | solution.py:223
  131.6 2.7 %collective-permute-start.15 = (f32[128,256]{1,0:T(8,128)S(1)}, f32[128,256]{1,0:T(8,128)S(1)}, u32[]{:S(2)}, u32[]{:S(2)}) collective-permute-start(f32[128,256]{1,0:T(8,128)S(1)} %get-tuple-element.92), channel_id=1, source_target_pairs={{1,2},{2,1},{3,4},{4,3},{5,6},{6,5},{7,8},{8,7},{9,10},{10,9},{11,... | collective-permute-start | bytes 393224 | tf_op jit(solution)/shard_map/ppermute | solution.py:223
  134.3 1.9 %collective-permute-start.16 = (f32[128,256]{1,0:T(8,128)S(1)}, f32[128,256]{1,0:T(8,128)S(1)}, u32[]{:S(2)}, u32[]{:S(2)}) collective-permute-start(f32[128,256]{1,0:T(8,128)S(1)} %get-tuple-element.93), channel_id=1, source_target_pairs={{16,32},{32,16},{48,64},{64,48},{80,96},{96,80},{112,128},{128,112... | collective-permute-start | bytes 393224 | tf_op jit(solution)/shard_map/ppermute | solution.py:223
  136.3 1.5 collective-permute-start.17
  137.7 3.3 %shard_map.119 = (f32[1152,256]{1,0:T(8,128)S(1)}, f32[1152,256]{1,0:T(8,128)S(1)}, bf16[1152,512]{1,0:T(8,128)(2,1)S(1)}) custom-call(s32[1]{0:T(128)S(6)} %copy.22.length, f32[1152,256]{1,0:T(8,128)S(1)} %get-tuple-element.90.local, bf16[1152,32]{1,0:T(8,128)(2,1)S(1)} %bitcast.23, f32[32,256]{1,0:T(8,128)S(1)} %get-tuple-element.95.coarse_out, ...), custom_call_target="tpu_custom_call" | custom-call | flops 679477248 | bytes 11022852 | tf_op jit(solution)/shard_map/pallas_call | solution.py:201
  142.1 2.5 %collective-permute-done.16.r2 = f32[128,256]{1,0:T(8,128)S(1)} collective-permute-done((f32[128,256]{1,0:T(8,128)S(1)}, f32[128,256]{1,0:T(8,128)S(1)}, u32[]{:S(2)}, u32[]{:S(2)}) %collective-permute-start.16) | collective-permute-done | bytes 131104 | tf_op jit(solution)/shard_map/ppermute | solution.py:223
  144.5 2.0 %shard_map.120 = (f32[1152,256]{1,0:T(8,128)}, f32[1152,256]{1,0:T(8,128)}) custom-call(s32[1]{0:T(128)S(6)} %copy.22.length, f32[128,256]{1,0:T(8,128)S(1)} %collective-permute-done.14.r0, f32[128,256]{1,0:T(8,128)S(1)} %collective-permute-done.15.r1, f32[128,256]{1,0:T(8,128)S(1)} %collective-permute-done.16.r2, ...), custom_call_target="tpu_custom_call" | custom-call | flops 1207959552 | bytes 7606788 | tf_op jit(solution)/shard_map/pallas_call | solution.py:201
  (93 shorter events, 18.5 us)
Async XLA Ops:
  2.5 16.7 %copy-start.11 = (bf16[1,32,1152]{2,1,0:T(8,128)(2,1)S(1)}, bf16[1,32,1152]{2,1,0:T(8,128)(2,1)}, u32[]{:S(2)}) copy-start(bf16[1,32,1152]{2,1,0:T(8,128)(2,1)} %param.16) | copy-start | bytes 221188
  3.3 17.7 %copy-start.18 = (f32[128,256]{1,0:T(8,128)}, f32[128,256]{1,0:T(8,128)S(1)}, u32[]{:S(2)}) copy-start(f32[128,256]{1,0:T(8,128)S(1)} %get-tuple-element.53.p0) | copy-start | bytes 393220
  3.4 17.7 %copy-start.20 = (f32[128,256]{1,0:T(8,128)}, f32[128,256]{1,0:T(8,128)S(1)}, u32[]{:S(2)}) copy-start(f32[128,256]{1,0:T(8,128)S(1)} %get-tuple-element.54.p1) | copy-start | bytes 393220
  3.4 17.7 %copy-start.22 = (f32[128,256]{1,0:T(8,128)}, f32[128,256]{1,0:T(8,128)S(1)}, u32[]{:S(2)}) copy-start(f32[128,256]{1,0:T(8,128)S(1)} %get-tuple-element.55.p2) | copy-start | bytes 393220
  3.4 17.7 %copy-start.24 = (f32[128,256]{1,0:T(8,128)}, f32[128,256]{1,0:T(8,128)S(1)}, u32[]{:S(2)}) copy-start(f32[128,256]{1,0:T(8,128)S(1)} %get-tuple-element.56.p3) | copy-start | bytes 393220
  3.4 11.1 %collective-permute-start = (f32[128,256]{1,0:T(8,128)S(1)}, f32[128,256]{1,0:T(8,128)S(1)}, u32[]{:S(2)}, u32[]{:S(2)}) collective-permute-start(f32[128,256]{1,0:T(8,128)S(1)} %get-tuple-element.53.p0), channel_id=1, source_target_pairs={{0,1},{1,0},{2,3},{3,2},{4,5},{5,4},{6,7},{7,6},{8,9},{9,8},{10,11... | collective-permute-start | bytes 393224 | tf_op jit(solution)/shard_map/ppermute | solution.py:223
  3.5 13.1 %collective-permute-start.1 = (f32[128,256]{1,0:T(8,128)S(1)}, f32[128,256]{1,0:T(8,128)S(1)}, u32[]{:S(2)}, u32[]{:S(2)}) collective-permute-start(f32[128,256]{1,0:T(8,128)S(1)} %get-tuple-element.54.p1), channel_id=1, source_target_pairs={{1,2},{2,1},{3,4},{4,3},{5,6},{6,5},{7,8},{8,7},{9,10},{10,9},{11,... | collective-permute-start | bytes 393224 | tf_op jit(solution)/shard_map/ppermute | solution.py:223
  11.3 7.9 %collective-permute-start.2 = (f32[128,256]{1,0:T(8,128)S(1)}, f32[128,256]{1,0:T(8,128)S(1)}, u32[]{:S(2)}, u32[]{:S(2)}) collective-permute-start(f32[128,256]{1,0:T(8,128)S(1)} %get-tuple-element.55.p2), channel_id=1, source_target_pairs={{16,32},{32,16},{48,64},{64,48},{80,96},{96,80},{112,128},{128,112... | collective-permute-start | bytes 393224 | tf_op jit(solution)/shard_map/ppermute | solution.py:223
  13.3 5.9 %collective-permute-start.3 = (f32[128,256]{1,0:T(8,128)S(1)}, f32[128,256]{1,0:T(8,128)S(1)}, u32[]{:S(2)}, u32[]{:S(2)}) collective-permute-start(f32[128,256]{1,0:T(8,128)S(1)} %get-tuple-element.56.p3), channel_id=1, source_target_pairs={{0,16},{16,0},{32,48},{48,32},{64,80},{80,64},{96,112},{112,96},{1... | collective-permute-start | bytes 393224 | tf_op jit(solution)/shard_map/ppermute | solution.py:223
  21.9 8.5 %copy-start.28 = (f32[1,1152]{1,0:T(1,128)S(1)}, f32[1,1152]{1,0:T(1,128)}, u32[]{:S(2)}) copy-start(f32[1,1152]{1,0:T(1,128)} %param.15) | copy-start | bytes 13828
  21.9 25.0 %all-to-all-start = ((f32[16,32,256]{2,1,0:T(8,128)}), f32[16,32,256]{2,1,0:T(8,128)}, u32[]{:S(2)}, u32[]{:S(2)}) async-start(f32[16,32,256]{2,1,0:T(8,128)} %get-tuple-element.59), calls=%async_computation | async-start | bytes 1048576 | tf_op jit(solution)/shard_map/all_to_all | solution.py:290
  48.1 14.6 %copy-start.13 = (f32[512,256]{1,0:T(8,128)S(1)}, f32[512,256]{1,0:T(8,128)}, u32[]{:S(2)}) copy-start(f32[512,256]{1,0:T(8,128)} %copy-done.12) | copy-start | bytes 1572868
  48.1 22.2 %copy-start.10 = (bf16[512,1152]{1,0:T(8,128)(2,1)S(1)}, bf16[512,1152]{1,0:T(8,128)(2,1)}, u32[]{:S(2)}) copy-start(bf16[512,1152]{1,0:T(8,128)(2,1)} %copy-done.9) | copy-start | bytes 3538948
  50.4 19.9 %copy-start.8 = (f32[1152,256]{1,0:T(8,128)S(1)}, f32[1152,256]{1,0:T(8,128)}, u32[]{:S(2)}) copy-start(f32[1152,256]{1,0:T(8,128)} %copy-done.7) | copy-start | bytes 3538948
  50.4 1.5 %collective-permute-start.4 = (f32[256,256]{1,0:T(8,128)S(1)}, f32[256,256]{1,0:T(8,128)S(1)}, u32[]{:S(2)}, u32[]{:S(2)}) collective-permute-start(f32[256,256]{1,0:T(8,128)S(1)} %get-tuple-element.64), channel_id=1, source_target_pairs={{0,16},{16,0},{32,48},{48,32},{64,80},{80,64},{96,112},{112,96},{1... | collective-permute-start | bytes 786440 | tf_op jit(solution)/shard_map/ppermute | solution.py:223
  63.1 8.6 %collective-permute-start.5 = (f32[128,256]{1,0:T(8,128)S(1)}, f32[128,256]{1,0:T(8,128)S(1)}, u32[]{:S(2)}, u32[]{:S(2)}) collective-permute-start(f32[128,256]{1,0:T(8,128)S(1)} %get-tuple-element.70.c0), channel_id=1, source_target_pairs={{0,1},{1,0},{2,3},{3,2},{4,5},{5,4},{6,7},{7,6},{8,9},{9,8},{10,11... | collective-permute-start | bytes 393224 | tf_op jit(solution)/shard_map/ppermute | solution.py:223
  64.7 10.9 %collective-permute-start.6 = (f32[128,256]{1,0:T(8,128)S(1)}, f32[128,256]{1,0:T(8,128)S(1)}, u32[]{:S(2)}, u32[]{:S(2)}) collective-permute-start(f32[128,256]{1,0:T(8,128)S(1)} %get-tuple-element.71.c1), channel_id=1, source_target_pairs={{1,2},{2,1},{3,4},{4,3},{5,6},{6,5},{7,8},{8,7},{9,10},{10,9},{11,... | collective-permute-start | bytes 393224 | tf_op jit(solution)/shard_map/ppermute | solution.py:223
  67.0 8.7 %collective-permute-start.7 = (f32[128,256]{1,0:T(8,128)S(1)}, f32[128,256]{1,0:T(8,128)S(1)}, u32[]{:S(2)}, u32[]{:S(2)}) collective-permute-start(f32[128,256]{1,0:T(8,128)S(1)} %get-tuple-element.72.c2), channel_id=1, source_target_pairs={{16,32},{32,16},{48,64},{64,48},{80,96},{96,80},{112,128},{128,112... | collective-permute-start | bytes 393224 | tf_op jit(solution)/shard_map/ppermute | solution.py:223
  68.9 6.8 %collective-permute-start.8 = (f32[128,256]{1,0:T(8,128)S(1)}, f32[128,256]{1,0:T(8,128)S(1)}, u32[]{:S(2)}, u32[]{:S(2)}) collective-permute-start(f32[128,256]{1,0:T(8,128)S(1)} %get-tuple-element.73.c3), channel_id=1, source_target_pairs={{0,16},{16,0},{32,48},{48,32},{64,80},{80,64},{96,112},{112,96},{1... | collective-permute-start | bytes 393224 | tf_op jit(solution)/shard_map/ppermute | solution.py:223
  70.3 5.4 %copy-start.19 = (f32[128,256]{1,0:T(8,128)S(1)}, f32[128,256]{1,0:T(8,128)}, u32[]{:S(2)}) copy-start(f32[128,256]{1,0:T(8,128)} %copy-done.18) | copy-start | bytes 393220
  75.7 8.7 %copy-start.1 = (bf16[1,1152,1152]{2,1,0:T(8,128)(2,1)S(1)}, bf16[1,1152,1152]{2,1,0:T(8,128)(2,1)}, u32[]{:S(2)}) copy-start(bf16[1,1152,1152]{2,1,0:T(8,128)(2,1)} %param.14) | copy-start | bytes 7962628
  76.1 11.6 %collective-permute-start.9 = (f32[128,256]{1,0:T(8,128)S(1)}, f32[128,256]{1,0:T(8,128)S(1)}, u32[]{:S(2)}, u32[]{:S(2)}) collective-permute-start(f32[128,256]{1,0:T(8,128)S(1)} %get-tuple-element.79), channel_id=1, source_target_pairs={{0,1},{1,0},{2,3},{3,2},{4,5},{5,4},{6,7},{7,6},{8,9},{9,8},{10,11... | collective-permute-start | bytes 393224 | tf_op jit(solution)/shard_map/ppermute | solution.py:223
  77.2 10.4 %collective-permute-start.10 = (f32[128,256]{1,0:T(8,128)S(1)}, f32[128,256]{1,0:T(8,128)S(1)}, u32[]{:S(2)}, u32[]{:S(2)}) collective-permute-start(f32[128,256]{1,0:T(8,128)S(1)} %get-tuple-element.80), channel_id=1, source_target_pairs={{1,2},{2,1},{3,4},{4,3},{5,6},{6,5},{7,8},{8,7},{9,10},{10,9},{11,... | collective-permute-start | bytes 393224 | tf_op jit(solution)/shard_map/ppermute | solution.py:223
  82.3 7.7 %collective-permute-start.11 = (f32[128,256]{1,0:T(8,128)S(1)}, f32[128,256]{1,0:T(8,128)S(1)}, u32[]{:S(2)}, u32[]{:S(2)}) collective-permute-start(f32[128,256]{1,0:T(8,128)S(1)} %get-tuple-element.81), channel_id=1, source_target_pairs={{16,32},{32,16},{48,64},{64,48},{80,96},{96,80},{112,128},{128,112... | collective-permute-start | bytes 393224 | tf_op jit(solution)/shard_map/ppermute | solution.py:223
  84.2 5.7 %collective-permute-start.12 = (f32[128,256]{1,0:T(8,128)S(1)}, f32[128,256]{1,0:T(8,128)S(1)}, u32[]{:S(2)}, u32[]{:S(2)}) collective-permute-start(f32[128,256]{1,0:T(8,128)S(1)} %get-tuple-element.82), channel_id=1, source_target_pairs={{0,16},{16,0},{32,48},{48,32},{64,80},{80,64},{96,112},{112,96},{1... | collective-permute-start | bytes 393224 | tf_op jit(solution)/shard_map/ppermute | solution.py:223
  89.9 25.8 %copy-start.4 = (f32[512,512]{1,0:T(8,128)S(1)}, f32[512,512]{1,0:T(8,128)}, u32[]{:S(2)}) copy-start(f32[512,512]{1,0:T(8,128)} %coarse.3) | copy-start | bytes 3145732
  89.9 26.5 %copy-start.6 = (bf16[1,1152,1152]{2,1,0:T(8,128)(2,1)S(1)}, bf16[1,1152,1152]{2,1,0:T(8,128)(2,1)}, u32[]{:S(2)}) copy-start(bf16[1,1152,1152]{2,1,0:T(8,128)(2,1)} %param.13) | copy-start | bytes 7962628
  116.3 1.6 %collective-permute-start.13 = (f32[256,256]{1,0:T(8,128)S(1)}, f32[256,256]{1,0:T(8,128)S(1)}, u32[]{:S(2)}, u32[]{:S(2)}) collective-permute-start(f32[256,256]{1,0:T(8,128)S(1)} %get-tuple-element.86), channel_id=1, source_target_pairs={{0,16},{16,0},{32,48},{48,32},{64,80},{80,64},{96,112},{112,96},{1... | collective-permute-start | bytes 786440 | tf_op jit(solution)/shard_map/ppermute | solution.py:223
  128.8 12.2 %collective-permute-start.14 = (f32[128,256]{1,0:T(8,128)S(1)}, f32[128,256]{1,0:T(8,128)S(1)}, u32[]{:S(2)}, u32[]{:S(2)}) collective-permute-start(f32[128,256]{1,0:T(8,128)S(1)} %get-tuple-element.91), channel_id=1, source_target_pairs={{0,1},{1,0},{2,3},{3,2},{4,5},{5,4},{6,7},{7,6},{8,9},{9,8},{10,11... | collective-permute-start | bytes 393224 | tf_op jit(solution)/shard_map/ppermute | solution.py:223
  131.6 10.5 %collective-permute-start.15 = (f32[128,256]{1,0:T(8,128)S(1)}, f32[128,256]{1,0:T(8,128)S(1)}, u32[]{:S(2)}, u32[]{:S(2)}) collective-permute-start(f32[128,256]{1,0:T(8,128)S(1)} %get-tuple-element.92), channel_id=1, source_target_pairs={{1,2},{2,1},{3,4},{4,3},{5,6},{6,5},{7,8},{8,7},{9,10},{10,9},{11,... | collective-permute-start | bytes 393224 | tf_op jit(solution)/shard_map/ppermute | solution.py:223
  134.3 10.2 %collective-permute-start.16 = (f32[128,256]{1,0:T(8,128)S(1)}, f32[128,256]{1,0:T(8,128)S(1)}, u32[]{:S(2)}, u32[]{:S(2)}) collective-permute-start(f32[128,256]{1,0:T(8,128)S(1)} %get-tuple-element.93), channel_id=1, source_target_pairs={{16,32},{32,16},{48,64},{64,48},{80,96},{96,80},{112,128},{128,112... | collective-permute-start | bytes 393224 | tf_op jit(solution)/shard_map/ppermute | solution.py:223
  136.3 8.3 %collective-permute-start.17 = (f32[128,256]{1,0:T(8,128)S(1)}, f32[128,256]{1,0:T(8,128)S(1)}, u32[]{:S(2)}, u32[]{:S(2)}) collective-permute-start(f32[128,256]{1,0:T(8,128)S(1)} %get-tuple-element.94), channel_id=1, source_target_pairs={{0,16},{16,0},{32,48},{48,32},{64,80},{80,64},{96,112},{112,96},{1... | collective-permute-start | bytes 393224 | tf_op jit(solution)/shard_map/ppermute | solution.py:223
  (16 other events, 42.6 us)
